TPU v7x, 32 devices: a whole 2x2x4 slice. The times are simulated.
32 devices in a mesh: sub: 2 (over x), gate: 16 (over z, y, core).
Axes of the slice: x: 2, y: 2, z: 4, core: 2. Of those that a mesh axis runs over, the one named last changes fastest.
Arguments:
- raw_echo: bfloat16 [2, 256, 16384], P(None, ('sub', 'gate')), may hold values from -6 to 6
- delays: int32 [256], P(('sub', 'gate')), may hold values from 0 to 64
Outputs:
- image: bfloat16 [2, 512, 16384], P(None, 'sub', 'gate')
All inputs are finite; a program needn't handle non-finite values.
Results may differ from a plain program's by a relative error of at most 0.009.
Values may be sent and summed in bfloat16 or wider, within the bound.
No kernel may reach another device: no remote copies, remote signals or barrier semaphores. Data moves between devices by JAX's collectives and lax.ppermute only.
A program may use at most 64 MiB of HBM per device.

v0:
```python
import math

import jax
import jax.numpy as jnp
from jax import lax
from jax.sharding import PartitionSpec as P

RADIX = 128
SAMPLES = 16384
ANGLES = 256
DELAY_MAX = 64


TWO_PI = 2.0 * math.pi


def partner(array, axis, apart):
    return lax.ppermute(array, axis, [(i, i ^ 1 << apart) for i in range(lax.axis_size(axis))])


def complex_blocks(real_part, imag_part):
    upper = jnp.stack([real_part, -imag_part], axis=1)
    lower = jnp.stack([imag_part, real_part], axis=1)
    return jnp.stack([upper, lower], axis=0).astype(jnp.bfloat16)


def dft_blocks(order):
    counter = jnp.arange(order, dtype=jnp.int32)
    product = counter[:, None] * counter[None, :] % order
    phases = -TWO_PI / order * product.astype(jnp.float32)
    factor = 1.0 / math.sqrt(order)
    return complex_blocks(jnp.cos(phases) * factor, jnp.sin(phases) * factor)


def steer_blocks(beam_count, pulse_count):
    beam_index = jnp.arange(beam_count, dtype=jnp.int32)
    pulse_index = jnp.arange(pulse_count, dtype=jnp.int32)
    modulus = 16 * beam_count
    product = (
        (2 * beam_index[:, None] - beam_count + 1)
        * (2 * pulse_index[None, :] - pulse_count + 1)
        % modulus
    )
    phases = -TWO_PI / modulus * product.astype(jnp.float32)
    factor = 1.0 / math.sqrt(pulse_count)
    return complex_blocks(jnp.cos(phases) * factor, jnp.sin(phases) * factor)


def interp_table(beam_count):
    half_count = beam_count // 2
    targets = jnp.arange(beam_count, dtype=jnp.float32)
    sources = jnp.arange(half_count, dtype=jnp.float32)
    distance = targets[:, None] * 0.5 - 0.25 - sources[None, :]
    taper = jnp.where(jnp.abs(distance) < 4.0, 0.5 + 0.5 * jnp.cos(math.pi * distance / 4.0), 0.0)
    return (jnp.sinc(distance) * taper).astype(jnp.bfloat16)


def rotation(center, numerator, depth, gate_pos):
    modulus = ANGLES * 2 ** (depth + 3)
    turns = jnp.mod(center * numerator, modulus).astype(jnp.float32) / modulus
    center_sq = (center * center).astype(jnp.float32)
    near_term = center_sq / (16.0 * (SAMPLES + gate_pos))
    phases = -TWO_PI * turns[:, None] - TWO_PI / (4 * ANGLES) * near_term[None, :]
    factor = 1.0 / math.sqrt(2.0)
    return (jnp.cos(phases) * factor, jnp.sin(phases) * factor)


def range_compress(raw_echo, delays):
    pulse_count = raw_echo.shape[1]
    dft_table = dft_blocks(RADIX)
    samples_grid = raw_echo.reshape(2, pulse_count, RADIX, RADIX)
    section_one = jnp.einsum(
        "akcn,cpnm->apkm", dft_table, samples_grid, preferred_element_type=jnp.float32
    )
    counter = jnp.arange(RADIX, dtype=jnp.int32)
    phases = -TWO_PI / SAMPLES * (counter[:, None] * counter[None, :]).astype(jnp.float32)
    cosine = jnp.cos(phases)
    sine_part = jnp.sin(phases)
    twisted = jnp.stack(
        [
            section_one[0] * cosine - section_one[1] * sine_part,
            section_one[0] * sine_part + section_one[1] * cosine,
        ]
    ).astype(jnp.bfloat16)
    spectrum = jnp.einsum("akcn,cpjn->apkj", dft_table, twisted, preferred_element_type=jnp.float32)
    rounded = spectrum.reshape(2, pulse_count, SAMPLES).astype(jnp.bfloat16)
    padded = jnp.pad(rounded, ((0, 0), (0, 0), (0, DELAY_MAX)))

    def shift_row(pulse_row, start):
        return lax.dynamic_slice_in_dim(pulse_row, start, SAMPLES, axis=1)

    return jax.vmap(shift_row, in_axes=(1, 0), out_axes=1)(padded, delays)


def merge_pair(child, depth, sub_index, sector, gate_pos, sub_pulses):
    half_count = ANGLES // 2
    side_bit = sub_index // 2 ** (depth - 1) % 2
    partner_full = partner(child, "sub", depth - 1)
    partner_half = lax.dynamic_slice_in_dim(partner_full, side_bit * half_count, half_count, axis=1)
    own_half = lax.dynamic_slice_in_dim(child, side_bit * half_count, half_count, axis=1)
    paired = jnp.stack([own_half, partner_half], axis=0)
    moved = jnp.einsum(
        "jh,kchg->kcjg", interp_table(ANGLES), paired, preferred_element_type=jnp.float32
    )
    sector_next = 2 * sector + side_bit
    row_index = sector_next * ANGLES + jnp.arange(ANGLES, dtype=jnp.int32)
    numerator = 2 * row_index + 1 - ANGLES * 2**depth
    offset = sub_pulses * 2 ** (depth - 1) // 2
    own_center = (2 * side_bit - 1) * offset
    total_real = jnp.zeros((ANGLES, child.shape[-1]), jnp.float32)
    total_imag = jnp.zeros((ANGLES, child.shape[-1]), jnp.float32)
    for member in range(2):
        center = own_center * (1 - 2 * member)
        cosine, sine_part = rotation(center, numerator, depth, gate_pos)
        total_real = total_real + cosine * moved[member, 0] - sine_part * moved[member, 1]
        total_imag = total_imag + sine_part * moved[member, 0] + cosine * moved[member, 1]
    merged = jnp.stack([total_real, total_imag], axis=0).astype(jnp.bfloat16)
    return (merged, sector_next)


def per_device(raw_echo, delays):
    gate_count = lax.axis_size("gate")
    sub_count = lax.axis_size("sub")
    pulse_count = raw_echo.shape[1]
    sub_pulses = pulse_count * gate_count
    gate_width = SAMPLES // gate_count
    depth_count = sub_count.bit_length() - 1
    compressed = range_compress(raw_echo, delays)
    steering = steer_blocks(ANGLES, sub_pulses)
    layout = compressed.reshape(2, pulse_count, gate_count, gate_width)
    received = lax.all_to_all(layout, "gate", split_axis=2, concat_axis=1, tiled=True)
    flat_block = received.reshape(2, received.shape[1], received.shape[3])
    current = jnp.einsum(
        "akcm,cmg->akg", steering, flat_block, preferred_element_type=jnp.float32
    ).astype(jnp.bfloat16)
    gate_pos = (
        lax.axis_index("gate") * gate_width + jnp.arange(gate_width, dtype=jnp.int32)
    ).astype(jnp.float32)
    sub_index = lax.axis_index("sub")
    sector = jnp.zeros((), jnp.int32)
    for depth in range(1, depth_count + 1):
        current, sector = merge_pair(current, depth, sub_index, sector, gate_pos, sub_pulses)
    return current


def solution(mesh):
    placed = (P(None, ("sub", "gate"), None), P(("sub", "gate")))
    return jax.shard_map(
        per_device, mesh=mesh, in_specs=placed, out_specs=P(None, "sub", "gate"), check_vma=False
    )
```

profile of v0, /device:TPU:0, one launch (start us, length us, event | category | flops | bytes accessed | tf_op | source)
XLA Modules:
  0.0 80.6 jit_solution(903267472870197480)
XLA Ops:
  0.0 0.3 negate_convert_fusion.1
  0.3 0.3 fusion.80
  0.6 0.3 fusion.75
  0.8 1.3 %convolution_bitcast_fusion.2 = f32[2,8,128,128]{3,2,1,0:T(8,128)S(1)} fusion(bf16[2,8,128,128]{3,1,2,0:T(8,128)(2,1)} %bitcast.101, bf16[1,128,2,128]{3,1,2,0:T(8,128)(2,1)S(1)} %get-tuple-element.42, bf16[1,128,2,128]{3,1,2,0:T(8,128)(2,1)S(1)} %get-tuple-element.41), kind=kOutput, calls=%fused_computation.9 | convolution fusion | flops 134479872 | bytes 1703936 | tf_op jit(solution)/shard_map/akcn,cpnm->apkm/dot_general | solution.py:72
  2.2 0.0 copy-start
  2.2 0.1 subtract_convert_fusion
  2.4 0.3 fusion.1
  2.7 0.3 copy.25
  3.0 0.2 convert_element_type.126
  3.2 0.4 copy.26
  3.7 0.0 copy-done
  3.7 16.0 %while.1 = (s32[]{:T(128)}, bf16[8,2,16448]{2,1,0:T(2,128)(2,1)S(1)}, s32[8,3]{0,1:T(4,128)S(1)}, bf16[8,2,16384]{2,1,0:T(2,128)(2,1)S(1)}, s32[]{:T(128)}) while((s32[]{:T(128)}, bf16[8,2,16448]{2,1,0:T(2,128)(2,1)S(1)}, s32[8,3]{0,1:T(4,128)S(1)}, bf16[8,2,16384]{2,1,0:T(2,128)(2,1)S(1)}, s32[]{:T(128)}) %tuple.31), condition=%wide.while_cond, body=%wide.while_body.sunk | while | flops 2 | bytes 131189 | solution.py:90
  3.7 0.1 constant_dynamic-slice_fusion.2
  3.8 0.6 fusion.108
  4.3 1.4 %dynamic-slice_dynamic-update-slice_fusion.2 = bf16[8,2,16384]{2,1,0:T(2,128)(2,1)S(1)} fusion(bf16[8,2,16384]{2,1,0:T(2,128)(2,1)S(1)} %get-tuple-element.89, s32[]{:T(128)} %get-tuple-element.86, bf16[8,2,16448]{2,1,0:T(2,128)(2,1)S(1)} %get-tuple-element.92, s32[]{:T(128)} %bitcast.99, s32[]{:T(128)} %bitcast.100), kind=kLoop, calls=%fused_computation.clone.1 | loop fusion | bytes 131084 | tf_op jit(solution)/shard_map/vmap()/gather
  5.7 0.1 constant_dynamic-slice_fusion.2
  5.8 0.6 fusion.108
  6.3 1.4 %dynamic-slice_dynamic-update-slice_fusion.2 = bf16[8,2,16384]{2,1,0:T(2,128)(2,1)S(1)} fusion(bf16[8,2,16384]{2,1,0:T(2,128)(2,1)S(1)} %get-tuple-element.89, s32[]{:T(128)} %get-tuple-element.86, bf16[8,2,16448]{2,1,0:T(2,128)(2,1)S(1)} %get-tuple-element.92, s32[]{:T(128)} %bitcast.99, s32[]{:T(128)} %bitcast.100), kind=kLoop, calls=%fused_computation.clone.1 | loop fusion | bytes 131084 | tf_op jit(solution)/shard_map/vmap()/gather
  7.7 0.1 constant_dynamic-slice_fusion.2
  7.8 0.6 fusion.108
  8.3 1.4 %dynamic-slice_dynamic-update-slice_fusion.2 = bf16[8,2,16384]{2,1,0:T(2,128)(2,1)S(1)} fusion(bf16[8,2,16384]{2,1,0:T(2,128)(2,1)S(1)} %get-tuple-element.89, s32[]{:T(128)} %get-tuple-element.86, bf16[8,2,16448]{2,1,0:T(2,128)(2,1)S(1)} %get-tuple-element.92, s32[]{:T(128)} %bitcast.99, s32[]{:T(128)} %bitcast.100), kind=kLoop, calls=%fused_computation.clone.1 | loop fusion | bytes 131084 | tf_op jit(solution)/shard_map/vmap()/gather
  9.7 0.1 constant_dynamic-slice_fusion.2
  9.8 0.6 fusion.108
  10.4 1.4 %dynamic-slice_dynamic-update-slice_fusion.2 = bf16[8,2,16384]{2,1,0:T(2,128)(2,1)S(1)} fusion(bf16[8,2,16384]{2,1,0:T(2,128)(2,1)S(1)} %get-tuple-element.89, s32[]{:T(128)} %get-tuple-element.86, bf16[8,2,16448]{2,1,0:T(2,128)(2,1)S(1)} %get-tuple-element.92, s32[]{:T(128)} %bitcast.99, s32[]{:T(128)} %bitcast.100), kind=kLoop, calls=%fused_computation.clone.1 | loop fusion | bytes 131084 | tf_op jit(solution)/shard_map/vmap()/gather
  11.7 0.1 constant_dynamic-slice_fusion.2
  11.8 0.6 fusion.108
  12.4 1.4 %dynamic-slice_dynamic-update-slice_fusion.2 = bf16[8,2,16384]{2,1,0:T(2,128)(2,1)S(1)} fusion(bf16[8,2,16384]{2,1,0:T(2,128)(2,1)S(1)} %get-tuple-element.89, s32[]{:T(128)} %get-tuple-element.86, bf16[8,2,16448]{2,1,0:T(2,128)(2,1)S(1)} %get-tuple-element.92, s32[]{:T(128)} %bitcast.99, s32[]{:T(128)} %bitcast.100), kind=kLoop, calls=%fused_computation.clone.1 | loop fusion | bytes 131084 | tf_op jit(solution)/shard_map/vmap()/gather
  13.7 0.1 constant_dynamic-slice_fusion.2
  13.8 0.6 fusion.108
  14.4 1.4 %dynamic-slice_dynamic-update-slice_fusion.2 = bf16[8,2,16384]{2,1,0:T(2,128)(2,1)S(1)} fusion(bf16[8,2,16384]{2,1,0:T(2,128)(2,1)S(1)} %get-tuple-element.89, s32[]{:T(128)} %get-tuple-element.86, bf16[8,2,16448]{2,1,0:T(2,128)(2,1)S(1)} %get-tuple-element.92, s32[]{:T(128)} %bitcast.99, s32[]{:T(128)} %bitcast.100), kind=kLoop, calls=%fused_computation.clone.1 | loop fusion | bytes 131084 | tf_op jit(solution)/shard_map/vmap()/gather
  15.7 0.1 constant_dynamic-slice_fusion.2
  15.8 0.6 fusion.108
  16.4 1.4 %dynamic-slice_dynamic-update-slice_fusion.2 = bf16[8,2,16384]{2,1,0:T(2,128)(2,1)S(1)} fusion(bf16[8,2,16384]{2,1,0:T(2,128)(2,1)S(1)} %get-tuple-element.89, s32[]{:T(128)} %get-tuple-element.86, bf16[8,2,16448]{2,1,0:T(2,128)(2,1)S(1)} %get-tuple-element.92, s32[]{:T(128)} %bitcast.99, s32[]{:T(128)} %bitcast.100), kind=kLoop, calls=%fused_computation.clone.1 | loop fusion | bytes 131084 | tf_op jit(solution)/shard_map/vmap()/gather
  17.7 0.1 constant_dynamic-slice_fusion.2
  17.8 0.6 fusion.108
  18.4 1.4 %dynamic-slice_dynamic-update-slice_fusion.2 = bf16[8,2,16384]{2,1,0:T(2,128)(2,1)S(1)} fusion(bf16[8,2,16384]{2,1,0:T(2,128)(2,1)S(1)} %get-tuple-element.89, s32[]{:T(128)} %get-tuple-element.86, bf16[8,2,16448]{2,1,0:T(2,128)(2,1)S(1)} %get-tuple-element.92, s32[]{:T(128)} %bitcast.99, s32[]{:T(128)} %bitcast.100), kind=kLoop, calls=%fused_computation.clone.1 | loop fusion | bytes 131084 | tf_op jit(solution)/shard_map/vmap()/gather
  19.7 0.4 reshape.681
  20.1 1.1 %copy.28 = bf16[2,8,16,1024]{3,1,0,2:T(8,128)(2,1)} copy(bf16[2,8,16,1024]{3,2,0,1:T(8,128)(2,1)S(1)} %reshape.681) | data formatting | bytes 1048576 | tf_op jit(solution)/shard_map/reshape | solution.py:130
  21.2 7.4 %all-to-all-start = ((bf16[2,8,16,1024]{3,1,0,2:T(8,128)(2,1)}), bf16[2,8,16,1024]{3,1,0,2:T(8,128)(2,1)S(1)}, u32[]{:S(2)}, u32[]{:S(2)}) async-start(bf16[2,8,16,1024]{3,1,0,2:T(8,128)(2,1)} %copy.28), calls=%async_computation | async-start | bytes 1048576 | tf_op jit(solution)/shard_map/all_to_all | solution.py:131
  28.6 0.6 negate_convert_fusion
  29.3 13.8 %all-to-all-done = bf16[2,8,16,1024]{3,1,0,2:T(8,128)(2,1)S(1)} async-done(((bf16[2,8,16,1024]{3,1,0,2:T(8,128)(2,1)}), bf16[2,8,16,1024]{3,1,0,2:T(8,128)(2,1)S(1)}, u32[]{:S(2)}, u32[]{:S(2)}) %all-to-all-start) | async-done | bytes 524320 | tf_op jit(solution)/shard_map/all_to_all | solution.py:131
  43.1 0.4 bitcast_convert_fusion
  43.5 1.6 %collective-permute-start = (bf16[2,256,1024]{2,1,0:T(8,128)(2,1)S(1)}, bf16[2,256,1024]{2,1,0:T(8,128)(2,1)S(1)}, u32[]{:S(2)}, u32[]{:S(2)}) collective-permute-start(bf16[2,256,1024]{2,1,0:T(8,128)(2,1)S(1)} %bitcast_convert_fusion), channel_id=1, source_target_pairs={{0,16},{16,0},{1,17},{17,1},{2,18},{18,2},{3,19},{19,3},{4,20},{20... | collective-permute-start | bytes 3145736 | tf_op jit(solution)/shard_map/ppermute | solution.py:18
  45.2 0.3 copy.30
  45.4 23.2 %collective-permute-done = bf16[2,256,1024]{2,1,0:T(8,128)(2,1)S(1)} collective-permute-done((bf16[2,256,1024]{2,1,0:T(8,128)(2,1)S(1)}, bf16[2,256,1024]{2,1,0:T(8,128)(2,1)S(1)}, u32[]{:S(2)}, u32[]{:S(2)}) %collective-permute-start) | collective-permute-done | bytes 1048608 | tf_op jit(solution)/shard_map/ppermute | solution.py:18
  68.7 0.3 copy.31
  69.0 1.4 %convolution_bitcast_fusion = f32[2,2,256,1024]{2,3,1,0:T(8,128)S(1)} fusion(bf16[1,2,128,1024]{2,3,1,0:T(8,128)(2,1)S(1)} %copy.31, bf16[1,2,128,1024]{2,3,1,0:T(8,128)(2,1)S(1)} %copy.30, f32[256]{0:T(256)S(1)} %multiply_add_fusion.1), kind=kOutput, calls=%fused_computation.2 | convolution fusion | flops 270303232 | bytes 5243904 | tf_op jit(solution)/shard_map/jh,kchg->kcjg/dot_general | solution.py:102
  70.4 8.8 %fusion.8 = (bf16[1,256,1024]{1,2,0:T(8,128)(2,1)S(1)}, bf16[1,256,1024]{1,2,0:T(8,128)(2,1)S(1)}) fusion(f32[2,2,256,1024]{2,3,1,0:T(8,128)S(1)} %convolution_bitcast_fusion, f32[256]{0:T(256)S(1)} %get-tuple-element.51, f32[1024]{0:T(1024)S(1)} %divide_multiply_fusion, f32[256]{0:T(256)S(1)} %get-tuple-element.50), kind=kLoop, calls=%fused_computation.18 | loop fusion | flops 5767168 | bytes 5249024 | tf_op jit(solution)/shard_map/convert
  79.2 0.1 pad_maximum_fusion
  79.3 1.3 %copy.32 = bf16[2,256,1024]{2,1,0:T(8,128)(2,1)} copy(bf16[2,256,1024]{1,2,0:T(8,128)(2,1)S(1)} %pad_maximum_fusion) | data formatting | bytes 2097152 | tf_op jit(solution)/shard_map/stack | solution.py:117
  (14 shorter events, 0.2 us)
Async XLA Ops:
  2.2 1.5 %copy-start = (s32[8]{0:T(128)S(1)}, s32[8]{0:T(128)}, u32[]{:S(2)}) copy-start(s32[8]{0:T(128)} %param.3) | copy-start | bytes 100
  21.2 21.9 %all-to-all-start = ((bf16[2,8,16,1024]{3,1,0,2:T(8,128)(2,1)}), bf16[2,8,16,1024]{3,1,0,2:T(8,128)(2,1)S(1)}, u32[]{:S(2)}, u32[]{:S(2)}) async-start(bf16[2,8,16,1024]{3,1,0,2:T(8,128)(2,1)} %copy.28), calls=%async_computation | async-start | bytes 1048576 | tf_op jit(solution)/shard_map/all_to_all | solution.py:131
  43.5 25.1 %collective-permute-start = (bf16[2,256,1024]{2,1,0:T(8,128)(2,1)S(1)}, bf16[2,256,1024]{2,1,0:T(8,128)(2,1)S(1)}, u32[]{:S(2)}, u32[]{:S(2)}) collective-permute-start(bf16[2,256,1024]{2,1,0:T(8,128)(2,1)S(1)} %bitcast_convert_fusion), channel_id=1, source_target_pairs={{0,16},{16,0},{1,17},{17,1},{2,18},{18,2},{3,19},{19,3},{4,20},{20... | collective-permute-start | bytes 3145736 | tf_op jit(solution)/shard_map/ppermute | solution.py:18
where the time goes:
time: 81 us; the launch traced here: 80.6 us
  waiting for transfers between devices  37 us (46%)
  local copies, waits for them, and re-layouts  20.2 us (25%)
  other arithmetic  10.6 us (13%)
  starting transfers between devices  8.95 us (11%)
  matrix products  3.48 us (4%)
    ppermute x1, waiting for transfers between devices, partner(): lax.ppermute(array, axis, [(i, i ^ 1 << apart) for i in range(lax.axis_si...  23.2 us
    gather x24, local copies, waits for them, and re-layouts  15.9 us
    all_to_all x1, waiting for transfers between devices, per_device(): lax.all_to_all(layout, 'gate', split_axis=2, concat_axis=1, tiled=True)  13.8 us
    another operation x5, other arithmetic  10.1 us
    all_to_all x1, starting transfers between devices, per_device(): lax.all_to_all(layout, 'gate', split_axis=2, concat_axis=1, tiled=True)  7.4 us
  transfers between devices with their start and end apart: 2, of which 2 were waited for; matrix products, arithmetic and copies ran while one was open for 1% of the time, Pallas kernels for 0%

commit v1 on v0

v1 whole, which is shorter than its diff:
```python
import math

import jax
import jax.numpy as jnp
import numpy as np
from jax import lax
from jax.experimental import pallas as pl
from jax.experimental.pallas import tpu as pltpu
from jax.sharding import PartitionSpec as P

RADIX = 128
SAMPLES = 16384
ANGLES = 256
DELAY_MAX = 64
LANES = 128
ROWS = RADIX + DELAY_MAX


TWO_PI = 2.0 * math.pi


def to_bf16(values):
    return np.asarray(values, np.float32).astype(jnp.bfloat16)


def rounded(values):
    return to_bf16(values).astype(np.float64)


def real_form(table):
    upper = np.concatenate([table.real, -table.imag], axis=1)
    lower = np.concatenate([table.imag, table.real], axis=1)
    return np.concatenate([upper, lower], axis=0)


def unit(phases):
    return np.cos(phases) + 1j * np.sin(phases)


def dft_table():
    counter = np.arange(RADIX)
    table = unit(-TWO_PI / RADIX * (counter[:, None] * counter[None, :] % RADIX)) / math.sqrt(RADIX)
    return rounded(table.real) + 1j * rounded(table.imag)


def twiddles():
    phases = -TWO_PI / SAMPLES * (np.arange(ROWS)[:, None] * np.arange(RADIX)[None, :])
    return np.stack([np.cos(phases), np.sin(phases)]).astype(np.float32)


def near_phases(depth_count, sub_pulses):
    centers = [sub_pulses * 2 ** (depth - 1) // 2 for depth in range(1, depth_count + 1)]
    center_sq = float(sum(center * center for center in centers))
    phases = -TWO_PI / (4 * ANGLES) * center_sq / (16.0 * (SAMPLES + np.arange(SAMPLES)))
    return np.stack([np.cos(phases), np.sin(phases)]).astype(np.float32).reshape(2, RADIX, RADIX)


def steer_table(sub_pulses):
    modulus = 16 * ANGLES
    beams = 2 * np.arange(ANGLES) - ANGLES + 1
    pulses = 2 * np.arange(sub_pulses) - sub_pulses + 1
    table = unit(-TWO_PI / modulus * (beams[:, None] * pulses[None, :] % modulus)) / math.sqrt(sub_pulses)
    return rounded(table.real) + 1j * rounded(table.imag)


def interp_table():
    distance = np.arange(ANGLES)[:, None] * 0.5 - 0.25 - np.arange(ANGLES // 2)[None, :]
    taper = np.where(np.abs(distance) < 4.0, 0.5 + 0.5 * np.cos(math.pi * distance / 4.0), 0.0)
    return rounded(np.sinc(distance) * taper)


def merge_table(depth, sector, center):
    modulus = ANGLES * 2 ** (depth + 3)
    row_index = sector * ANGLES + np.arange(ANGLES)
    numerator = 2 * row_index + 1 - ANGLES * 2**depth
    turns = (center * numerator) % modulus / modulus
    return unit(-TWO_PI * turns)[:, None] * interp_table() / math.sqrt(2.0)


def by_source(table, pulse_count):
    rows = table.shape[0]
    return table.reshape(rows, 2, -1, pulse_count).transpose(0, 2, 1, 3).reshape(rows, -1)


def image_tables(sub_pulses, pulse_count):
    half = ANGLES // 2
    steer = steer_table(sub_pulses)
    tables = []
    for sub in range(2):
        beams = steer[sub * half : (sub + 1) * half]
        own = (2 * sub - 1) * (sub_pulses // 2)
        parts = [real_form(merge_table(1, sub, center) @ beams) for center in (own, -own)]
        tables.append(np.concatenate([by_source(part, pulse_count) for part in parts], axis=1))
    return to_bf16(np.stack(tables))


def compress_kernel(
    delays, raw, first, second, twiddle, near, out, lines, grid_in, section, twisted, turned
):
    pulse_count = raw.shape[1]
    blocks, _, width = out.shape
    span = RADIX * pulse_count
    for part in range(2):
        for step in range(RADIX):
            lines[pl.ds(part * span + step * pulse_count, pulse_count), :] = raw[
                part, :, pl.ds(step * LANES, LANES)
            ].astype(jnp.float32)
    for part in range(2):
        for pulse in range(pulse_count):
            grid_in[pl.ds(part * RADIX, RADIX), pl.ds(pulse * LANES, LANES)] = lines[
                pl.ds(part * span + pulse, RADIX, stride=pulse_count), :
            ].astype(jnp.bfloat16)
    for pulse in range(pulse_count):
        columns = pl.ds(pulse * LANES, LANES)
        sums = jnp.dot(first[...], grid_in[:, columns], preferred_element_type=jnp.float32)
        for part in range(2):
            own = sums[part * RADIX : (part + 1) * RADIX]
            section[pulse, part, pl.ds(0, RADIX), :] = own
            section[pulse, part, pl.ds(RADIX, DELAY_MAX), :] = own[:DELAY_MAX]
    for pulse in range(pulse_count):
        window = pl.ds(delays[pulse], RADIX)
        real_part = section[pulse, 0, window, :]
        imag_part = section[pulse, 1, window, :]
        cosine = twiddle[0, window, :]
        sine_part = twiddle[1, window, :]
        rows = pl.ds(pulse * RADIX, RADIX)
        twisted[rows, pl.ds(0, LANES)] = (real_part * cosine - imag_part * sine_part).astype(jnp.bfloat16)
        twisted[rows, pl.ds(LANES, LANES)] = (real_part * sine_part + imag_part * cosine).astype(jnp.bfloat16)
    row_index = lax.broadcasted_iota(jnp.int32, (RADIX, LANES), 0)
    lane_index = lax.broadcasted_iota(jnp.int32, (RADIX, LANES), 1)
    gates = row_index * LANES + lane_index
    for pulse in range(pulse_count):
        sums = lax.dot_general(
            second[...],
            twisted[pl.ds(pulse * RADIX, RADIX), :],
            (((1,), (1,)), ((), ())),
            preferred_element_type=jnp.float32,
        )
        inside = gates < SAMPLES - delays[pulse]
        real_part, imag_part = sums[:RADIX], sums[RADIX:]
        cosine, sine_part = near[0], near[1]
        turned[pl.ds(pulse, RADIX, stride=pulse_count), :] = jnp.where(
            inside, real_part * cosine - imag_part * sine_part, 0.0
        )
        turned[pl.ds(span + pulse, RADIX, stride=pulse_count), :] = jnp.where(
            inside, real_part * sine_part + imag_part * cosine, 0.0
        )
    for step in range(RADIX):
        block, column = divmod(step * LANES, width)
        rows = pl.ds(step * pulse_count, pulse_count)
        both = jnp.concatenate(
            [turned[rows, :], turned[pl.ds(span + step * pulse_count, pulse_count), :]], axis=0
        )
        out[block, :, pl.ds(column, LANES)] = both.astype(jnp.bfloat16)


def range_compress(raw_echo, delays, depth_count, sub_pulses, gate_count):
    pulse_count = raw_echo.shape[1]
    width = SAMPLES // gate_count
    span = RADIX * pulse_count
    dft = to_bf16(real_form(dft_table()))
    vmem = pl.BlockSpec(memory_space=pltpu.VMEM)
    return pl.pallas_call(
        compress_kernel,
        out_shape=jax.ShapeDtypeStruct((gate_count, 2 * pulse_count, width), jnp.bfloat16),
        in_specs=[pl.BlockSpec(memory_space=pltpu.SMEM)] + [vmem] * 5,
        out_specs=vmem,
        scratch_shapes=[
            pltpu.VMEM((2 * span, LANES), jnp.float32),
            pltpu.VMEM((2 * RADIX, pulse_count * LANES), jnp.bfloat16),
            pltpu.VMEM((pulse_count, 2, ROWS, LANES), jnp.float32),
            pltpu.VMEM((span, 2 * LANES), jnp.bfloat16),
            pltpu.VMEM((2 * span, LANES), jnp.float32),
        ],
        compiler_params=pltpu.CompilerParams(vmem_limit_bytes=32 * 2**20),
        name="compress",
    )(delays, raw_echo, dft, dft, twiddles(), near_phases(depth_count, sub_pulses))


def image_kernel(table, own, other, out):
    depth = own.shape[0]
    rows, columns = out.shape
    tile_rows, tile_columns = min(rows, 256), min(columns, 256)
    for row in range(0, rows, tile_rows):
        for column in range(0, columns, tile_columns):
            place = pl.ds(row, tile_rows), pl.ds(column, tile_columns)
            total = jnp.dot(
                table[place[0], pl.ds(0, depth)], own[:, place[1]], preferred_element_type=jnp.float32
            ) + jnp.dot(
                table[place[0], pl.ds(depth, depth)], other[:, place[1]], preferred_element_type=jnp.float32
            )
            out[place] = total.astype(jnp.bfloat16)


def form_image(table, own, other):
    vmem = pl.BlockSpec(memory_space=pltpu.VMEM)
    image = pl.pallas_call(
        image_kernel,
        out_shape=jax.ShapeDtypeStruct((2 * ANGLES, own.shape[1]), jnp.bfloat16),
        in_specs=[vmem] * 3,
        out_specs=vmem,
        compiler_params=pltpu.CompilerParams(vmem_limit_bytes=32 * 2**20),
        name="image",
    )(table, own, other)
    return image.reshape(2, ANGLES, own.shape[1])


def partner(array, axis, apart):
    return lax.ppermute(array, axis, [(i, i ^ 1 << apart) for i in range(lax.axis_size(axis))])


def merge_levels(received, pulse_count, sub_pulses, depth_count):
    half = ANGLES // 2
    sub_index = lax.axis_index("sub")
    steering = to_bf16(by_source(real_form(steer_table(sub_pulses)), pulse_count))
    current = jnp.dot(steering, received, preferred_element_type=jnp.float32).astype(jnp.bfloat16)
    current = current.reshape(2, ANGLES, -1)
    sector = jnp.zeros((), jnp.int32)
    interp = jnp.asarray(interp_table(), jnp.float32)
    for depth in range(1, depth_count + 1):
        side_bit = sub_index // 2 ** (depth - 1) % 2
        sent = lax.dynamic_slice_in_dim(current, (1 - side_bit) * half, half, axis=1)
        kept = lax.dynamic_slice_in_dim(current, side_bit * half, half, axis=1)
        arrived = partner(sent, "sub", depth - 1)
        sector = 2 * sector + side_bit
        modulus = ANGLES * 2 ** (depth + 3)
        numerator = 2 * (sector * ANGLES + jnp.arange(ANGLES, dtype=jnp.int32)) + 1 - ANGLES * 2**depth
        center = (2 * side_bit - 1) * (sub_pulses * 2 ** (depth - 1) // 2)
        total = 0.0
        for child, place in ((kept, center), (arrived, -center)):
            turns = jnp.mod(place * numerator, modulus).astype(jnp.float32) / modulus
            cosine = (jnp.cos(TWO_PI * turns) * math.sqrt(0.5))[:, None] * interp
            sine_part = (-jnp.sin(TWO_PI * turns) * math.sqrt(0.5))[:, None] * interp
            table = jnp.stack([jnp.stack([cosine, -sine_part]), jnp.stack([sine_part, cosine])])
            total = total + jnp.einsum(
                "akjh,khg->ajg", table.astype(jnp.bfloat16), child, preferred_element_type=jnp.float32
            )
        current = total.astype(jnp.bfloat16)
    return current


def per_device(raw_echo, delays):
    gate_count = lax.axis_size("gate")
    sub_count = lax.axis_size("sub")
    pulse_count = raw_echo.shape[1]
    sub_pulses = pulse_count * gate_count
    depth_count = sub_count.bit_length() - 1
    compressed = range_compress(raw_echo, delays, depth_count, sub_pulses, gate_count)
    received = lax.all_to_all(compressed, "gate", split_axis=0, concat_axis=0, tiled=True)
    received = received.reshape(2 * sub_pulses, SAMPLES // gate_count)
    if depth_count != 1:
        return merge_levels(received, pulse_count, sub_pulses, depth_count)
    other = partner(received, "sub", 0)
    tables = jnp.asarray(image_tables(sub_pulses, pulse_count))
    table = lax.dynamic_index_in_dim(tables, lax.axis_index("sub"), 0, keepdims=False)
    return form_image(table, received, other)


def solution(mesh):
    placed = (P(None, ("sub", "gate"), None), P(("sub", "gate")))
    return jax.shard_map(
        per_device, mesh=mesh, in_specs=placed, out_specs=P(None, "sub", "gate"), check_vma=False
    )
```

time: 81 us -> 43.7 us (0.54)
  waiting for transfers between devices: 37 us -> 12.3 us
  blocking collectives: 0 us -> 21.6 us
  local copies, waits for them, and re-layouts: 20.2 us -> 4.47 us
  other arithmetic: 10.6 us -> 0 us
  starting transfers between devices: 8.95 us -> 1.5 us
  Pallas kernels: 0 us -> 3.55 us
  matrix products: 3.48 us -> 0 us
    all_to_all x0 -> x1, blocking collectives: none -> 21.6 us  [per_device(): lax.all_to_all(compressed, 'gate', split_axis=0, concat_axis=0, tiled=True)]
    gather x24 -> x0, local copies, waits for them, and re-layouts: 15.9 us -> none
    all_to_all x1 -> x0, waiting for transfers between devices: 13.8 us -> none  [per_device(): lax.all_to_all(layout, 'gate', split_axis=2, concat_axis=1, tiled=True)]
    ppermute x1, waiting for transfers between devices: 23.2 us -> 12.3 us  [partner(): lax.ppermute(array, axis, [(i, i ^ 1 << apart) for i in range(lax.axis_si...]
    another operation x8 -> x0, other arithmetic: 10.2 us -> none
    all_to_all x1 -> x0, starting transfers between devices: 7.4 us -> none  [per_device(): lax.all_to_all(layout, 'gate', split_axis=2, concat_axis=1, tiled=True)]
    unnamed x4 -> x12, local copies, waits for them, and re-layouts: 0.42 us -> 4.43 us
    pallas_call x0 -> x2, Pallas kernels: none -> 3.55 us  [the longest x1 1.85 us: range_compress(): pl.pallas_call(compress_kernel, out_shape=jax.ShapeDtypeStruct((gate_coun...]
  transfers between devices with their start and end apart: 2 -> 1, of which waited for: 2 -> 1; matrix products, arithmetic and copies ran while one was open for 1% -> 0% of each run, Pallas kernels for 0% -> 0%
where the time goes in v1:
time: 43.7 us; the launch traced here: 43.5 us
  blocking collectives  21.6 us (49%)
  waiting for transfers between devices  12.3 us (28%)
  local copies, waits for them, and re-layouts  4.47 us (10%)
  Pallas kernels  3.55 us (8%)
  starting transfers between devices  1.5 us (3%)
    all_to_all x1, blocking collectives, per_device(): lax.all_to_all(compressed, 'gate', split_axis=0, concat_axis=0, tiled=True)  21.6 us
    ppermute x1, waiting for transfers between devices, partner(): lax.ppermute(array, axis, [(i, i ^ 1 << apart) for i in range(lax.axis_si...  12.3 us
    unnamed x12, local copies, waits for them, and re-layouts  4.43 us
    pallas_call x1, Pallas kernels, range_compress(): pl.pallas_call(compress_kernel, out_shape=jax.ShapeDtypeStruct((gate_coun...  1.85 us
    pallas_call x1, Pallas kernels, form_image(): pl.pallas_call(image_kernel, out_shape=jax.ShapeDtypeStruct((2 * ANGLES,...  1.69 us
    ppermute x1, starting transfers between devices, partner(): lax.ppermute(array, axis, [(i, i ^ 1 << apart) for i in range(lax.axis_si...  1.5 us
  transfers between devices with their start and end apart: 1, of which 1 were waited for; matrix products, arithmetic and copies ran while one was open for 0% of the time, Pallas kernels for 0%

profile of v1, /device:TPU:0, one launch (start us, length us, event | category | flops | bytes accessed | tf_op | source)
XLA Modules:
  0.0 43.5 jit_solution(9486795792880600418)
XLA Ops:
  0.0 0.0 copy-start
  0.0 0.9 %copy-done = bf16[256,256]{1,0:T(8,128)(2,1)S(1)} copy-done((bf16[256,256]{1,0:T(8,128)(2,1)S(1)}, bf16[256,256]{1,0:T(8,128)(2,1)}, u32[]{:S(2)}) %copy-start) | copy-done | bytes 131096
  0.9 0.0 copy-start.1
  0.9 1.0 %copy-done.1 = bf16[2,8,16384]{2,1,0:T(8,128)(2,1)S(1)} copy-done((bf16[2,8,16384]{2,1,0:T(8,128)(2,1)S(1)}, bf16[2,8,16384]{2,1,0:T(8,128)(2,1)}, u32[]{:S(2)}) %copy-start.1) | copy-done | bytes 524312
  1.9 0.0 copy-start.2
  1.9 0.9 %copy-done.2 = f32[2,192,128]{2,1,0:T(8,128)S(1)} copy-done((f32[2,192,128]{2,1,0:T(8,128)S(1)}, f32[2,192,128]{2,1,0:T(8,128)}, u32[]{:S(2)}) %copy-start.2) | copy-done | bytes 196632
  2.9 0.0 copy-start.3
  2.9 0.9 %copy-done.3 = f32[2,128,128]{2,1,0:T(8,128)S(1)} copy-done((f32[2,128,128]{2,1,0:T(8,128)S(1)}, f32[2,128,128]{2,1,0:T(8,128)}, u32[]{:S(2)}) %copy-start.3) | copy-done | bytes 131096
  3.8 0.0 copy-start.4
  3.8 0.7 %copy-done.4 = s32[8]{0:T(128)S(1)} copy-done((s32[8]{0:T(128)S(1)}, s32[8]{0:T(128)}, u32[]{:S(2)}) %copy-start.4) | copy-done | bytes 56
  4.4 0.0 copy-start.5
  4.4 1.9 %compress.1 = bf16[16,16,1024]{2,1,0:T(8,128)(2,1)S(1)} custom-call(s32[8]{0:T(128)S(1)} %copy-done.4, bf16[2,8,16384]{2,1,0:T(8,128)(2,1)S(1)} %copy-done.1, bf16[256,256]{1,0:T(8,128)(2,1)S(1)} %copy-done, bf16[256,256]{1,0:T(8,128)(2,1)S(1)} %copy-done, f32[2,192,128]{2,1,0:T(8,128)S(1)} %copy-done.2, f32[2,128,128]{2,1,0:T(8,128)S(1)} %copy-done.3), custom_call_target="tpu_custom_call" | custom-call | tf_op jit(solution)/shard_map/compress/pallas_call | solution.py:163
  6.3 21.6 %all_to_all.5 = bf16[16,16,1024]{2,1,0:T(8,128)(2,1)S(1)} all-to-all(bf16[16,16,1024]{2,1,0:T(8,128)(2,1)S(1)} %compress.1), channel_id=1, replica_groups=mesh['sub'=2,'gate'=16] {'gate'}, dimensions={0} | all-to-all | bytes 1048576 | tf_op jit(solution)/shard_map/all_to_all | solution.py:249
  27.9 1.5 %collective-permute-start = (bf16[256,1024]{1,0:T(8,128)(2,1)S(1)}, bf16[256,1024]{1,0:T(8,128)(2,1)S(1)}, u32[]{:S(2)}, u32[]{:S(2)}) collective-permute-start(bf16[256,1024]{1,0:T(8,128)(2,1)S(1)} %bitcast.4), channel_id=1, source_target_pairs={{0,16},{16,0},{1,17},{17,1},{2,18},{18,2},{3,19},{19,3},{4,20},{20... | collective-permute-start | bytes 1572872 | tf_op jit(solution)/shard_map/ppermute | solution.py:209
  29.4 0.0 copy-done.5
  29.5 12.3 %collective-permute-done.other = bf16[256,1024]{1,0:T(8,128)(2,1)S(1)} collective-permute-done((bf16[256,1024]{1,0:T(8,128)(2,1)S(1)}, bf16[256,1024]{1,0:T(8,128)(2,1)S(1)}, u32[]{:S(2)}, u32[]{:S(2)}) %collective-permute-start) | collective-permute-done | bytes 524320 | tf_op jit(solution)/shard_map/ppermute | solution.py:209
  41.8 1.7 %image.1 = bf16[512,1024]{1,0:T(8,128)(2,1)} custom-call(bf16[512,512]{1,0:T(8,128)(2,1)S(1)} %dynamic-slice_bitcast_fusion.table, bf16[256,1024]{1,0:T(8,128)(2,1)S(1)} %bitcast.5, bf16[256,1024]{1,0:T(8,128)(2,1)S(1)} %collective-permute-done.other), custom_call_target="tpu_custom_call" | custom-call | tf_op jit(solution)/shard_map/image/pallas_call | solution.py:197
  (1 shorter events, 0.0 us)
Async XLA Ops:
  0.0 0.9 %copy-start = (bf16[256,256]{1,0:T(8,128)(2,1)S(1)}, bf16[256,256]{1,0:T(8,128)(2,1)}, u32[]{:S(2)}) copy-start(bf16[256,256]{1,0:T(8,128)(2,1)} %constant.20.clone.first.second) | copy-start | bytes 393220
  0.9 1.0 %copy-start.1 = (bf16[2,8,16384]{2,1,0:T(8,128)(2,1)S(1)}, bf16[2,8,16384]{2,1,0:T(8,128)(2,1)}, u32[]{:S(2)}) copy-start(bf16[2,8,16384]{2,1,0:T(8,128)(2,1)} %raw.1) | copy-start | bytes 1572868
  1.9 0.9 %copy-start.2 = (f32[2,192,128]{2,1,0:T(8,128)S(1)}, f32[2,192,128]{2,1,0:T(8,128)}, u32[]{:S(2)}) copy-start(f32[2,192,128]{2,1,0:T(8,128)} %constant.21.clone.twiddle) | copy-start | bytes 589828
  2.9 0.9 %copy-start.3 = (f32[2,128,128]{2,1,0:T(8,128)S(1)}, f32[2,128,128]{2,1,0:T(8,128)}, u32[]{:S(2)}) copy-start(f32[2,128,128]{2,1,0:T(8,128)} %constant.22.clone.near) | copy-start | bytes 393220
  3.8 0.7 %copy-start.4 = (s32[8]{0:T(128)S(1)}, s32[8]{0:T(128)}, u32[]{:S(2)}) copy-start(s32[8]{0:T(128)} %delays.1) | copy-start | bytes 100
  4.4 25.0 %copy-start.5 = (bf16[2,512,512]{2,1,0:T(8,128)(2,1)S(1)}, bf16[2,512,512]{2,1,0:T(8,128)(2,1)}, u32[]{:S(2)}) copy-start(bf16[2,512,512]{2,1,0:T(8,128)(2,1)} %constant.23.clone) | copy-start | bytes 3145732
  27.9 13.8 %collective-permute-start = (bf16[256,1024]{1,0:T(8,128)(2,1)S(1)}, bf16[256,1024]{1,0:T(8,128)(2,1)S(1)}, u32[]{:S(2)}, u32[]{:S(2)}) collective-permute-start(bf16[256,1024]{1,0:T(8,128)(2,1)S(1)} %bitcast.4), channel_id=1, source_target_pairs={{0,16},{16,0},{1,17},{17,1},{2,18},{18,2},{3,19},{19,3},{4,20},{20... | collective-permute-start | bytes 1572872 | tf_op jit(solution)/shard_map/ppermute | solution.py:209

commit v2 on v1

--- a/solution.py
+++ b/solution.py
@@ -1,3 +1,4 @@
+import functools
 import math
 
 import jax
@@ -13,6 +14,7 @@
 ANGLES = 256
 DELAY_MAX = 64
 LANES = 128
+RAW_PIECES = 4
 ROWS = RADIX + DELAY_MAX
 
 
@@ -95,13 +97,35 @@
 
 
 def compress_kernel(
-    delays, raw, first, second, twiddle, near, out, lines, grid_in, section, twisted, turned
+    plan, delays, raw_far, dft_far, twiddle_far, near_far, *refs
 ):
+    outs = refs[: len(plan)]
+    (
+    raw, dft, twiddle, near, arrived, lines, grid_in, section, twisted, turned,
+    ) = refs[len(plan) :]
     pulse_count = raw.shape[1]
-    blocks, _, width = out.shape
+    width = outs[0].shape[-1]
+    me = lax.axis_index("gate")
     span = RADIX * pulse_count
-    for part in range(2):
-        for step in range(RADIX):
+    piece = SAMPLES // RAW_PIECES
+    pieces = [
+        pltpu.make_async_copy(
+            raw_far.at[:, :, pl.ds(index * piece, piece)],
+            raw.at[:, :, pl.ds(index * piece, piece)],
+            arrived.at[index],
+        )
+        for index in range(RAW_PIECES)
+    ]
+    tables = [
+        pltpu.make_async_copy(far, here, arrived.at[RAW_PIECES + index])
+        for index, (far, here) in enumerate(((dft_far, dft), (twiddle_far, twiddle), (near_far, near)))
+    ]
+    for copy in pieces + tables:
+        copy.start()
+    for step in range(RADIX):
+        if step * LANES % piece == 0:
+            pieces[step * LANES // piece].wait()
+        for part in range(2):
             lines[pl.ds(part * span + step * pulse_count, pulse_count), :] = raw[
                 part, :, pl.ds(step * LANES, LANES)
             ].astype(jnp.float32)
@@ -110,13 +134,15 @@
             grid_in[pl.ds(part * RADIX, RADIX), pl.ds(pulse * LANES, LANES)] = lines[
                 pl.ds(part * span + pulse, RADIX, stride=pulse_count), :
             ].astype(jnp.bfloat16)
+    tables[0].wait()
     for pulse in range(pulse_count):
         columns = pl.ds(pulse * LANES, LANES)
-        sums = jnp.dot(first[...], grid_in[:, columns], preferred_element_type=jnp.float32)
+        sums = jnp.dot(dft[...], grid_in[:, columns], preferred_element_type=jnp.float32)
         for part in range(2):
             own = sums[part * RADIX : (part + 1) * RADIX]
             section[pulse, part, pl.ds(0, RADIX), :] = own
             section[pulse, part, pl.ds(RADIX, DELAY_MAX), :] = own[:DELAY_MAX]
+    tables[1].wait()
     for pulse in range(pulse_count):
         window = pl.ds(delays[pulse], RADIX)
         real_part = section[pulse, 0, window, :]
@@ -129,9 +155,10 @@
     row_index = lax.broadcasted_iota(jnp.int32, (RADIX, LANES), 0)
     lane_index = lax.broadcasted_iota(jnp.int32, (RADIX, LANES), 1)
     gates = row_index * LANES + lane_index
+    tables[2].wait()
     for pulse in range(pulse_count):
         sums = lax.dot_general(
-            second[...],
+            dft[...],
             twisted[pl.ds(pulse * RADIX, RADIX), :],
             (((1,), (1,)), ((), ())),
             preferred_element_type=jnp.float32,
@@ -145,64 +172,79 @@
         turned[pl.ds(span + pulse, RADIX, stride=pulse_count), :] = jnp.where(
             inside, real_part * sine_part + imag_part * cosine, 0.0
         )
-    for step in range(RADIX):
-        block, column = divmod(step * LANES, width)
-        rows = pl.ds(step * pulse_count, pulse_count)
-        both = jnp.concatenate(
-            [turned[rows, :], turned[pl.ds(span + step * pulse_count, pulse_count), :]], axis=0
-        )
-        out[block, :, pl.ds(column, LANES)] = both.astype(jnp.bfloat16)
-
-
-def range_compress(raw_echo, delays, depth_count, sub_pulses, gate_count):
+    block_rows = width // LANES * pulse_count
+    for out, places in zip(outs, plan, strict=True):
+        for index, apart in enumerate(places):
+            start = pl.multiple_of((me ^ apart) * block_rows, block_rows)
+            for step in range(width // LANES):
+                rows = pl.ds(start + step * pulse_count, pulse_count)
+                both = jnp.concatenate([turned[rows, :], turned[pl.ds(span + start + step * pulse_count, pulse_count), :]], axis=0)
+                out[index, :, pl.ds(step * LANES, LANES)] = both.astype(jnp.bfloat16)
+
+
+def range_compress(raw_echo, delays, depth_count, sub_pulses, plan):
+    gate_count = lax.axis_size("gate")
     pulse_count = raw_echo.shape[1]
     width = SAMPLES // gate_count
     span = RADIX * pulse_count
     dft = to_bf16(real_form(dft_table()))
-    vmem = pl.BlockSpec(memory_space=pltpu.VMEM)
+    twiddle, near = twiddles(), near_phases(depth_count, sub_pulses)
     return pl.pallas_call(
-        compress_kernel,
-        out_shape=jax.ShapeDtypeStruct((gate_count, 2 * pulse_count, width), jnp.bfloat16),
-        in_specs=[pl.BlockSpec(memory_space=pltpu.SMEM)] + [vmem] * 5,
-        out_specs=vmem,
+        functools.partial(compress_kernel, plan),
+        out_shape=[
+            pltpu.VMEM((len(places), 2 * pulse_count, width), jnp.bfloat16) for places in plan
+        ],
+        in_specs=[pl.BlockSpec(memory_space=pltpu.SMEM)] + [pl.BlockSpec(memory_space=pltpu.HBM)] * 4,
+        out_specs=[pl.BlockSpec(memory_space=pltpu.VMEM)] * len(plan),
         scratch_shapes=[
+            pltpu.VMEM(raw_echo.shape, raw_echo.dtype),
+            pltpu.VMEM(dft.shape, dft.dtype),
+            pltpu.VMEM(twiddle.shape, twiddle.dtype),
+            pltpu.VMEM(near.shape, near.dtype),
+            pltpu.SemaphoreType.DMA((RAW_PIECES + 3,)),
             pltpu.VMEM((2 * span, LANES), jnp.float32),
             pltpu.VMEM((2 * RADIX, pulse_count * LANES), jnp.bfloat16),
             pltpu.VMEM((pulse_count, 2, ROWS, LANES), jnp.float32),
             pltpu.VMEM((span, 2 * LANES), jnp.bfloat16),
             pltpu.VMEM((2 * span, LANES), jnp.float32),
         ],
-        compiler_params=pltpu.CompilerParams(vmem_limit_bytes=32 * 2**20),
+        compiler_params=pltpu.CompilerParams(vmem_limit_bytes=60 * 2**20),
         name="compress",
-    )(delays, raw_echo, dft, dft, twiddles(), near_phases(depth_count, sub_pulses))
-
-
-def image_kernel(table, own, other, out):
-    depth = own.shape[0]
+    )(delays, raw_echo, dft, twiddle, near)
+
+
+def image_kernel(plan, table, *refs):
+    arrays, (out, data) = refs[: len(plan)], refs[len(plan) :]
     rows, columns = out.shape
+    depth = data.shape[0]
+    block = arrays[0].shape[1]
+    me = lax.axis_index("gate")
+    for array, (side, places) in zip(arrays, plan, strict=True):
+        for index, apart in enumerate(places):
+            start = pl.multiple_of(side * (depth // 2) + (me ^ apart) * block, block)
+            data[pl.ds(start, block), :] = array[index]
     tile_rows, tile_columns = min(rows, 256), min(columns, 256)
     for row in range(0, rows, tile_rows):
         for column in range(0, columns, tile_columns):
             place = pl.ds(row, tile_rows), pl.ds(column, tile_columns)
-            total = jnp.dot(
-                table[place[0], pl.ds(0, depth)], own[:, place[1]], preferred_element_type=jnp.float32
-            ) + jnp.dot(
-                table[place[0], pl.ds(depth, depth)], other[:, place[1]], preferred_element_type=jnp.float32
-            )
-            out[place] = total.astype(jnp.bfloat16)
-
-
-def form_image(table, own, other):
+            out[place] = jnp.dot(
+                table[place[0], :], data[:, place[1]], preferred_element_type=jnp.float32
+            ).astype(jnp.bfloat16)
+
+
+def form_image(table, arrays, plan):
     vmem = pl.BlockSpec(memory_space=pltpu.VMEM)
+    width = arrays[0].shape[-1]
     image = pl.pallas_call(
-        image_kernel,
-        out_shape=jax.ShapeDtypeStruct((2 * ANGLES, own.shape[1]), jnp.bfloat16),
-        in_specs=[vmem] * 3,
+        functools.partial(image_kernel, plan),
+        out_shape=jax.ShapeDtypeStruct((2 * ANGLES, width), jnp.bfloat16),
+        in_specs=[vmem] * (1 + len(arrays)),
         out_specs=vmem,
+        scratch_shapes=[pltpu.VMEM((table.shape[1], width), jnp.bfloat16)],
         compiler_params=pltpu.CompilerParams(vmem_limit_bytes=32 * 2**20),
         name="image",
-    )(table, own, other)
-    return image.reshape(2, ANGLES, own.shape[1])
+    )(table, *arrays)
+    return image.reshape(2, ANGLES, width)
 
 
 def partner(array, axis, apart):
@@ -239,21 +281,55 @@
     return current
 
 
+def swap(array, apart, other_sub=False):
+    count = lax.axis_size("gate")
+    if not other_sub:
+        return lax.ppermute(array, "gate", [(i, i ^ apart) for i in range(count)])
+    pairs = [(i, i ^ (count + apart)) for i in range(2 * count)]
+    return lax.ppermute(array, ("sub", "gate"), pairs)
+
+
+CORE, Y, Z = 1, 2, 4
+
+
+def corner_turn(send):
+    near, far = [0, Y], [CORE, CORE | Y]
+    plan = [near, [Z + i for i in near], [2 * Z + i for i in near], [3 * Z + i for i in near]]
+    plan.append([k * Z + i for k in range(4) for i in far])
+    own = send(plan)
+    mate = swap(own[4], CORE).reshape((4,) + own[0].shape)
+    both = [jnp.stack(pair, axis=1) for pair in zip(own[:4], mate, strict=True)]
+    moved = both[:1] + [swap(both[k], k * Z) for k in range(1, 4)]
+    groups = [moved[:2], moved[2:]]
+    arrays, places = [], []
+    for index, pair in enumerate(groups):
+        home = jnp.concatenate([half[0] for half in pair])
+        away = jnp.concatenate([half[1] for half in pair])
+        apart = [k * Z + core for k in (2 * index, 2 * index + 1) for core in (0, CORE)]
+        apart_y = [i + Y for i in apart]
+        arrays += [home, swap(away, Y, True), swap(home, 0, True), swap(away, Y)]
+        places += [(0, apart), (1, apart_y), (1, apart), (0, apart_y)]
+    return arrays, places
+
+
 def per_device(raw_echo, delays):
     gate_count = lax.axis_size("gate")
     sub_count = lax.axis_size("sub")
     pulse_count = raw_echo.shape[1]
     sub_pulses = pulse_count * gate_count
     depth_count = sub_count.bit_length() - 1
-    compressed = range_compress(raw_echo, delays, depth_count, sub_pulses, gate_count)
-    received = lax.all_to_all(compressed, "gate", split_axis=0, concat_axis=0, tiled=True)
-    received = received.reshape(2 * sub_pulses, SAMPLES // gate_count)
-    if depth_count != 1:
+    send = functools.partial(range_compress, raw_echo, delays, depth_count, sub_pulses)
+    if (sub_count, gate_count) != (2, 16):
+        (compressed,) = send([range(gate_count)])
+        me = lax.axis_index("gate")
+        ordered = compressed[me ^ jnp.arange(gate_count)]
+        received = lax.all_to_all(ordered, "gate", split_axis=0, concat_axis=0, tiled=True)
+        received = received.reshape(2 * sub_pulses, SAMPLES // gate_count)
         return merge_levels(received, pulse_count, sub_pulses, depth_count)
-    other = partner(received, "sub", 0)
+    arrays, places = corner_turn(send)
     tables = jnp.asarray(image_tables(sub_pulses, pulse_count))
     table = lax.dynamic_index_in_dim(tables, lax.axis_index("sub"), 0, keepdims=False)
-    return form_image(table, received, other)
+    return form_image(table, arrays, places)
 
 
 def solution(mesh):

time: 43.7 us -> 33.9 us (0.78)
  blocking collectives: 21.6 us -> 0 us
  starting transfers between devices: 1.5 us -> 13.4 us
  local copies, waits for them, and re-layouts: 4.47 us -> 0.1 us
  waiting for transfers between devices: 12.3 us -> 15 us
  Pallas kernels: 3.55 us -> 4.94 us
    all_to_all x1 -> x0, blocking collectives: 21.6 us -> none  [per_device(): lax.all_to_all(compressed, 'gate', split_axis=0, concat_axis=0, tiled=True)]
    ppermute x1 -> x10, starting transfers between devices: 1.5 us -> 13.4 us  [the longest x6 9.52 us: swap(): return lax.ppermute(array, 'gate', [(i, i ^ apart) for i in range(count)])]
    unnamed x12 -> x2, local copies, waits for them, and re-layouts: 4.43 us -> 0.01 us
    ppermute x1 -> x10, waiting for transfers between devices: 12.3 us -> 15 us  [the longest x6 13.3 us: swap(): return lax.ppermute(array, 'gate', [(i, i ^ apart) for i in range(count)])]
    pallas_call x2, Pallas kernels: 3.55 us -> 4.94 us  [the longest x1 3.18 us: range_compress(): pl.pallas_call(functools.partial(compress_kernel, plan), out_shape=[pltpu...]
  transfers between devices with their start and end apart: 1 -> 10, of which waited for: 1 -> 6; matrix products, arithmetic and copies ran while one was open for 0% -> 0% of each run, Pallas kernels for 0% -> 0%
where the time goes in v2:
time: 33.9 us; the launch traced here: 33.7 us
  waiting for transfers between devices  15 us (44%)
  starting transfers between devices  13.4 us (40%)
  Pallas kernels  4.94 us (15%)
    ppermute x6, waiting for transfers between devices, swap(): return lax.ppermute(array, 'gate', [(i, i ^ apart) for i in range(count)])  13.3 us
    ppermute x6, starting transfers between devices, swap(): return lax.ppermute(array, 'gate', [(i, i ^ apart) for i in range(count)])  9.52 us
    ppermute x4, starting transfers between devices, swap(): return lax.ppermute(array, ('sub', 'gate'), pairs)  3.9 us
    pallas_call x1, Pallas kernels, range_compress(): pl.pallas_call(functools.partial(compress_kernel, plan), out_shape=[pltpu...  3.18 us
    pallas_call x1, Pallas kernels, form_image(): pl.pallas_call(functools.partial(image_kernel, plan), out_shape=jax.Shape...  1.76 us
    ppermute x4, waiting for transfers between devices, swap(): return lax.ppermute(array, ('sub', 'gate'), pairs)  1.76 us
  transfers between devices with their start and end apart: 10, of which 6 were waited for; matrix products, arithmetic and copies ran while one was open for 0% of the time, Pallas kernels for 0%

profile of v2, /device:TPU:0, one launch (start us, length us, event | category | flops | bytes accessed | tf_op | source)
XLA Modules:
  0.0 33.7 jit_solution(15112004017786101638)
XLA Ops:
  0.0 3.2 %compress.1 = (bf16[2,16,1024]{2,1,0:T(8,128)(2,1)S(1)}, bf16[2,16,1024]{2,1,0:T(8,128)(2,1)S(1)}, bf16[2,16,1024]{2,1,0:T(8,128)(2,1)S(1)}, bf16[2,16,1024]{2,1,0:T(8,128)(2,1)S(1)}, bf16[8,16,1024]{2,1,0:T(8,128)(2,1)S(1)}) custom-call(s32[8]{0:T(128)} %delays.1, bf16[2,8,16384]{2,1,0:T(8,128)(2,1)} %raw_far.1, bf16[256,256]{1,0:T(8,128)(2,1)} %constant.20.clone.dft_far, ...), custom_call_target="tpu_custom_call" | custom-call | tf_op jit(solution)/shard_map/compress/pallas_call | solution.py:192
  3.2 0.5 %collective-permute-start = (bf16[8,16,1024]{2,1,0:T(8,128)(2,1)S(1)}, bf16[8,16,1024]{2,1,0:T(8,128)(2,1)S(1)}, u32[]{:S(2)}, u32[]{:S(2)}) collective-permute-start(bf16[8,16,1024]{2,1,0:T(8,128)(2,1)S(1)} %get-tuple-element.11), channel_id=1, source_target_pairs={{0,1},{1,0},{2,3},{3,2},{4,5},{5,4},{6,7},{7,6},{8,9},{9,8},{10,11... | collective-permute-start | bytes 786440 | tf_op jit(solution)/shard_map/ppermute | solution.py:287
  3.7 1.2 %collective-permute-done = bf16[8,16,1024]{2,1,0:T(8,128)(2,1)S(1)} collective-permute-done((bf16[8,16,1024]{2,1,0:T(8,128)(2,1)S(1)}, bf16[8,16,1024]{2,1,0:T(8,128)(2,1)S(1)}, u32[]{:S(2)}, u32[]{:S(2)}) %collective-permute-start) | collective-permute-done | bytes 262176 | tf_op jit(solution)/shard_map/ppermute | solution.py:287
  5.0 3.0 %collective-permute-start.1 = (bf16[2,2,16,1024]{3,2,0,1:T(8,128)(2,1)S(1)}, bf16[2,2,16,1024]{3,2,0,1:T(8,128)(2,1)S(1)}, u32[]{:S(2)}, u32[]{:S(2)}) collective-permute-start(bf16[2,2,16,1024]{3,2,0,1:T(8,128)(2,1)S(1)} %pad_maximum_fusion), channel_id=1, source_target_pairs={{0,4},{1,5},{2,6},{3,7},{4,0},{5,1},{6,2},{7,3},{8,12},{9,13},{10,... | collective-permute-start | bytes 393224 | tf_op jit(solution)/shard_map/ppermute | solution.py:287
  8.0 2.5 %collective-permute-start.6 = (bf16[2,2,16,1024]{3,2,1,0:T(8,128)(2,1)S(1)}, bf16[2,2,16,1024]{3,2,1,0:T(8,128)(2,1)S(1)}, u32[]{:S(2)}, u32[]{:S(2)}) collective-permute-start(bf16[2,2,16,1024]{3,2,1,0:T(8,128)(2,1)S(1)} %copy.8), channel_id=1, source_target_pairs={{0,12},{1,13},{2,14},{3,15},{4,8},{5,9},{6,10},{7,11},{8,4},{9,5},... | collective-permute-start | bytes 393224 | tf_op jit(solution)/shard_map/ppermute | solution.py:287
  10.5 0.2 collective-permute-start.5
  10.6 0.0 copy-start
  10.7 1.1 %collective-permute-done.1 = bf16[2,2,16,1024]{3,2,0,1:T(8,128)(2,1)S(1)} collective-permute-done((bf16[2,2,16,1024]{3,2,0,1:T(8,128)(2,1)S(1)}, bf16[2,2,16,1024]{3,2,0,1:T(8,128)(2,1)S(1)}, u32[]{:S(2)}, u32[]{:S(2)}) %collective-permute-start.1) | collective-permute-done | bytes 131104 | tf_op jit(solution)/shard_map/ppermute | solution.py:287
  11.8 1.8 %collective-permute-start.4 = (bf16[4,16,1024]{2,1,0:T(8,128)(2,1)S(1)}, bf16[4,16,1024]{2,1,0:T(8,128)(2,1)S(1)}, u32[]{:S(2)}, u32[]{:S(2)}) collective-permute-start(bf16[4,16,1024]{2,1,0:T(8,128)(2,1)S(1)} %pad_maximum_fusion.2), channel_id=1, source_target_pairs={{0,2},{1,3},{2,0},{3,1},{4,6},{5,7},{6,4},{7,5},{8,10},{9,11},{10,... | collective-permute-start | bytes 393224 | tf_op jit(solution)/shard_map/ppermute | solution.py:287
  13.6 1.4 %collective-permute-start.2 = (bf16[4,16,1024]{2,1,0:T(8,128)(2,1)S(1)}, bf16[4,16,1024]{2,1,0:T(8,128)(2,1)S(1)}, u32[]{:S(2)}, u32[]{:S(2)}) collective-permute-start(bf16[4,16,1024]{2,1,0:T(8,128)(2,1)S(1)} %pad_maximum_fusion.2), channel_id=1, source_target_pairs={{0,18},{1,19},{2,16},{3,17},{4,22},{5,23},{6,20},{7,21},{8,26},{9,... | collective-permute-start | bytes 393224 | tf_op jit(solution)/shard_map/ppermute | solution.py:289
  15.0 0.4 %collective-permute-start.3 = (bf16[4,16,1024]{2,1,0:T(8,128)(2,1)S(1)}, bf16[4,16,1024]{2,1,0:T(8,128)(2,1)S(1)}, u32[]{:S(2)}, u32[]{:S(2)}) collective-permute-start(bf16[4,16,1024]{2,1,0:T(8,128)(2,1)S(1)} %pad_maximum_fusion.1.refs_0_), channel_id=1, source_target_pairs={{0,16},{1,17},{2,18},{3,19},{4,20},{5,21},{6,22},{7,23},{8,24},{9,... | collective-permute-start | bytes 393224 | tf_op jit(solution)/shard_map/ppermute | solution.py:289
  15.4 2.2 %collective-permute-done.6 = bf16[2,2,16,1024]{3,2,1,0:T(8,128)(2,1)S(1)} collective-permute-done((bf16[2,2,16,1024]{3,2,1,0:T(8,128)(2,1)S(1)}, bf16[2,2,16,1024]{3,2,1,0:T(8,128)(2,1)S(1)}, u32[]{:S(2)}, u32[]{:S(2)}) %collective-permute-start.6) | collective-permute-done | bytes 131104 | tf_op jit(solution)/shard_map/ppermute | solution.py:287
  17.7 4.8 %collective-permute-done.5 = bf16[2,2,16,1024]{3,2,1,0:T(8,128)(2,1)S(1)} collective-permute-done((bf16[2,2,16,1024]{3,2,1,0:T(8,128)(2,1)S(1)}, bf16[2,2,16,1024]{3,2,1,0:T(8,128)(2,1)S(1)}, u32[]{:S(2)}, u32[]{:S(2)}) %collective-permute-start.5) | collective-permute-done | bytes 131104 | tf_op jit(solution)/shard_map/ppermute | solution.py:287
  22.5 1.6 %collective-permute-start.8 = (bf16[4,16,1024]{2,1,0:T(8,128)(2,1)S(1)}, bf16[4,16,1024]{2,1,0:T(8,128)(2,1)S(1)}, u32[]{:S(2)}, u32[]{:S(2)}) collective-permute-start(bf16[4,16,1024]{2,1,0:T(8,128)(2,1)S(1)} %pad_maximum_fusion.5.refs_4_), channel_id=1, source_target_pairs={{0,16},{1,17},{2,18},{3,19},{4,20},{5,21},{6,22},{7,23},{8,24},{9,... | collective-permute-start | bytes 393224 | tf_op jit(solution)/shard_map/ppermute | solution.py:289
  24.1 1.6 %collective-permute-start.9 = (bf16[4,16,1024]{2,1,0:T(8,128)(2,1)S(1)}, bf16[4,16,1024]{2,1,0:T(8,128)(2,1)S(1)}, u32[]{:S(2)}, u32[]{:S(2)}) collective-permute-start(bf16[4,16,1024]{2,1,0:T(8,128)(2,1)S(1)} %pad_maximum_fusion.6), channel_id=1, source_target_pairs={{0,2},{1,3},{2,0},{3,1},{4,6},{5,7},{6,4},{7,5},{8,10},{9,11},{10,... | collective-permute-start | bytes 393224 | tf_op jit(solution)/shard_map/ppermute | solution.py:287
  25.7 0.0 collective-permute-done.3.refs_2_
  25.7 0.5 %collective-permute-start.7 = (bf16[4,16,1024]{2,1,0:T(8,128)(2,1)S(1)}, bf16[4,16,1024]{2,1,0:T(8,128)(2,1)S(1)}, u32[]{:S(2)}, u32[]{:S(2)}) collective-permute-start(bf16[4,16,1024]{2,1,0:T(8,128)(2,1)S(1)} %pad_maximum_fusion.6), channel_id=1, source_target_pairs={{0,18},{1,19},{2,16},{3,17},{4,22},{5,23},{6,20},{7,21},{8,26},{9,... | collective-permute-start | bytes 393224 | tf_op jit(solution)/shard_map/ppermute | solution.py:289
  26.2 0.0 copy-done
  26.2 0.0 collective-permute-done.4.refs_3_
  26.2 0.0 collective-permute-done.2.refs_1_
  26.2 1.8 %collective-permute-done.8.refs_6_ = bf16[4,16,1024]{2,1,0:T(8,128)(2,1)S(1)} collective-permute-done((bf16[4,16,1024]{2,1,0:T(8,128)(2,1)S(1)}, bf16[4,16,1024]{2,1,0:T(8,128)(2,1)S(1)}, u32[]{:S(2)}, u32[]{:S(2)}) %collective-permute-start.8) | collective-permute-done | bytes 131104 | tf_op jit(solution)/shard_map/ppermute | solution.py:289
  28.0 4.0 %collective-permute-done.9.refs_7_ = bf16[4,16,1024]{2,1,0:T(8,128)(2,1)S(1)} collective-permute-done((bf16[4,16,1024]{2,1,0:T(8,128)(2,1)S(1)}, bf16[4,16,1024]{2,1,0:T(8,128)(2,1)S(1)}, u32[]{:S(2)}, u32[]{:S(2)}) %collective-permute-start.9) | collective-permute-done | bytes 131104 | tf_op jit(solution)/shard_map/ppermute | solution.py:287
  32.0 0.0 collective-permute-done.7.refs_5_
  32.0 1.8 %image.1 = bf16[512,1024]{1,0:T(8,128)(2,1)} custom-call(bf16[512,512]{1,0:T(8,128)(2,1)S(1)} %dynamic-slice_bitcast_fusion.table, bf16[4,16,1024]{2,1,0:T(8,128)(2,1)S(1)} %pad_maximum_fusion.1.refs_0_, bf16[4,16,1024]{2,1,0:T(8,128)(2,1)S(1)} %collective-permute-done.2.refs_1_, bf16[4,16,1024]{2,1,0:T(8,128)(2,1)S(1)} %collective-permute-done.3.refs_2_, ...), custom_call_target="tpu_custom_call" | custom-call | tf_op jit(solution)/shard_map/image/pallas_call | solution.py:238
  (14 shorter events, 0.2 us)
Async XLA Ops:
  3.2 1.7 %collective-permute-start = (bf16[8,16,1024]{2,1,0:T(8,128)(2,1)S(1)}, bf16[8,16,1024]{2,1,0:T(8,128)(2,1)S(1)}, u32[]{:S(2)}, u32[]{:S(2)}) collective-permute-start(bf16[8,16,1024]{2,1,0:T(8,128)(2,1)S(1)} %get-tuple-element.11), channel_id=1, source_target_pairs={{0,1},{1,0},{2,3},{3,2},{4,5},{5,4},{6,7},{7,6},{8,9},{9,8},{10,11... | collective-permute-start | bytes 786440 | tf_op jit(solution)/shard_map/ppermute | solution.py:287
  5.0 6.8 %collective-permute-start.1 = (bf16[2,2,16,1024]{3,2,0,1:T(8,128)(2,1)S(1)}, bf16[2,2,16,1024]{3,2,0,1:T(8,128)(2,1)S(1)}, u32[]{:S(2)}, u32[]{:S(2)}) collective-permute-start(bf16[2,2,16,1024]{3,2,0,1:T(8,128)(2,1)S(1)} %pad_maximum_fusion), channel_id=1, source_target_pairs={{0,4},{1,5},{2,6},{3,7},{4,0},{5,1},{6,2},{7,3},{8,12},{9,13},{10,... | collective-permute-start | bytes 393224 | tf_op jit(solution)/shard_map/ppermute | solution.py:287
  8.0 9.7 %collective-permute-start.6 = (bf16[2,2,16,1024]{3,2,1,0:T(8,128)(2,1)S(1)}, bf16[2,2,16,1024]{3,2,1,0:T(8,128)(2,1)S(1)}, u32[]{:S(2)}, u32[]{:S(2)}) collective-permute-start(bf16[2,2,16,1024]{3,2,1,0:T(8,128)(2,1)S(1)} %copy.8), channel_id=1, source_target_pairs={{0,12},{1,13},{2,14},{3,15},{4,8},{5,9},{6,10},{7,11},{8,4},{9,5},... | collective-permute-start | bytes 393224 | tf_op jit(solution)/shard_map/ppermute | solution.py:287
  10.5 12.0 %collective-permute-start.5 = (bf16[2,2,16,1024]{3,2,1,0:T(8,128)(2,1)S(1)}, bf16[2,2,16,1024]{3,2,1,0:T(8,128)(2,1)S(1)}, u32[]{:S(2)}, u32[]{:S(2)}) collective-permute-start(bf16[2,2,16,1024]{3,2,1,0:T(8,128)(2,1)S(1)} %pad_maximum_fusion.3), channel_id=1, source_target_pairs={{0,8},{1,9},{2,10},{3,11},{4,12},{5,13},{6,14},{7,15},{8,0},{9,1},... | collective-permute-start | bytes 393224 | tf_op jit(solution)/shard_map/ppermute | solution.py:287
  10.6 15.5 %copy-start = (bf16[2,512,512]{2,1,0:T(8,128)(2,1)S(1)}, bf16[2,512,512]{2,1,0:T(8,128)(2,1)}, u32[]{:S(2)}) copy-start(bf16[2,512,512]{2,1,0:T(8,128)(2,1)} %constant.23.clone) | copy-start | bytes 3145732
  11.8 14.4 %collective-permute-start.4 = (bf16[4,16,1024]{2,1,0:T(8,128)(2,1)S(1)}, bf16[4,16,1024]{2,1,0:T(8,128)(2,1)S(1)}, u32[]{:S(2)}, u32[]{:S(2)}) collective-permute-start(bf16[4,16,1024]{2,1,0:T(8,128)(2,1)S(1)} %pad_maximum_fusion.2), channel_id=1, source_target_pairs={{0,2},{1,3},{2,0},{3,1},{4,6},{5,7},{6,4},{7,5},{8,10},{9,11},{10,... | collective-permute-start | bytes 393224 | tf_op jit(solution)/shard_map/ppermute | solution.py:287
  13.6 12.7 %collective-permute-start.2 = (bf16[4,16,1024]{2,1,0:T(8,128)(2,1)S(1)}, bf16[4,16,1024]{2,1,0:T(8,128)(2,1)S(1)}, u32[]{:S(2)}, u32[]{:S(2)}) collective-permute-start(bf16[4,16,1024]{2,1,0:T(8,128)(2,1)S(1)} %pad_maximum_fusion.2), channel_id=1, source_target_pairs={{0,18},{1,19},{2,16},{3,17},{4,22},{5,23},{6,20},{7,21},{8,26},{9,... | collective-permute-start | bytes 393224 | tf_op jit(solution)/shard_map/ppermute | solution.py:289
  15.0 10.7 %collective-permute-start.3 = (bf16[4,16,1024]{2,1,0:T(8,128)(2,1)S(1)}, bf16[4,16,1024]{2,1,0:T(8,128)(2,1)S(1)}, u32[]{:S(2)}, u32[]{:S(2)}) collective-permute-start(bf16[4,16,1024]{2,1,0:T(8,128)(2,1)S(1)} %pad_maximum_fusion.1.refs_0_), channel_id=1, source_target_pairs={{0,16},{1,17},{2,18},{3,19},{4,20},{5,21},{6,22},{7,23},{8,24},{9,... | collective-permute-start | bytes 393224 | tf_op jit(solution)/shard_map/ppermute | solution.py:289
  22.5 5.5 %collective-permute-start.8 = (bf16[4,16,1024]{2,1,0:T(8,128)(2,1)S(1)}, bf16[4,16,1024]{2,1,0:T(8,128)(2,1)S(1)}, u32[]{:S(2)}, u32[]{:S(2)}) collective-permute-start(bf16[4,16,1024]{2,1,0:T(8,128)(2,1)S(1)} %pad_maximum_fusion.5.refs_4_), channel_id=1, source_target_pairs={{0,16},{1,17},{2,18},{3,19},{4,20},{5,21},{6,22},{7,23},{8,24},{9,... | collective-permute-start | bytes 393224 | tf_op jit(solution)/shard_map/ppermute | solution.py:289
  24.1 7.8 %collective-permute-start.9 = (bf16[4,16,1024]{2,1,0:T(8,128)(2,1)S(1)}, bf16[4,16,1024]{2,1,0:T(8,128)(2,1)S(1)}, u32[]{:S(2)}, u32[]{:S(2)}) collective-permute-start(bf16[4,16,1024]{2,1,0:T(8,128)(2,1)S(1)} %pad_maximum_fusion.6), channel_id=1, source_target_pairs={{0,2},{1,3},{2,0},{3,1},{4,6},{5,7},{6,4},{7,5},{8,10},{9,11},{10,... | collective-permute-start | bytes 393224 | tf_op jit(solution)/shard_map/ppermute | solution.py:287
  25.7 6.3 %collective-permute-start.7 = (bf16[4,16,1024]{2,1,0:T(8,128)(2,1)S(1)}, bf16[4,16,1024]{2,1,0:T(8,128)(2,1)S(1)}, u32[]{:S(2)}, u32[]{:S(2)}) collective-permute-start(bf16[4,16,1024]{2,1,0:T(8,128)(2,1)S(1)} %pad_maximum_fusion.6), channel_id=1, source_target_pairs={{0,18},{1,19},{2,16},{3,17},{4,22},{5,23},{6,20},{7,21},{8,26},{9,... | collective-permute-start | bytes 393224 | tf_op jit(solution)/shard_map/ppermute | solution.py:289

commit v3 on v2

--- a/solution.py
+++ b/solution.py
@@ -213,38 +213,52 @@
     )(delays, raw_echo, dft, twiddle, near)
 
 
-def image_kernel(plan, table, *refs):
-    arrays, (out, data) = refs[: len(plan)], refs[len(plan) :]
-    rows, columns = out.shape
-    depth = data.shape[0]
+def image_kernel(plan, far, has_total, table, *refs):
+    arrays, refs = refs[: len(plan)], refs[len(plan) :]
+    total, (out, data, columns) = (refs[0], refs[1:]) if has_total else (None, refs)
+    half = data.shape[0] // 2
     block = arrays[0].shape[1]
     me = lax.axis_index("gate")
+    lower = (me ^ far) // FAR * half
     for array, (side, places) in zip(arrays, plan, strict=True):
         for index, apart in enumerate(places):
-            start = pl.multiple_of(side * (depth // 2) + (me ^ apart) * block, block)
-            data[pl.ds(start, block), :] = array[index]
-    tile_rows, tile_columns = min(rows, 256), min(columns, 256)
-    for row in range(0, rows, tile_rows):
-        for column in range(0, columns, tile_columns):
-            place = pl.ds(row, tile_rows), pl.ds(column, tile_columns)
-            out[place] = jnp.dot(
-                table[place[0], :], data[:, place[1]], preferred_element_type=jnp.float32
-            ).astype(jnp.bfloat16)
+            if apart // FAR * FAR == far:
+                start = side * half + (me ^ apart) * block - lower
+                data[pl.ds(pl.multiple_of(start, block), block), :] = array[index]
+    for side in range(2):
+        source = pl.multiple_of(side * 2 * half + lower, half)
+        columns[:, pl.ds(side * half, half)] = table[:, pl.ds(source, half)]
+    tile = 256
+    for row in range(0, out.shape[0], tile):
+        for column in range(0, out.shape[1], tile):
+            place = pl.ds(row, tile), pl.ds(column, tile)
+            sums = jnp.dot(columns[place[0], :], data[:, place[1]], preferred_element_type=jnp.float32)
+            if has_total:
+                sums = sums + total[place]
+            out[place] = sums.astype(out.dtype)
 
 
 def form_image(table, arrays, plan):
+    rows, depth = table.shape[0], table.shape[1] // 2
+    shape = rows, arrays[0].shape[-1]
     vmem = pl.BlockSpec(memory_space=pltpu.VMEM)
-    width = arrays[0].shape[-1]
-    image = pl.pallas_call(
-        functools.partial(image_kernel, plan),
-        out_shape=jax.ShapeDtypeStruct((2 * ANGLES, width), jnp.bfloat16),
-        in_specs=[vmem] * (1 + len(arrays)),
-        out_specs=vmem,
-        scratch_shapes=[pltpu.VMEM((table.shape[1], width), jnp.bfloat16)],
-        compiler_params=pltpu.CompilerParams(vmem_limit_bytes=32 * 2**20),
-        name="image",
-    )(table, *arrays)
-    return image.reshape(2, ANGLES, width)
+    total = []
+    for far in (0, FAR):
+        used = [i for i, (_, places) in enumerate(plan) if any(apart // FAR * FAR == far for apart in places)]
+        image = pl.pallas_call(
+            functools.partial(image_kernel, [plan[i] for i in used], far, bool(total)),
+            out_shape=jax.ShapeDtypeStruct(shape, jnp.bfloat16) if far else pltpu.VMEM(shape, jnp.float32),
+            in_specs=[vmem] * (1 + len(used) + len(total)),
+            out_specs=vmem,
+            scratch_shapes=[pltpu.VMEM((depth, shape[1]), jnp.bfloat16), pltpu.VMEM((rows, depth), jnp.bfloat16)],
+            cost_estimate=pl.CostEstimate(
+                flops=2 * depth * math.prod(shape), bytes_accessed=4 * math.prod(shape), transcendentals=0
+            ),
+            compiler_params=pltpu.CompilerParams(vmem_limit_bytes=32 * 2**20),
+            name="image",
+        )(table, *[arrays[i] for i in used], *total)
+        total = [image]
+    return image.reshape(2, ANGLES, shape[1])
 
 
 def partner(array, axis, apart):
@@ -289,23 +303,37 @@
     return lax.ppermute(array, ("sub", "gate"), pairs)
 
 
-CORE, Y, Z = 1, 2, 4
+CORE, Y, Z, FAR = 1, 2, 4, 8
+
+
+def after(array, other):
+    return lax.optimization_barrier((array, other))[0]
 
 
 def corner_turn(send):
-    near, far = [0, Y], [CORE, CORE | Y]
-    plan = [near, [Z + i for i in near], [2 * Z + i for i in near], [3 * Z + i for i in near]]
-    plan.append([k * Z + i for k in range(4) for i in far])
-    own = send(plan)
-    mate = swap(own[4], CORE).reshape((4,) + own[0].shape)
-    both = [jnp.stack(pair, axis=1) for pair in zip(own[:4], mate, strict=True)]
-    moved = both[:1] + [swap(both[k], k * Z) for k in range(1, 4)]
-    groups = [moved[:2], moved[2:]]
+    plan = [[place * Z, place * Z + Y] for place in range(4)]
+    plan.append([place * Z + CORE + y for place in (0, 1, 3) for y in (0, Y)])
+    plan.append([2 * Z + CORE, 2 * Z + CORE + Y])
+    here, one, two, three, mates, mates_two = send(plan)
+    width = here.shape[-1]
+    mates = swap(mates, CORE)
+    mates_two = swap(after(mates_two, mates), CORE)
+    mates = mates.reshape(3, 2, -1, width)
+    two = swap(two, 2 * Z)
+    one = swap(jnp.stack([one, mates[1]], axis=1), Z)
+    three = swap(jnp.stack([three, mates[2]], axis=1), 3 * Z)
+    mates_two = swap(mates_two, 2 * Z)
+    two = after(two, one)
+    here = jnp.stack([here, mates[0]], axis=1)
+    two = jnp.stack([two, mates_two], axis=1)
+    near = [0, CORE, Z, Z + CORE]
+    groups = [
+        ([here[0], one[0]], [here[1], one[1]], near),
+        ([two[0], three[0]], [two[1], three[1]], [FAR + i for i in near]),
+    ]
     arrays, places = [], []
-    for index, pair in enumerate(groups):
-        home = jnp.concatenate([half[0] for half in pair])
-        away = jnp.concatenate([half[1] for half in pair])
-        apart = [k * Z + core for k in (2 * index, 2 * index + 1) for core in (0, CORE)]
+    for home, away, apart in groups:
+        home, away = jnp.concatenate(home), jnp.concatenate(away)
         apart_y = [i + Y for i in apart]
         arrays += [home, swap(away, Y, True), swap(home, 0, True), swap(away, Y)]
         places += [(0, apart), (1, apart_y), (1, apart), (0, apart_y)]

time: 33.9 us -> 30.8 us (0.909)
  waiting for transfers between devices: 15 us -> 9.55 us
  starting transfers between devices: 13.4 us -> 15.5 us
  Pallas kernels: 4.94 us -> 5.28 us
    ppermute x6 -> x8, waiting for transfers between devices: 13.3 us -> 5.3 us  [swap(): return lax.ppermute(array, 'gate', [(i, i ^ apart) for i in range(count)])]
    ppermute x4, waiting for transfers between devices: 1.76 us -> 4.25 us  [swap(): return lax.ppermute(array, ('sub', 'gate'), pairs)]
    ppermute x6 -> x8, starting transfers between devices: 9.52 us -> 11.3 us  [swap(): return lax.ppermute(array, 'gate', [(i, i ^ apart) for i in range(count)])]
    ppermute x4, starting transfers between devices: 3.9 us -> 4.27 us  [swap(): return lax.ppermute(array, ('sub', 'gate'), pairs)]
    pallas_call x1 -> x2, Pallas kernels: 1.76 us -> 1.96 us  [form_image(): pl.pallas_call(functools.partial(image_kernel, [plan[i] for i in used], f...]
  transfers between devices with their start and end apart: 10 -> 12, of which waited for: 6 -> 3; matrix products, arithmetic and copies ran while one was open for 0% -> 1% of each run, Pallas kernels for 0% -> 2%
where the time goes in v3:
time: 30.8 us; the launch traced here: 30.7 us
  starting transfers between devices  15.5 us (50%)
  waiting for transfers between devices  9.55 us (31%)
  Pallas kernels  5.28 us (17%)
    ppermute x8, starting transfers between devices, swap(): return lax.ppermute(array, 'gate', [(i, i ^ apart) for i in range(count)])  11.3 us
    ppermute x8, waiting for transfers between devices, swap(): return lax.ppermute(array, 'gate', [(i, i ^ apart) for i in range(count)])  5.3 us
    ppermute x4, starting transfers between devices, swap(): return lax.ppermute(array, ('sub', 'gate'), pairs)  4.27 us
    ppermute x4, waiting for transfers between devices, swap(): return lax.ppermute(array, ('sub', 'gate'), pairs)  4.25 us
    pallas_call x1, Pallas kernels, range_compress(): pl.pallas_call(functools.partial(compress_kernel, plan), out_shape=[pltpu...  3.32 us
    pallas_call x2, Pallas kernels, form_image(): pl.pallas_call(functools.partial(image_kernel, [plan[i] for i in used], f...  1.96 us
  transfers between devices with their start and end apart: 12, of which 3 were waited for; matrix products, arithmetic and copies ran while one was open for 1% of the time, Pallas kernels for 2%

profile of v3, /device:TPU:0, one launch (start us, length us, event | category | flops | bytes accessed | tf_op | source)
XLA Modules:
  0.0 30.7 jit_solution(15468245667492317788)
XLA Ops:
  0.0 0.0 copy-start
  0.0 3.3 %compress.1 = (bf16[2,16,1024]{2,1,0:T(8,128)(2,1)S(1)}, bf16[2,16,1024]{2,1,0:T(8,128)(2,1)S(1)}, bf16[2,16,1024]{2,1,0:T(8,128)(2,1)S(1)}, bf16[2,16,1024]{2,1...) custom-call(s32[8]{0:T(128)} %delays.1, bf16[2,8,16384]{2,1,0:T(8,128)(2,1)} %raw_far.1, ...), custom_call_target="tpu_custom_call" | custom-call | tf_op jit(solution)/shard_map/compress/pallas_call | solution.py:192
  3.3 0.5 %collective-permute-start.1 = (bf16[6,16,1024]{2,1,0:T(8,128)(2,1)S(1)}, bf16[6,16,1024]{2,1,0:T(8,128)(2,1)S(1)}, u32[]{:S(2)}, u32[]{:S(2)}) collective-permute-start(bf16[6,16,1024]{2,1,0:T(8,128)(2,1)S(1)} %get-tuple-element.15), channel_id=1, source_target_pairs={{0,1},{1,0},{2,3},{3,2},{4,5},{5,4},{6,7},{7,6},{8,9},{9,8},{10,11... | collective-permute-start | bytes 589832 | tf_op jit(solution)/shard_map/ppermute | solution.py:301
  3.9 3.7 %collective-permute-start = (bf16[2,16,1024]{2,1,0:T(8,128)(2,1)S(1)}, bf16[2,16,1024]{2,1,0:T(8,128)(2,1)S(1)}, u32[]{:S(2)}, u32[]{:S(2)}) collective-permute-start(bf16[2,16,1024]{2,1,0:T(8,128)(2,1)S(1)} %get-tuple-element.13), channel_id=1, source_target_pairs={{0,8},{1,9},{2,10},{3,11},{4,12},{5,13},{6,14},{7,15},{8,0},{9,1},... | collective-permute-start | bytes 196616 | tf_op jit(solution)/shard_map/ppermute | solution.py:301
  7.5 0.0 collective-permute-done.1
  7.5 0.2 collective-permute-start.3
  7.7 1.6 %collective-permute-start.2 = (bf16[2,2,16,1024]{3,2,1,0:T(8,128)(2,1)S(1)}, bf16[2,2,16,1024]{3,2,1,0:T(8,128)(2,1)S(1)}, u32[]{:S(2)}, u32[]{:S(2)}) collective-permute-start(bf16[2,2,16,1024]{3,2,1,0:T(8,128)(2,1)S(1)} %pad_maximum_fusion), channel_id=1, source_target_pairs={{0,4},{1,5},{2,6},{3,7},{4,0},{5,1},{6,2},{7,3},{8,12},{9,13},{10,... | collective-permute-start | bytes 393224 | tf_op jit(solution)/shard_map/ppermute | solution.py:301
  9.4 1.3 %collective-permute-start.5 = (bf16[2,2,16,1024]{3,2,1,0:T(8,128)(2,1)S(1)}, bf16[2,2,16,1024]{3,2,1,0:T(8,128)(2,1)S(1)}, u32[]{:S(2)}, u32[]{:S(2)}) collective-permute-start(bf16[2,2,16,1024]{3,2,1,0:T(8,128)(2,1)S(1)} %pad_maximum_fusion.1), channel_id=1, source_target_pairs={{0,12},{1,13},{2,14},{3,15},{4,8},{5,9},{6,10},{7,11},{8,4},{9,5},... | collective-permute-start | bytes 393224 | tf_op jit(solution)/shard_map/ppermute | solution.py:301
  10.7 0.0 collective-permute-done.3
  10.7 0.7 %collective-permute-start.4 = (bf16[2,16,1024]{2,1,0:T(8,128)(2,1)S(1)}, bf16[2,16,1024]{2,1,0:T(8,128)(2,1)S(1)}, u32[]{:S(2)}, u32[]{:S(2)}) collective-permute-start(bf16[2,16,1024]{2,1,0:T(8,128)(2,1)S(1)} %collective-permute-done.3), channel_id=1, source_target_pairs={{0,8},{1,9},{2,10},{3,11},{4,12},{5,13},{6,14},{7,15},{8,0},{9,1},... | collective-permute-start | bytes 196616 | tf_op jit(solution)/shard_map/ppermute | solution.py:301
  11.4 2.3 %collective-permute-done.2 = bf16[2,2,16,1024]{3,2,1,0:T(8,128)(2,1)S(1)} collective-permute-done((bf16[2,2,16,1024]{3,2,1,0:T(8,128)(2,1)S(1)}, bf16[2,2,16,1024]{3,2,1,0:T(8,128)(2,1)S(1)}, u32[]{:S(2)}, u32[]{:S(2)}) %collective-permute-start.2) | collective-permute-done | bytes 131104 | tf_op jit(solution)/shard_map/ppermute | solution.py:301
  13.8 1.6 %collective-permute-start.11 = (bf16[4,16,1024]{2,1,0:T(8,128)(2,1)S(1)}, bf16[4,16,1024]{2,1,0:T(8,128)(2,1)S(1)}, u32[]{:S(2)}, u32[]{:S(2)}) collective-permute-start(bf16[4,16,1024]{2,1,0:T(8,128)(2,1)S(1)} %pad_maximum_fusion.5), channel_id=1, source_target_pairs={{0,2},{1,3},{2,0},{3,1},{4,6},{5,7},{6,4},{7,5},{8,10},{9,11},{10,... | collective-permute-start | bytes 393224 | tf_op jit(solution)/shard_map/ppermute | solution.py:301
  15.4 1.4 %collective-permute-start.9 = (bf16[4,16,1024]{2,1,0:T(8,128)(2,1)S(1)}, bf16[4,16,1024]{2,1,0:T(8,128)(2,1)S(1)}, u32[]{:S(2)}, u32[]{:S(2)}) collective-permute-start(bf16[4,16,1024]{2,1,0:T(8,128)(2,1)S(1)} %pad_maximum_fusion.5), channel_id=1, source_target_pairs={{0,18},{1,19},{2,16},{3,17},{4,22},{5,23},{6,20},{7,21},{8,26},{9,... | collective-permute-start | bytes 393224 | tf_op jit(solution)/shard_map/ppermute | solution.py:303
  16.9 0.0 collective-permute-done
  16.9 0.5 %collective-permute-start.10 = (bf16[4,16,1024]{2,1,0:T(8,128)(2,1)S(1)}, bf16[4,16,1024]{2,1,0:T(8,128)(2,1)S(1)}, u32[]{:S(2)}, u32[]{:S(2)}) collective-permute-start(bf16[4,16,1024]{2,1,0:T(8,128)(2,1)S(1)} %pad_maximum_fusion.4.refs_0_), channel_id=1, source_target_pairs={{0,16},{1,17},{2,18},{3,19},{4,20},{5,21},{6,22},{7,23},{8,24},{9,... | collective-permute-start | bytes 393224 | tf_op jit(solution)/shard_map/ppermute | solution.py:303
  17.4 3.0 %collective-permute-done.4 = bf16[2,16,1024]{2,1,0:T(8,128)(2,1)S(1)} collective-permute-done((bf16[2,16,1024]{2,1,0:T(8,128)(2,1)S(1)}, bf16[2,16,1024]{2,1,0:T(8,128)(2,1)S(1)}, u32[]{:S(2)}, u32[]{:S(2)}) %collective-permute-start.4) | collective-permute-done | bytes 65568 | tf_op jit(solution)/shard_map/ppermute | solution.py:301
  20.4 0.0 collective-permute-done.5
  20.5 1.6 %collective-permute-start.8 = (bf16[4,16,1024]{2,1,0:T(8,128)(2,1)S(1)}, bf16[4,16,1024]{2,1,0:T(8,128)(2,1)S(1)}, u32[]{:S(2)}, u32[]{:S(2)}) collective-permute-start(bf16[4,16,1024]{2,1,0:T(8,128)(2,1)S(1)} %pad_maximum_fusion.3), channel_id=1, source_target_pairs={{0,2},{1,3},{2,0},{3,1},{4,6},{5,7},{6,4},{7,5},{8,10},{9,11},{10,... | collective-permute-start | bytes 393224 | tf_op jit(solution)/shard_map/ppermute | solution.py:301
  22.1 1.4 %collective-permute-start.6 = (bf16[4,16,1024]{2,1,0:T(8,128)(2,1)S(1)}, bf16[4,16,1024]{2,1,0:T(8,128)(2,1)S(1)}, u32[]{:S(2)}, u32[]{:S(2)}) collective-permute-start(bf16[4,16,1024]{2,1,0:T(8,128)(2,1)S(1)} %pad_maximum_fusion.3), channel_id=1, source_target_pairs={{0,18},{1,19},{2,16},{3,17},{4,22},{5,23},{6,20},{7,21},{8,26},{9,... | collective-permute-start | bytes 393224 | tf_op jit(solution)/shard_map/ppermute | solution.py:303
  23.5 0.0 collective-permute-done.10.refs_2_
  23.5 0.9 %collective-permute-start.7 = (bf16[4,16,1024]{2,1,0:T(8,128)(2,1)S(1)}, bf16[4,16,1024]{2,1,0:T(8,128)(2,1)S(1)}, u32[]{:S(2)}, u32[]{:S(2)}) collective-permute-start(bf16[4,16,1024]{2,1,0:T(8,128)(2,1)S(1)} %pad_maximum_fusion.2.refs_0_), channel_id=1, source_target_pairs={{0,16},{1,17},{2,18},{3,19},{4,20},{5,21},{6,22},{7,23},{8,24},{9,... | collective-permute-start | bytes 393224 | tf_op jit(solution)/shard_map/ppermute | solution.py:303
  24.4 0.0 copy-done
  24.4 0.0 collective-permute-done.11.refs_3_
  24.4 0.0 collective-permute-done.9.refs_1_
  24.5 0.5 %image.2.refs_4_ = f32[512,1024]{1,0:T(8,128)S(1)} custom-call(bf16[512,512]{1,0:T(8,128)(2,1)S(1)} %dynamic-slice_bitcast_fusion.table, bf16[4,16,1024]{2,1,0:T(8,128)(2,1)S(1)} %pad_maximum_fusion.4.refs_0_, bf16[4,16,1024]{2,1,0:T(8,128)(2,1)S(1)} %collective-permute-done.9.refs_1_, bf16[4,16,1024]{2,1,0:T(8,128)(2,1)S(1)} %collective-permute-done.10.refs_2_, ...), custom_call_target="tpu_custom_call" | custom-call | flops 268435456 | bytes 2097152 | tf_op jit(solution)/shard_map/image/pallas_call | solution.py:248
  24.9 4.2 %collective-permute-done.7.refs_2_ = bf16[4,16,1024]{2,1,0:T(8,128)(2,1)S(1)} collective-permute-done((bf16[4,16,1024]{2,1,0:T(8,128)(2,1)S(1)}, bf16[4,16,1024]{2,1,0:T(8,128)(2,1)S(1)}, u32[]{:S(2)}, u32[]{:S(2)}) %collective-permute-start.7) | collective-permute-done | bytes 131104 | tf_op jit(solution)/shard_map/ppermute | solution.py:303
  29.2 0.0 collective-permute-done.8.refs_3_
  29.2 0.0 collective-permute-done.6.refs_1_
  29.2 1.5 %image.3 = bf16[512,1024]{1,0:T(8,128)(2,1)} custom-call(bf16[512,512]{1,0:T(8,128)(2,1)S(1)} %dynamic-slice_bitcast_fusion.table, bf16[4,16,1024]{2,1,0:T(8,128)(2,1)S(1)} %pad_maximum_fusion.2.refs_0_, bf16[4,16,1024]{2,1,0:T(8,128)(2,1)S(1)} %collective-permute-done.6.refs_1_, bf16[4,16,1024]{2,1,0:T(8,128)(2,1)S(1)} %collective-permute-done.7.refs_2_, ...), custom_call_target="tpu_custom_call" | custom-call | flops 268435456 | bytes 2097152 | tf_op jit(solution)/shard_map/image/pallas_call | solution.py:248
  (12 shorter events, 0.2 us)
Async XLA Ops:
  0.0 24.4 %copy-start = (bf16[2,512,512]{2,1,0:T(8,128)(2,1)S(1)}, bf16[2,512,512]{2,1,0:T(8,128)(2,1)}, u32[]{:S(2)}) copy-start(bf16[2,512,512]{2,1,0:T(8,128)(2,1)} %constant.23.clone) | copy-start | bytes 3145732
  3.3 4.2 %collective-permute-start.1 = (bf16[6,16,1024]{2,1,0:T(8,128)(2,1)S(1)}, bf16[6,16,1024]{2,1,0:T(8,128)(2,1)S(1)}, u32[]{:S(2)}, u32[]{:S(2)}) collective-permute-start(bf16[6,16,1024]{2,1,0:T(8,128)(2,1)S(1)} %get-tuple-element.15), channel_id=1, source_target_pairs={{0,1},{1,0},{2,3},{3,2},{4,5},{5,4},{6,7},{7,6},{8,9},{9,8},{10,11... | collective-permute-start | bytes 589832 | tf_op jit(solution)/shard_map/ppermute | solution.py:301
  3.9 13.0 %collective-permute-start = (bf16[2,16,1024]{2,1,0:T(8,128)(2,1)S(1)}, bf16[2,16,1024]{2,1,0:T(8,128)(2,1)S(1)}, u32[]{:S(2)}, u32[]{:S(2)}) collective-permute-start(bf16[2,16,1024]{2,1,0:T(8,128)(2,1)S(1)} %get-tuple-element.13), channel_id=1, source_target_pairs={{0,8},{1,9},{2,10},{3,11},{4,12},{5,13},{6,14},{7,15},{8,0},{9,1},... | collective-permute-start | bytes 196616 | tf_op jit(solution)/shard_map/ppermute | solution.py:301
  7.5 3.2 %collective-permute-start.3 = (bf16[2,16,1024]{2,1,0:T(8,128)(2,1)S(1)}, bf16[2,16,1024]{2,1,0:T(8,128)(2,1)S(1)}, u32[]{:S(2)}, u32[]{:S(2)}) collective-permute-start(bf16[2,16,1024]{2,1,0:T(8,128)(2,1)S(1)} %get-tuple-element.18), channel_id=1, source_target_pairs={{0,1},{1,0},{2,3},{3,2},{4,5},{5,4},{6,7},{7,6},{8,9},{9,8},{10,11... | collective-permute-start | bytes 196616 | tf_op jit(solution)/shard_map/ppermute | solution.py:301
  7.7 6.0 %collective-permute-start.2 = (bf16[2,2,16,1024]{3,2,1,0:T(8,128)(2,1)S(1)}, bf16[2,2,16,1024]{3,2,1,0:T(8,128)(2,1)S(1)}, u32[]{:S(2)}, u32[]{:S(2)}) collective-permute-start(bf16[2,2,16,1024]{3,2,1,0:T(8,128)(2,1)S(1)} %pad_maximum_fusion), channel_id=1, source_target_pairs={{0,4},{1,5},{2,6},{3,7},{4,0},{5,1},{6,2},{7,3},{8,12},{9,13},{10,... | collective-permute-start | bytes 393224 | tf_op jit(solution)/shard_map/ppermute | solution.py:301
  9.4 11.1 %collective-permute-start.5 = (bf16[2,2,16,1024]{3,2,1,0:T(8,128)(2,1)S(1)}, bf16[2,2,16,1024]{3,2,1,0:T(8,128)(2,1)S(1)}, u32[]{:S(2)}, u32[]{:S(2)}) collective-permute-start(bf16[2,2,16,1024]{3,2,1,0:T(8,128)(2,1)S(1)} %pad_maximum_fusion.1), channel_id=1, source_target_pairs={{0,12},{1,13},{2,14},{3,15},{4,8},{5,9},{6,10},{7,11},{8,4},{9,5},... | collective-permute-start | bytes 393224 | tf_op jit(solution)/shard_map/ppermute | solution.py:301
  10.7 9.7 %collective-permute-start.4 = (bf16[2,16,1024]{2,1,0:T(8,128)(2,1)S(1)}, bf16[2,16,1024]{2,1,0:T(8,128)(2,1)S(1)}, u32[]{:S(2)}, u32[]{:S(2)}) collective-permute-start(bf16[2,16,1024]{2,1,0:T(8,128)(2,1)S(1)} %collective-permute-done.3), channel_id=1, source_target_pairs={{0,8},{1,9},{2,10},{3,11},{4,12},{5,13},{6,14},{7,15},{8,0},{9,1},... | collective-permute-start | bytes 196616 | tf_op jit(solution)/shard_map/ppermute | solution.py:301
  13.8 10.6 %collective-permute-start.11 = (bf16[4,16,1024]{2,1,0:T(8,128)(2,1)S(1)}, bf16[4,16,1024]{2,1,0:T(8,128)(2,1)S(1)}, u32[]{:S(2)}, u32[]{:S(2)}) collective-permute-start(bf16[4,16,1024]{2,1,0:T(8,128)(2,1)S(1)} %pad_maximum_fusion.5), channel_id=1, source_target_pairs={{0,2},{1,3},{2,0},{3,1},{4,6},{5,7},{6,4},{7,5},{8,10},{9,11},{10,... | collective-permute-start | bytes 393224 | tf_op jit(solution)/shard_map/ppermute | solution.py:301
  15.4 9.0 %collective-permute-start.9 = (bf16[4,16,1024]{2,1,0:T(8,128)(2,1)S(1)}, bf16[4,16,1024]{2,1,0:T(8,128)(2,1)S(1)}, u32[]{:S(2)}, u32[]{:S(2)}) collective-permute-start(bf16[4,16,1024]{2,1,0:T(8,128)(2,1)S(1)} %pad_maximum_fusion.5), channel_id=1, source_target_pairs={{0,18},{1,19},{2,16},{3,17},{4,22},{5,23},{6,20},{7,21},{8,26},{9,... | collective-permute-start | bytes 393224 | tf_op jit(solution)/shard_map/ppermute | solution.py:303
  16.9 6.6 %collective-permute-start.10 = (bf16[4,16,1024]{2,1,0:T(8,128)(2,1)S(1)}, bf16[4,16,1024]{2,1,0:T(8,128)(2,1)S(1)}, u32[]{:S(2)}, u32[]{:S(2)}) collective-permute-start(bf16[4,16,1024]{2,1,0:T(8,128)(2,1)S(1)} %pad_maximum_fusion.4.refs_0_), channel_id=1, source_target_pairs={{0,16},{1,17},{2,18},{3,19},{4,20},{5,21},{6,22},{7,23},{8,24},{9,... | collective-permute-start | bytes 393224 | tf_op jit(solution)/shard_map/ppermute | solution.py:303
  20.5 8.7 %collective-permute-start.8 = (bf16[4,16,1024]{2,1,0:T(8,128)(2,1)S(1)}, bf16[4,16,1024]{2,1,0:T(8,128)(2,1)S(1)}, u32[]{:S(2)}, u32[]{:S(2)}) collective-permute-start(bf16[4,16,1024]{2,1,0:T(8,128)(2,1)S(1)} %pad_maximum_fusion.3), channel_id=1, source_target_pairs={{0,2},{1,3},{2,0},{3,1},{4,6},{5,7},{6,4},{7,5},{8,10},{9,11},{10,... | collective-permute-start | bytes 393224 | tf_op jit(solution)/shard_map/ppermute | solution.py:301
  22.1 7.1 %collective-permute-start.6 = (bf16[4,16,1024]{2,1,0:T(8,128)(2,1)S(1)}, bf16[4,16,1024]{2,1,0:T(8,128)(2,1)S(1)}, u32[]{:S(2)}, u32[]{:S(2)}) collective-permute-start(bf16[4,16,1024]{2,1,0:T(8,128)(2,1)S(1)} %pad_maximum_fusion.3), channel_id=1, source_target_pairs={{0,18},{1,19},{2,16},{3,17},{4,22},{5,23},{6,20},{7,21},{8,26},{9,... | collective-permute-start | bytes 393224 | tf_op jit(solution)/shard_map/ppermute | solution.py:303
  23.5 5.7 %collective-permute-start.7 = (bf16[4,16,1024]{2,1,0:T(8,128)(2,1)S(1)}, bf16[4,16,1024]{2,1,0:T(8,128)(2,1)S(1)}, u32[]{:S(2)}, u32[]{:S(2)}) collective-permute-start(bf16[4,16,1024]{2,1,0:T(8,128)(2,1)S(1)} %pad_maximum_fusion.2.refs_0_), channel_id=1, source_target_pairs={{0,16},{1,17},{2,18},{3,19},{4,20},{5,21},{6,22},{7,23},{8,24},{9,... | collective-permute-start | bytes 393224 | tf_op jit(solution)/shard_map/ppermute | solution.py:303

commit v4 on v3

--- a/solution.py
+++ b/solution.py
@@ -97,11 +97,11 @@
 
 
 def compress_kernel(
-    plan, delays, raw_far, dft_far, twiddle_far, near_far, *refs
+    plan, delays_far, raw_far, dft_far, twiddle_far, near_far, *refs
 ):
     outs = refs[: len(plan)]
     (
-    raw, dft, twiddle, near, arrived, lines, grid_in, section, twisted, turned,
+    delays, raw, dft, twiddle, near, arrived, lines, grid_in, section, twisted, turned,
     ) = refs[len(plan) :]
     pulse_count = raw.shape[1]
     width = outs[0].shape[-1]
@@ -118,7 +118,9 @@
     ]
     tables = [
         pltpu.make_async_copy(far, here, arrived.at[RAW_PIECES + index])
-        for index, (far, here) in enumerate(((dft_far, dft), (twiddle_far, twiddle), (near_far, near)))
+        for index, (far, here) in enumerate(
+            ((dft_far, dft), (delays_far, delays), (twiddle_far, twiddle), (near_far, near))
+        )
     ]
     for copy in pieces + tables:
         copy.start()
@@ -143,6 +145,7 @@
             section[pulse, part, pl.ds(0, RADIX), :] = own
             section[pulse, part, pl.ds(RADIX, DELAY_MAX), :] = own[:DELAY_MAX]
     tables[1].wait()
+    tables[2].wait()
     for pulse in range(pulse_count):
         window = pl.ds(delays[pulse], RADIX)
         real_part = section[pulse, 0, window, :]
@@ -155,7 +158,7 @@
     row_index = lax.broadcasted_iota(jnp.int32, (RADIX, LANES), 0)
     lane_index = lax.broadcasted_iota(jnp.int32, (RADIX, LANES), 1)
     gates = row_index * LANES + lane_index
-    tables[2].wait()
+    tables[3].wait()
     for pulse in range(pulse_count):
         sums = lax.dot_general(
             dft[...],
@@ -194,14 +197,15 @@
         out_shape=[
             pltpu.VMEM((len(places), 2 * pulse_count, width), jnp.bfloat16) for places in plan
         ],
-        in_specs=[pl.BlockSpec(memory_space=pltpu.SMEM)] + [pl.BlockSpec(memory_space=pltpu.HBM)] * 4,
+        in_specs=[pl.BlockSpec(memory_space=pltpu.HBM)] * 5,
         out_specs=[pl.BlockSpec(memory_space=pltpu.VMEM)] * len(plan),
         scratch_shapes=[
+            pltpu.SMEM(delays.shape, delays.dtype),
             pltpu.VMEM(raw_echo.shape, raw_echo.dtype),
             pltpu.VMEM(dft.shape, dft.dtype),
             pltpu.VMEM(twiddle.shape, twiddle.dtype),
             pltpu.VMEM(near.shape, near.dtype),
-            pltpu.SemaphoreType.DMA((RAW_PIECES + 3,)),
+            pltpu.SemaphoreType.DMA((RAW_PIECES + 4,)),
             pltpu.VMEM((2 * span, LANES), jnp.float32),
             pltpu.VMEM((2 * RADIX, pulse_count * LANES), jnp.bfloat16),
             pltpu.VMEM((pulse_count, 2, ROWS, LANES), jnp.float32),
@@ -215,7 +219,10 @@
 
 def image_kernel(plan, far, has_total, table, *refs):
     arrays, refs = refs[: len(plan)], refs[len(plan) :]
-    total, (out, data, columns) = (refs[0], refs[1:]) if has_total else (None, refs)
+    if has_total:
+        total, out_far, data, columns, out, sent = refs
+    else:
+        out, data, columns = refs
     half = data.shape[0] // 2
     block = arrays[0].shape[1]
     me = lax.axis_index("gate")
@@ -229,6 +236,7 @@
         source = pl.multiple_of(side * 2 * half + lower, half)
         columns[:, pl.ds(side * half, half)] = table[:, pl.ds(source, half)]
     tile = 256
+    copies = []
     for row in range(0, out.shape[0], tile):
         for column in range(0, out.shape[1], tile):
             place = pl.ds(row, tile), pl.ds(column, tile)
@@ -236,6 +244,11 @@
             if has_total:
                 sums = sums + total[place]
             out[place] = sums.astype(out.dtype)
+            if has_total:
+                copies.append(pltpu.make_async_copy(out.at[place], out_far.at[place], sent.at[len(copies)]))
+                copies[-1].start()
+    for copy in copies:
+        copy.wait()
 
 
 def form_image(table, arrays, plan):
@@ -249,8 +262,9 @@
             functools.partial(image_kernel, [plan[i] for i in used], far, bool(total)),
             out_shape=jax.ShapeDtypeStruct(shape, jnp.bfloat16) if far else pltpu.VMEM(shape, jnp.float32),
             in_specs=[vmem] * (1 + len(used) + len(total)),
-            out_specs=vmem,
-            scratch_shapes=[pltpu.VMEM((depth, shape[1]), jnp.bfloat16), pltpu.VMEM((rows, depth), jnp.bfloat16)],
+            out_specs=pl.BlockSpec(memory_space=pltpu.HBM) if far else vmem,
+            scratch_shapes=[pltpu.VMEM((depth, shape[1]), jnp.bfloat16), pltpu.VMEM((rows, depth), jnp.bfloat16)]
+            + ([pltpu.VMEM(shape, jnp.bfloat16), pltpu.SemaphoreType.DMA((rows // 256 * (shape[1] // 256),))] if far else []),
             cost_estimate=pl.CostEstimate(
                 flops=2 * depth * math.prod(shape), bytes_accessed=4 * math.prod(shape), transcendentals=0
             ),

time: 30.8 us -> 30 us (0.974)
  Pallas kernels: 5.28 us -> 4.45 us
    pallas_call x1, Pallas kernels: 3.32 us -> 2.63 us  [range_compress(): pl.pallas_call(functools.partial(compress_kernel, plan), out_shape=[pltpu...]
where the time goes in v4:
time: 30 us; the launch traced here: 29.8 us
  starting transfers between devices  15.5 us (52%)
  waiting for transfers between devices  9.55 us (32%)
  Pallas kernels  4.45 us (15%)
    ppermute x8, starting transfers between devices, swap(): return lax.ppermute(array, 'gate', [(i, i ^ apart) for i in range(count)])  11.3 us
    ppermute x8, waiting for transfers between devices, swap(): return lax.ppermute(array, 'gate', [(i, i ^ apart) for i in range(count)])  5.3 us
    ppermute x4, starting transfers between devices, swap(): return lax.ppermute(array, ('sub', 'gate'), pairs)  4.27 us
    ppermute x4, waiting for transfers between devices, swap(): return lax.ppermute(array, ('sub', 'gate'), pairs)  4.25 us
    pallas_call x1, Pallas kernels, range_compress(): pl.pallas_call(functools.partial(compress_kernel, plan), out_shape=[pltpu...  2.63 us
    pallas_call x2, Pallas kernels, form_image(): pl.pallas_call(functools.partial(image_kernel, [plan[i] for i in used], f...  1.81 us
  transfers between devices with their start and end apart: 12, of which 3 were waited for; matrix products, arithmetic and copies ran while one was open for 1% of the time, Pallas kernels for 2%

profile of v4, /device:TPU:0, one launch (start us, length us, event | category | flops | bytes accessed | tf_op | source)
XLA Modules:
  0.0 29.8 jit_solution(3419218649451792285)
XLA Ops:
  0.0 0.0 copy-start
  0.0 2.6 %compress.1 = (bf16[2,16,1024]{2,1,0:T(8,128)(2,1)S(1)}, bf16[2,16,1024]{2,1,0:T(8,128)(2,1)S(1)}, bf16[2,16,1024]{2,1,0:T(8,128)(2,1)S(1)}, bf16[2,16,1024]{2,1...) custom-call(s32[8]{0:T(128)} %delays_far.1, bf16[2,8,16384]{2,1,0:T(8,128)(2,1)} %raw_far.1, ...), custom_call_target="tpu_custom_call" | custom-call | tf_op jit(solution)/shard_map/compress/pallas_call | solution.py:195
  2.6 0.5 %collective-permute-start.1 = (bf16[6,16,1024]{2,1,0:T(8,128)(2,1)S(1)}, bf16[6,16,1024]{2,1,0:T(8,128)(2,1)S(1)}, u32[]{:S(2)}, u32[]{:S(2)}) collective-permute-start(bf16[6,16,1024]{2,1,0:T(8,128)(2,1)S(1)} %get-tuple-element.15), channel_id=1, source_target_pairs={{0,1},{1,0},{2,3},{3,2},{4,5},{5,4},{6,7},{7,6},{8,9},{9,8},{10,11... | collective-permute-start | bytes 589832 | tf_op jit(solution)/shard_map/ppermute | solution.py:315
  3.2 3.7 %collective-permute-start = (bf16[2,16,1024]{2,1,0:T(8,128)(2,1)S(1)}, bf16[2,16,1024]{2,1,0:T(8,128)(2,1)S(1)}, u32[]{:S(2)}, u32[]{:S(2)}) collective-permute-start(bf16[2,16,1024]{2,1,0:T(8,128)(2,1)S(1)} %get-tuple-element.13), channel_id=1, source_target_pairs={{0,8},{1,9},{2,10},{3,11},{4,12},{5,13},{6,14},{7,15},{8,0},{9,1},... | collective-permute-start | bytes 196616 | tf_op jit(solution)/shard_map/ppermute | solution.py:315
  6.8 0.0 collective-permute-done.1
  6.8 0.2 collective-permute-start.3
  7.0 1.6 %collective-permute-start.2 = (bf16[2,2,16,1024]{3,2,1,0:T(8,128)(2,1)S(1)}, bf16[2,2,16,1024]{3,2,1,0:T(8,128)(2,1)S(1)}, u32[]{:S(2)}, u32[]{:S(2)}) collective-permute-start(bf16[2,2,16,1024]{3,2,1,0:T(8,128)(2,1)S(1)} %pad_maximum_fusion), channel_id=1, source_target_pairs={{0,4},{1,5},{2,6},{3,7},{4,0},{5,1},{6,2},{7,3},{8,12},{9,13},{10,... | collective-permute-start | bytes 393224 | tf_op jit(solution)/shard_map/ppermute | solution.py:315
  8.7 1.3 %collective-permute-start.5 = (bf16[2,2,16,1024]{3,2,1,0:T(8,128)(2,1)S(1)}, bf16[2,2,16,1024]{3,2,1,0:T(8,128)(2,1)S(1)}, u32[]{:S(2)}, u32[]{:S(2)}) collective-permute-start(bf16[2,2,16,1024]{3,2,1,0:T(8,128)(2,1)S(1)} %pad_maximum_fusion.1), channel_id=1, source_target_pairs={{0,12},{1,13},{2,14},{3,15},{4,8},{5,9},{6,10},{7,11},{8,4},{9,5},... | collective-permute-start | bytes 393224 | tf_op jit(solution)/shard_map/ppermute | solution.py:315
  10.0 0.0 collective-permute-done.3
  10.0 0.7 %collective-permute-start.4 = (bf16[2,16,1024]{2,1,0:T(8,128)(2,1)S(1)}, bf16[2,16,1024]{2,1,0:T(8,128)(2,1)S(1)}, u32[]{:S(2)}, u32[]{:S(2)}) collective-permute-start(bf16[2,16,1024]{2,1,0:T(8,128)(2,1)S(1)} %collective-permute-done.3), channel_id=1, source_target_pairs={{0,8},{1,9},{2,10},{3,11},{4,12},{5,13},{6,14},{7,15},{8,0},{9,1},... | collective-permute-start | bytes 196616 | tf_op jit(solution)/shard_map/ppermute | solution.py:315
  10.8 2.3 %collective-permute-done.2 = bf16[2,2,16,1024]{3,2,1,0:T(8,128)(2,1)S(1)} collective-permute-done((bf16[2,2,16,1024]{3,2,1,0:T(8,128)(2,1)S(1)}, bf16[2,2,16,1024]{3,2,1,0:T(8,128)(2,1)S(1)}, u32[]{:S(2)}, u32[]{:S(2)}) %collective-permute-start.2) | collective-permute-done | bytes 131104 | tf_op jit(solution)/shard_map/ppermute | solution.py:315
  13.1 1.6 %collective-permute-start.11 = (bf16[4,16,1024]{2,1,0:T(8,128)(2,1)S(1)}, bf16[4,16,1024]{2,1,0:T(8,128)(2,1)S(1)}, u32[]{:S(2)}, u32[]{:S(2)}) collective-permute-start(bf16[4,16,1024]{2,1,0:T(8,128)(2,1)S(1)} %pad_maximum_fusion.5), channel_id=1, source_target_pairs={{0,2},{1,3},{2,0},{3,1},{4,6},{5,7},{6,4},{7,5},{8,10},{9,11},{10,... | collective-permute-start | bytes 393224 | tf_op jit(solution)/shard_map/ppermute | solution.py:315
  14.8 1.4 %collective-permute-start.9 = (bf16[4,16,1024]{2,1,0:T(8,128)(2,1)S(1)}, bf16[4,16,1024]{2,1,0:T(8,128)(2,1)S(1)}, u32[]{:S(2)}, u32[]{:S(2)}) collective-permute-start(bf16[4,16,1024]{2,1,0:T(8,128)(2,1)S(1)} %pad_maximum_fusion.5), channel_id=1, source_target_pairs={{0,18},{1,19},{2,16},{3,17},{4,22},{5,23},{6,20},{7,21},{8,26},{9,... | collective-permute-start | bytes 393224 | tf_op jit(solution)/shard_map/ppermute | solution.py:317
  16.2 0.0 collective-permute-done
  16.2 0.5 %collective-permute-start.10 = (bf16[4,16,1024]{2,1,0:T(8,128)(2,1)S(1)}, bf16[4,16,1024]{2,1,0:T(8,128)(2,1)S(1)}, u32[]{:S(2)}, u32[]{:S(2)}) collective-permute-start(bf16[4,16,1024]{2,1,0:T(8,128)(2,1)S(1)} %pad_maximum_fusion.4.refs_0_), channel_id=1, source_target_pairs={{0,16},{1,17},{2,18},{3,19},{4,20},{5,21},{6,22},{7,23},{8,24},{9,... | collective-permute-start | bytes 393224 | tf_op jit(solution)/shard_map/ppermute | solution.py:317
  16.8 3.0 %collective-permute-done.4 = bf16[2,16,1024]{2,1,0:T(8,128)(2,1)S(1)} collective-permute-done((bf16[2,16,1024]{2,1,0:T(8,128)(2,1)S(1)}, bf16[2,16,1024]{2,1,0:T(8,128)(2,1)S(1)}, u32[]{:S(2)}, u32[]{:S(2)}) %collective-permute-start.4) | collective-permute-done | bytes 65568 | tf_op jit(solution)/shard_map/ppermute | solution.py:315
  19.7 0.0 collective-permute-done.5
  19.8 1.6 %collective-permute-start.8 = (bf16[4,16,1024]{2,1,0:T(8,128)(2,1)S(1)}, bf16[4,16,1024]{2,1,0:T(8,128)(2,1)S(1)}, u32[]{:S(2)}, u32[]{:S(2)}) collective-permute-start(bf16[4,16,1024]{2,1,0:T(8,128)(2,1)S(1)} %pad_maximum_fusion.3), channel_id=1, source_target_pairs={{0,2},{1,3},{2,0},{3,1},{4,6},{5,7},{6,4},{7,5},{8,10},{9,11},{10,... | collective-permute-start | bytes 393224 | tf_op jit(solution)/shard_map/ppermute | solution.py:315
  21.4 1.4 %collective-permute-start.6 = (bf16[4,16,1024]{2,1,0:T(8,128)(2,1)S(1)}, bf16[4,16,1024]{2,1,0:T(8,128)(2,1)S(1)}, u32[]{:S(2)}, u32[]{:S(2)}) collective-permute-start(bf16[4,16,1024]{2,1,0:T(8,128)(2,1)S(1)} %pad_maximum_fusion.3), channel_id=1, source_target_pairs={{0,18},{1,19},{2,16},{3,17},{4,22},{5,23},{6,20},{7,21},{8,26},{9,... | collective-permute-start | bytes 393224 | tf_op jit(solution)/shard_map/ppermute | solution.py:317
  22.8 0.0 collective-permute-done.10.refs_2_
  22.8 0.9 %collective-permute-start.7 = (bf16[4,16,1024]{2,1,0:T(8,128)(2,1)S(1)}, bf16[4,16,1024]{2,1,0:T(8,128)(2,1)S(1)}, u32[]{:S(2)}, u32[]{:S(2)}) collective-permute-start(bf16[4,16,1024]{2,1,0:T(8,128)(2,1)S(1)} %pad_maximum_fusion.2.refs_0_), channel_id=1, source_target_pairs={{0,16},{1,17},{2,18},{3,19},{4,20},{5,21},{6,22},{7,23},{8,24},{9,... | collective-permute-start | bytes 393224 | tf_op jit(solution)/shard_map/ppermute | solution.py:317
  23.7 0.0 copy-done
  23.7 0.0 collective-permute-done.11.refs_3_
  23.8 0.0 collective-permute-done.9.refs_1_
  23.8 0.5 %image.2.refs_4_ = f32[512,1024]{1,0:T(8,128)S(1)} custom-call(bf16[512,512]{1,0:T(8,128)(2,1)S(1)} %dynamic-slice_bitcast_fusion.table, bf16[4,16,1024]{2,1,0:T(8,128)(2,1)S(1)} %pad_maximum_fusion.4.refs_0_, bf16[4,16,1024]{2,1,0:T(8,128)(2,1)S(1)} %collective-permute-done.9.refs_1_, bf16[4,16,1024]{2,1,0:T(8,128)(2,1)S(1)} %collective-permute-done.10.refs_2_, ...), custom_call_target="tpu_custom_call" | custom-call | flops 268435456 | bytes 2097152 | tf_op jit(solution)/shard_map/image/pallas_call | solution.py:261
  24.3 4.2 %collective-permute-done.7.refs_2_ = bf16[4,16,1024]{2,1,0:T(8,128)(2,1)S(1)} collective-permute-done((bf16[4,16,1024]{2,1,0:T(8,128)(2,1)S(1)}, bf16[4,16,1024]{2,1,0:T(8,128)(2,1)S(1)}, u32[]{:S(2)}, u32[]{:S(2)}) %collective-permute-start.7) | collective-permute-done | bytes 131104 | tf_op jit(solution)/shard_map/ppermute | solution.py:317
  28.5 0.0 collective-permute-done.8.refs_3_
  28.5 0.0 collective-permute-done.6.refs_1_
  28.5 1.3 %image.3 = bf16[512,1024]{1,0:T(8,128)(2,1)} custom-call(bf16[512,512]{1,0:T(8,128)(2,1)S(1)} %dynamic-slice_bitcast_fusion.table, bf16[4,16,1024]{2,1,0:T(8,128)(2,1)S(1)} %pad_maximum_fusion.2.refs_0_, bf16[4,16,1024]{2,1,0:T(8,128)(2,1)S(1)} %collective-permute-done.6.refs_1_, bf16[4,16,1024]{2,1,0:T(8,128)(2,1)S(1)} %collective-permute-done.7.refs_2_, ...), custom_call_target="tpu_custom_call" | custom-call | flops 268435456 | bytes 2097152 | tf_op jit(solution)/shard_map/image/pallas_call | solution.py:261
  (12 shorter events, 0.2 us)
Async XLA Ops:
  0.0 23.7 %copy-start = (bf16[2,512,512]{2,1,0:T(8,128)(2,1)S(1)}, bf16[2,512,512]{2,1,0:T(8,128)(2,1)}, u32[]{:S(2)}) copy-start(bf16[2,512,512]{2,1,0:T(8,128)(2,1)} %constant.23.clone) | copy-start | bytes 3145732
  2.6 4.2 %collective-permute-start.1 = (bf16[6,16,1024]{2,1,0:T(8,128)(2,1)S(1)}, bf16[6,16,1024]{2,1,0:T(8,128)(2,1)S(1)}, u32[]{:S(2)}, u32[]{:S(2)}) collective-permute-start(bf16[6,16,1024]{2,1,0:T(8,128)(2,1)S(1)} %get-tuple-element.15), channel_id=1, source_target_pairs={{0,1},{1,0},{2,3},{3,2},{4,5},{5,4},{6,7},{7,6},{8,9},{9,8},{10,11... | collective-permute-start | bytes 589832 | tf_op jit(solution)/shard_map/ppermute | solution.py:315
  3.2 13.0 %collective-permute-start = (bf16[2,16,1024]{2,1,0:T(8,128)(2,1)S(1)}, bf16[2,16,1024]{2,1,0:T(8,128)(2,1)S(1)}, u32[]{:S(2)}, u32[]{:S(2)}) collective-permute-start(bf16[2,16,1024]{2,1,0:T(8,128)(2,1)S(1)} %get-tuple-element.13), channel_id=1, source_target_pairs={{0,8},{1,9},{2,10},{3,11},{4,12},{5,13},{6,14},{7,15},{8,0},{9,1},... | collective-permute-start | bytes 196616 | tf_op jit(solution)/shard_map/ppermute | solution.py:315
  6.8 3.2 %collective-permute-start.3 = (bf16[2,16,1024]{2,1,0:T(8,128)(2,1)S(1)}, bf16[2,16,1024]{2,1,0:T(8,128)(2,1)S(1)}, u32[]{:S(2)}, u32[]{:S(2)}) collective-permute-start(bf16[2,16,1024]{2,1,0:T(8,128)(2,1)S(1)} %get-tuple-element.18), channel_id=1, source_target_pairs={{0,1},{1,0},{2,3},{3,2},{4,5},{5,4},{6,7},{7,6},{8,9},{9,8},{10,11... | collective-permute-start | bytes 196616 | tf_op jit(solution)/shard_map/ppermute | solution.py:315
  7.0 6.0 %collective-permute-start.2 = (bf16[2,2,16,1024]{3,2,1,0:T(8,128)(2,1)S(1)}, bf16[2,2,16,1024]{3,2,1,0:T(8,128)(2,1)S(1)}, u32[]{:S(2)}, u32[]{:S(2)}) collective-permute-start(bf16[2,2,16,1024]{3,2,1,0:T(8,128)(2,1)S(1)} %pad_maximum_fusion), channel_id=1, source_target_pairs={{0,4},{1,5},{2,6},{3,7},{4,0},{5,1},{6,2},{7,3},{8,12},{9,13},{10,... | collective-permute-start | bytes 393224 | tf_op jit(solution)/shard_map/ppermute | solution.py:315
  8.7 11.1 %collective-permute-start.5 = (bf16[2,2,16,1024]{3,2,1,0:T(8,128)(2,1)S(1)}, bf16[2,2,16,1024]{3,2,1,0:T(8,128)(2,1)S(1)}, u32[]{:S(2)}, u32[]{:S(2)}) collective-permute-start(bf16[2,2,16,1024]{3,2,1,0:T(8,128)(2,1)S(1)} %pad_maximum_fusion.1), channel_id=1, source_target_pairs={{0,12},{1,13},{2,14},{3,15},{4,8},{5,9},{6,10},{7,11},{8,4},{9,5},... | collective-permute-start | bytes 393224 | tf_op jit(solution)/shard_map/ppermute | solution.py:315
  10.0 9.7 %collective-permute-start.4 = (bf16[2,16,1024]{2,1,0:T(8,128)(2,1)S(1)}, bf16[2,16,1024]{2,1,0:T(8,128)(2,1)S(1)}, u32[]{:S(2)}, u32[]{:S(2)}) collective-permute-start(bf16[2,16,1024]{2,1,0:T(8,128)(2,1)S(1)} %collective-permute-done.3), channel_id=1, source_target_pairs={{0,8},{1,9},{2,10},{3,11},{4,12},{5,13},{6,14},{7,15},{8,0},{9,1},... | collective-permute-start | bytes 196616 | tf_op jit(solution)/shard_map/ppermute | solution.py:315
  13.1 10.6 %collective-permute-start.11 = (bf16[4,16,1024]{2,1,0:T(8,128)(2,1)S(1)}, bf16[4,16,1024]{2,1,0:T(8,128)(2,1)S(1)}, u32[]{:S(2)}, u32[]{:S(2)}) collective-permute-start(bf16[4,16,1024]{2,1,0:T(8,128)(2,1)S(1)} %pad_maximum_fusion.5), channel_id=1, source_target_pairs={{0,2},{1,3},{2,0},{3,1},{4,6},{5,7},{6,4},{7,5},{8,10},{9,11},{10,... | collective-permute-start | bytes 393224 | tf_op jit(solution)/shard_map/ppermute | solution.py:315
  14.8 9.0 %collective-permute-start.9 = (bf16[4,16,1024]{2,1,0:T(8,128)(2,1)S(1)}, bf16[4,16,1024]{2,1,0:T(8,128)(2,1)S(1)}, u32[]{:S(2)}, u32[]{:S(2)}) collective-permute-start(bf16[4,16,1024]{2,1,0:T(8,128)(2,1)S(1)} %pad_maximum_fusion.5), channel_id=1, source_target_pairs={{0,18},{1,19},{2,16},{3,17},{4,22},{5,23},{6,20},{7,21},{8,26},{9,... | collective-permute-start | bytes 393224 | tf_op jit(solution)/shard_map/ppermute | solution.py:317
  16.2 6.6 %collective-permute-start.10 = (bf16[4,16,1024]{2,1,0:T(8,128)(2,1)S(1)}, bf16[4,16,1024]{2,1,0:T(8,128)(2,1)S(1)}, u32[]{:S(2)}, u32[]{:S(2)}) collective-permute-start(bf16[4,16,1024]{2,1,0:T(8,128)(2,1)S(1)} %pad_maximum_fusion.4.refs_0_), channel_id=1, source_target_pairs={{0,16},{1,17},{2,18},{3,19},{4,20},{5,21},{6,22},{7,23},{8,24},{9,... | collective-permute-start | bytes 393224 | tf_op jit(solution)/shard_map/ppermute | solution.py:317
  19.8 8.7 %collective-permute-start.8 = (bf16[4,16,1024]{2,1,0:T(8,128)(2,1)S(1)}, bf16[4,16,1024]{2,1,0:T(8,128)(2,1)S(1)}, u32[]{:S(2)}, u32[]{:S(2)}) collective-permute-start(bf16[4,16,1024]{2,1,0:T(8,128)(2,1)S(1)} %pad_maximum_fusion.3), channel_id=1, source_target_pairs={{0,2},{1,3},{2,0},{3,1},{4,6},{5,7},{6,4},{7,5},{8,10},{9,11},{10,... | collective-permute-start | bytes 393224 | tf_op jit(solution)/shard_map/ppermute | solution.py:315
  21.4 7.1 %collective-permute-start.6 = (bf16[4,16,1024]{2,1,0:T(8,128)(2,1)S(1)}, bf16[4,16,1024]{2,1,0:T(8,128)(2,1)S(1)}, u32[]{:S(2)}, u32[]{:S(2)}) collective-permute-start(bf16[4,16,1024]{2,1,0:T(8,128)(2,1)S(1)} %pad_maximum_fusion.3), channel_id=1, source_target_pairs={{0,18},{1,19},{2,16},{3,17},{4,22},{5,23},{6,20},{7,21},{8,26},{9,... | collective-permute-start | bytes 393224 | tf_op jit(solution)/shard_map/ppermute | solution.py:317
  22.8 5.7 %collective-permute-start.7 = (bf16[4,16,1024]{2,1,0:T(8,128)(2,1)S(1)}, bf16[4,16,1024]{2,1,0:T(8,128)(2,1)S(1)}, u32[]{:S(2)}, u32[]{:S(2)}) collective-permute-start(bf16[4,16,1024]{2,1,0:T(8,128)(2,1)S(1)} %pad_maximum_fusion.2.refs_0_), channel_id=1, source_target_pairs={{0,16},{1,17},{2,18},{3,19},{4,20},{5,21},{6,22},{7,23},{8,24},{9,... | collective-permute-start | bytes 393224 | tf_op jit(solution)/shard_map/ppermute | solution.py:317

commit v5 on v4

--- a/solution.py
+++ b/solution.py
@@ -137,13 +137,16 @@
                 pl.ds(part * span + pulse, RADIX, stride=pulse_count), :
             ].astype(jnp.bfloat16)
     tables[0].wait()
-    for pulse in range(pulse_count):
-        columns = pl.ds(pulse * LANES, LANES)
+    for first in range(0, pulse_count, 4):
+        columns = pl.ds(first * LANES, 4 * LANES)
         sums = jnp.dot(dft[...], grid_in[:, columns], preferred_element_type=jnp.float32)
-        for part in range(2):
-            own = sums[part * RADIX : (part + 1) * RADIX]
-            section[pulse, part, pl.ds(0, RADIX), :] = own
-            section[pulse, part, pl.ds(RADIX, DELAY_MAX), :] = own[:DELAY_MAX]
+        for pulse in range(first, first + 4):
+            for part in range(2):
+                own = sums[
+                    part * RADIX : (part + 1) * RADIX, (pulse - first) * LANES : (pulse - first + 1) * LANES
+                ]
+                section[pulse, part, pl.ds(0, RADIX), :] = own
+                section[pulse, part, pl.ds(RADIX, DELAY_MAX), :] = own[:DELAY_MAX]
     tables[1].wait()
     tables[2].wait()
     for pulse in range(pulse_count):
@@ -155,26 +158,33 @@
         rows = pl.ds(pulse * RADIX, RADIX)
         twisted[rows, pl.ds(0, LANES)] = (real_part * cosine - imag_part * sine_part).astype(jnp.bfloat16)
         twisted[rows, pl.ds(LANES, LANES)] = (real_part * sine_part + imag_part * cosine).astype(jnp.bfloat16)
-    row_index = lax.broadcasted_iota(jnp.int32, (RADIX, LANES), 0)
-    lane_index = lax.broadcasted_iota(jnp.int32, (RADIX, LANES), 1)
-    gates = row_index * LANES + lane_index
     tables[3].wait()
-    for pulse in range(pulse_count):
+    last_rows = RADIX - 8
+    gates = (
+        lax.broadcasted_iota(jnp.int32, (8, LANES), 0) + last_rows
+    ) * LANES + lax.broadcasted_iota(jnp.int32, (8, LANES), 1)
+    cosine, sine_part = near[0], near[1]
+    for first in range(0, pulse_count, 4):
         sums = lax.dot_general(
             dft[...],
-            twisted[pl.ds(pulse * RADIX, RADIX), :],
+            twisted[pl.ds(first * RADIX, 4 * RADIX), :],
             (((1,), (1,)), ((), ())),
             preferred_element_type=jnp.float32,
         )
-        inside = gates < SAMPLES - delays[pulse]
-        real_part, imag_part = sums[:RADIX], sums[RADIX:]
-        cosine, sine_part = near[0], near[1]
-        turned[pl.ds(pulse, RADIX, stride=pulse_count), :] = jnp.where(
-            inside, real_part * cosine - imag_part * sine_part, 0.0
-        )
-        turned[pl.ds(span + pulse, RADIX, stride=pulse_count), :] = jnp.where(
-            inside, real_part * sine_part + imag_part * cosine, 0.0
-        )
+        for pulse in range(first, first + 4):
+            own = sums[:, (pulse - first) * LANES : (pulse - first + 1) * LANES]
+            real_part, imag_part = own[:RADIX], own[RADIX:]
+            parts = (
+                real_part * cosine - imag_part * sine_part,
+                real_part * sine_part + imag_part * cosine,
+            )
+            inside = gates < SAMPLES - delays[pulse]
+            for part, values in enumerate(parts):
+                start = part * span + pulse
+                turned[pl.ds(start, last_rows, stride=pulse_count), :] = values[:last_rows]
+                turned[pl.ds(start + last_rows * pulse_count, 8, stride=pulse_count), :] = jnp.where(
+                    inside, values[last_rows:], 0.0
+                )
     block_rows = width // LANES * pulse_count
     for out, places in zip(outs, plan, strict=True):
         for index, apart in enumerate(places):
@@ -336,14 +346,14 @@
     two = swap(two, 2 * Z)
     one = swap(jnp.stack([one, mates[1]], axis=1), Z)
     three = swap(jnp.stack([three, mates[2]], axis=1), 3 * Z)
-    mates_two = swap(mates_two, 2 * Z)
+    two_away = swap(mates_two[1:], 2 * Z)
+    two_home = swap(mates_two[:1], 2 * Z)
     two = after(two, one)
     here = jnp.stack([here, mates[0]], axis=1)
-    two = jnp.stack([two, mates_two], axis=1)
     near = [0, CORE, Z, Z + CORE]
     groups = [
         ([here[0], one[0]], [here[1], one[1]], near),
-        ([two[0], three[0]], [two[1], three[1]], [FAR + i for i in near]),
+        ([two[:1], two_home, three[0]], [two[1:], two_away, three[1]], [FAR + i for i in near]),
     ]
     arrays, places = [], []
     for home, away, apart in groups:

time: 30 us -> 29.6 us (0.987)
  waiting for transfers between devices: 9.55 us -> 5.5 us
  starting transfers between devices: 15.5 us -> 19.4 us
    ppermute x8 -> x9, waiting for transfers between devices: 5.3 us -> 1.72 us  [swap(): return lax.ppermute(array, 'gate', [(i, i ^ apart) for i in range(count)])]
    ppermute x8 -> x9, starting transfers between devices: 11.3 us -> 13.5 us  [swap(): return lax.ppermute(array, 'gate', [(i, i ^ apart) for i in range(count)])]
    ppermute x4, starting transfers between devices: 4.27 us -> 5.88 us  [swap(): return lax.ppermute(array, ('sub', 'gate'), pairs)]
    ppermute x4, waiting for transfers between devices: 4.25 us -> 3.78 us  [swap(): return lax.ppermute(array, ('sub', 'gate'), pairs)]
  transfers between devices with their start and end apart: 12 -> 13, of which waited for: 3 -> 3; matrix products, arithmetic and copies ran while one was open for 1% -> 1% of each run, Pallas kernels for 2% -> 2%
where the time goes in v5:
time: 29.6 us; the launch traced here: 29.5 us
  starting transfers between devices  19.4 us (66%)
  waiting for transfers between devices  5.5 us (19%)
  Pallas kernels  4.27 us (14%)
    ppermute x9, starting transfers between devices, swap(): return lax.ppermute(array, 'gate', [(i, i ^ apart) for i in range(count)])  13.5 us
    ppermute x4, starting transfers between devices, swap(): return lax.ppermute(array, ('sub', 'gate'), pairs)  5.88 us
    ppermute x4, waiting for transfers between devices, swap(): return lax.ppermute(array, ('sub', 'gate'), pairs)  3.78 us
    pallas_call x1, Pallas kernels, range_compress(): pl.pallas_call(functools.partial(compress_kernel, plan), out_shape=[pltpu...  2.46 us
    pallas_call x2, Pallas kernels, form_image(): pl.pallas_call(functools.partial(image_kernel, [plan[i] for i in used], f...  1.81 us
    ppermute x9, waiting for transfers between devices, swap(): return lax.ppermute(array, 'gate', [(i, i ^ apart) for i in range(count)])  1.72 us
  transfers between devices with their start and end apart: 13, of which 3 were waited for; matrix products, arithmetic and copies ran while one was open for 1% of the time, Pallas kernels for 2%

profile of v5, /device:TPU:0, one launch (start us, length us, event | category | flops | bytes accessed | tf_op | source)
XLA Modules:
  0.0 29.5 jit_solution(6069383036790943421)
XLA Ops:
  0.0 0.0 copy-start
  0.0 2.5 %compress.1 = (bf16[2,16,1024]{2,1,0:T(8,128)(2,1)S(1)}, bf16[2,16,1024]{2,1,0:T(8,128)(2,1)S(1)}, bf16[2,16,1024]{2,1,0:T(8,128)(2,1)S(1)}, bf16[2,16,1024]{2,1...) custom-call(s32[8]{0:T(128)} %delays_far.1, bf16[2,8,16384]{2,1,0:T(8,128)(2,1)} %raw_far.1, ...), custom_call_target="tpu_custom_call" | custom-call | tf_op jit(solution)/shard_map/compress/pallas_call | solution.py:205
  2.5 0.5 %collective-permute-start.1 = (bf16[6,16,1024]{2,1,0:T(8,128)(2,1)S(1)}, bf16[6,16,1024]{2,1,0:T(8,128)(2,1)S(1)}, u32[]{:S(2)}, u32[]{:S(2)}) collective-permute-start(bf16[6,16,1024]{2,1,0:T(8,128)(2,1)S(1)} %get-tuple-element.15), channel_id=1, source_target_pairs={{0,1},{1,0},{2,3},{3,2},{4,5},{5,4},{6,7},{7,6},{8,9},{9,8},{10,11... | collective-permute-start | bytes 589832 | tf_op jit(solution)/shard_map/ppermute | solution.py:325
  3.0 3.7 %collective-permute-start = (bf16[2,16,1024]{2,1,0:T(8,128)(2,1)S(1)}, bf16[2,16,1024]{2,1,0:T(8,128)(2,1)S(1)}, u32[]{:S(2)}, u32[]{:S(2)}) collective-permute-start(bf16[2,16,1024]{2,1,0:T(8,128)(2,1)S(1)} %get-tuple-element.13), channel_id=1, source_target_pairs={{0,8},{1,9},{2,10},{3,11},{4,12},{5,13},{6,14},{7,15},{8,0},{9,1},... | collective-permute-start | bytes 196616 | tf_op jit(solution)/shard_map/ppermute | solution.py:325
  6.6 0.0 collective-permute-done.1
  6.6 0.2 collective-permute-start.3
  6.9 1.6 %collective-permute-start.2 = (bf16[2,2,16,1024]{3,2,1,0:T(8,128)(2,1)S(1)}, bf16[2,2,16,1024]{3,2,1,0:T(8,128)(2,1)S(1)}, u32[]{:S(2)}, u32[]{:S(2)}) collective-permute-start(bf16[2,2,16,1024]{3,2,1,0:T(8,128)(2,1)S(1)} %pad_maximum_fusion), channel_id=1, source_target_pairs={{0,4},{1,5},{2,6},{3,7},{4,0},{5,1},{6,2},{7,3},{8,12},{9,13},{10,... | collective-permute-start | bytes 393224 | tf_op jit(solution)/shard_map/ppermute | solution.py:325
  8.5 1.3 %collective-permute-start.5 = (bf16[2,2,16,1024]{3,2,1,0:T(8,128)(2,1)S(1)}, bf16[2,2,16,1024]{3,2,1,0:T(8,128)(2,1)S(1)}, u32[]{:S(2)}, u32[]{:S(2)}) collective-permute-start(bf16[2,2,16,1024]{3,2,1,0:T(8,128)(2,1)S(1)} %pad_maximum_fusion.1), channel_id=1, source_target_pairs={{0,12},{1,13},{2,14},{3,15},{4,8},{5,9},{6,10},{7,11},{8,4},{9,5},... | collective-permute-start | bytes 393224 | tf_op jit(solution)/shard_map/ppermute | solution.py:325
  9.8 0.0 collective-permute-done.3
  9.9 0.7 %collective-permute-start.6 = (bf16[1,16,1024]{2,1,0:T(8,128)(2,1)S(1)}, bf16[1,16,1024]{2,1,0:T(8,128)(2,1)S(1)}, u32[]{:S(2)}, u32[]{:S(2)}) collective-permute-start(bf16[1,16,1024]{2,1,0:T(8,128)(2,1)S(1)} %get-tuple-element.32), channel_id=1, source_target_pairs={{0,8},{1,9},{2,10},{3,11},{4,12},{5,13},{6,14},{7,15},{8,0},{9,1},... | collective-permute-start | bytes 98312 | tf_op jit(solution)/shard_map/ppermute | solution.py:325
  10.6 2.2 %collective-permute-start.4 = (bf16[1,16,1024]{2,1,0:T(8,128)(2,1)S(1)}, bf16[1,16,1024]{2,1,0:T(8,128)(2,1)S(1)}, u32[]{:S(2)}, u32[]{:S(2)}) collective-permute-start(bf16[1,16,1024]{2,1,0:T(8,128)(2,1)S(1)} %get-tuple-element.33), channel_id=1, source_target_pairs={{0,8},{1,9},{2,10},{3,11},{4,12},{5,13},{6,14},{7,15},{8,0},{9,1},... | collective-permute-start | bytes 98312 | tf_op jit(solution)/shard_map/ppermute | solution.py:325
  12.8 0.0 collective-permute-done.2
  12.9 1.6 %collective-permute-start.12 = (bf16[4,16,1024]{2,1,0:T(8,128)(2,1)S(1)}, bf16[4,16,1024]{2,1,0:T(8,128)(2,1)S(1)}, u32[]{:S(2)}, u32[]{:S(2)}) collective-permute-start(bf16[4,16,1024]{2,1,0:T(8,128)(2,1)S(1)} %pad_maximum_fusion.5), channel_id=1, source_target_pairs={{0,2},{1,3},{2,0},{3,1},{4,6},{5,7},{6,4},{7,5},{8,10},{9,11},{10,... | collective-permute-start | bytes 393224 | tf_op jit(solution)/shard_map/ppermute | solution.py:325
  14.6 0.0 collective-permute-done
  14.6 1.4 %collective-permute-start.10 = (bf16[4,16,1024]{2,1,0:T(8,128)(2,1)S(1)}, bf16[4,16,1024]{2,1,0:T(8,128)(2,1)S(1)}, u32[]{:S(2)}, u32[]{:S(2)}) collective-permute-start(bf16[4,16,1024]{2,1,0:T(8,128)(2,1)S(1)} %pad_maximum_fusion.5), channel_id=1, source_target_pairs={{0,18},{1,19},{2,16},{3,17},{4,22},{5,23},{6,20},{7,21},{8,26},{9,... | collective-permute-start | bytes 393224 | tf_op jit(solution)/shard_map/ppermute | solution.py:327
  16.0 0.8 %collective-permute-done.5 = bf16[2,2,16,1024]{3,2,1,0:T(8,128)(2,1)S(1)} collective-permute-done((bf16[2,2,16,1024]{3,2,1,0:T(8,128)(2,1)S(1)}, bf16[2,2,16,1024]{3,2,1,0:T(8,128)(2,1)S(1)}, u32[]{:S(2)}, u32[]{:S(2)}) %collective-permute-start.5) | collective-permute-done | bytes 131104 | tf_op jit(solution)/shard_map/ppermute | solution.py:325
  16.8 1.5 %collective-permute-start.11 = (bf16[4,16,1024]{2,1,0:T(8,128)(2,1)S(1)}, bf16[4,16,1024]{2,1,0:T(8,128)(2,1)S(1)}, u32[]{:S(2)}, u32[]{:S(2)}) collective-permute-start(bf16[4,16,1024]{2,1,0:T(8,128)(2,1)S(1)} %pad_maximum_fusion.4.refs_0_), channel_id=1, source_target_pairs={{0,16},{1,17},{2,18},{3,19},{4,20},{5,21},{6,22},{7,23},{8,24},{9,... | collective-permute-start | bytes 393224 | tf_op jit(solution)/shard_map/ppermute | solution.py:327
  18.3 0.9 %collective-permute-done.6 = bf16[1,16,1024]{2,1,0:T(8,128)(2,1)S(1)} collective-permute-done((bf16[1,16,1024]{2,1,0:T(8,128)(2,1)S(1)}, bf16[1,16,1024]{2,1,0:T(8,128)(2,1)S(1)}, u32[]{:S(2)}, u32[]{:S(2)}) %collective-permute-start.6) | collective-permute-done | bytes 32800 | tf_op jit(solution)/shard_map/ppermute | solution.py:325
  19.2 1.6 %collective-permute-start.9 = (bf16[4,16,1024]{2,1,0:T(8,128)(2,1)S(1)}, bf16[4,16,1024]{2,1,0:T(8,128)(2,1)S(1)}, u32[]{:S(2)}, u32[]{:S(2)}) collective-permute-start(bf16[4,16,1024]{2,1,0:T(8,128)(2,1)S(1)} %pad_maximum_fusion.3), channel_id=1, source_target_pairs={{0,2},{1,3},{2,0},{3,1},{4,6},{5,7},{6,4},{7,5},{8,10},{9,11},{10,... | collective-permute-start | bytes 393224 | tf_op jit(solution)/shard_map/ppermute | solution.py:325
  20.8 0.0 collective-permute-done.4
  20.8 1.4 %collective-permute-start.7 = (bf16[4,16,1024]{2,1,0:T(8,128)(2,1)S(1)}, bf16[4,16,1024]{2,1,0:T(8,128)(2,1)S(1)}, u32[]{:S(2)}, u32[]{:S(2)}) collective-permute-start(bf16[4,16,1024]{2,1,0:T(8,128)(2,1)S(1)} %pad_maximum_fusion.3), channel_id=1, source_target_pairs={{0,18},{1,19},{2,16},{3,17},{4,22},{5,23},{6,20},{7,21},{8,26},{9,... | collective-permute-start | bytes 393224 | tf_op jit(solution)/shard_map/ppermute | solution.py:327
  22.3 0.0 collective-permute-done.11.refs_2_
  22.3 1.5 %collective-permute-start.8 = (bf16[4,16,1024]{2,1,0:T(8,128)(2,1)S(1)}, bf16[4,16,1024]{2,1,0:T(8,128)(2,1)S(1)}, u32[]{:S(2)}, u32[]{:S(2)}) collective-permute-start(bf16[4,16,1024]{2,1,0:T(8,128)(2,1)S(1)} %pad_maximum_fusion.2.refs_0_), channel_id=1, source_target_pairs={{0,16},{1,17},{2,18},{3,19},{4,20},{5,21},{6,22},{7,23},{8,24},{9,... | collective-permute-start | bytes 393224 | tf_op jit(solution)/shard_map/ppermute | solution.py:327
  23.8 0.0 copy-done
  23.8 0.0 collective-permute-done.12.refs_3_
  23.8 0.0 collective-permute-done.10.refs_1_
  23.9 0.5 %image.2.refs_4_ = f32[512,1024]{1,0:T(8,128)S(1)} custom-call(bf16[512,512]{1,0:T(8,128)(2,1)S(1)} %dynamic-slice_bitcast_fusion.table, bf16[4,16,1024]{2,1,0:T(8,128)(2,1)S(1)} %pad_maximum_fusion.4.refs_0_, bf16[4,16,1024]{2,1,0:T(8,128)(2,1)S(1)} %collective-permute-done.10.refs_1_, bf16[4,16,1024]{2,1,0:T(8,128)(2,1)S(1)} %collective-permute-done.11.refs_2_, ...), custom_call_target="tpu_custom_call" | custom-call | flops 268435456 | bytes 2097152 | tf_op jit(solution)/shard_map/image/pallas_call | solution.py:271
  24.4 3.8 %collective-permute-done.8.refs_2_ = bf16[4,16,1024]{2,1,0:T(8,128)(2,1)S(1)} collective-permute-done((bf16[4,16,1024]{2,1,0:T(8,128)(2,1)S(1)}, bf16[4,16,1024]{2,1,0:T(8,128)(2,1)S(1)}, u32[]{:S(2)}, u32[]{:S(2)}) %collective-permute-start.8) | collective-permute-done | bytes 131104 | tf_op jit(solution)/shard_map/ppermute | solution.py:327
  28.1 0.0 collective-permute-done.9.refs_3_
  28.1 0.0 collective-permute-done.7.refs_1_
  28.1 1.3 %image.3 = bf16[512,1024]{1,0:T(8,128)(2,1)} custom-call(bf16[512,512]{1,0:T(8,128)(2,1)S(1)} %dynamic-slice_bitcast_fusion.table, bf16[4,16,1024]{2,1,0:T(8,128)(2,1)S(1)} %pad_maximum_fusion.2.refs_0_, bf16[4,16,1024]{2,1,0:T(8,128)(2,1)S(1)} %collective-permute-done.7.refs_1_, bf16[4,16,1024]{2,1,0:T(8,128)(2,1)S(1)} %collective-permute-done.8.refs_2_, ...), custom_call_target="tpu_custom_call" | custom-call | flops 268435456 | bytes 2097152 | tf_op jit(solution)/shard_map/image/pallas_call | solution.py:271
  (13 shorter events, 0.2 us)
Async XLA Ops:
  0.0 23.8 %copy-start = (bf16[2,512,512]{2,1,0:T(8,128)(2,1)S(1)}, bf16[2,512,512]{2,1,0:T(8,128)(2,1)}, u32[]{:S(2)}) copy-start(bf16[2,512,512]{2,1,0:T(8,128)(2,1)} %constant.23.clone) | copy-start | bytes 3145732
  2.5 4.2 %collective-permute-start.1 = (bf16[6,16,1024]{2,1,0:T(8,128)(2,1)S(1)}, bf16[6,16,1024]{2,1,0:T(8,128)(2,1)S(1)}, u32[]{:S(2)}, u32[]{:S(2)}) collective-permute-start(bf16[6,16,1024]{2,1,0:T(8,128)(2,1)S(1)} %get-tuple-element.15), channel_id=1, source_target_pairs={{0,1},{1,0},{2,3},{3,2},{4,5},{5,4},{6,7},{7,6},{8,9},{9,8},{10,11... | collective-permute-start | bytes 589832 | tf_op jit(solution)/shard_map/ppermute | solution.py:325
  3.0 11.6 %collective-permute-start = (bf16[2,16,1024]{2,1,0:T(8,128)(2,1)S(1)}, bf16[2,16,1024]{2,1,0:T(8,128)(2,1)S(1)}, u32[]{:S(2)}, u32[]{:S(2)}) collective-permute-start(bf16[2,16,1024]{2,1,0:T(8,128)(2,1)S(1)} %get-tuple-element.13), channel_id=1, source_target_pairs={{0,8},{1,9},{2,10},{3,11},{4,12},{5,13},{6,14},{7,15},{8,0},{9,1},... | collective-permute-start | bytes 196616 | tf_op jit(solution)/shard_map/ppermute | solution.py:325
  6.6 3.2 %collective-permute-start.3 = (bf16[2,16,1024]{2,1,0:T(8,128)(2,1)S(1)}, bf16[2,16,1024]{2,1,0:T(8,128)(2,1)S(1)}, u32[]{:S(2)}, u32[]{:S(2)}) collective-permute-start(bf16[2,16,1024]{2,1,0:T(8,128)(2,1)S(1)} %get-tuple-element.18), channel_id=1, source_target_pairs={{0,1},{1,0},{2,3},{3,2},{4,5},{5,4},{6,7},{7,6},{8,9},{9,8},{10,11... | collective-permute-start | bytes 196616 | tf_op jit(solution)/shard_map/ppermute | solution.py:325
  6.9 6.0 %collective-permute-start.2 = (bf16[2,2,16,1024]{3,2,1,0:T(8,128)(2,1)S(1)}, bf16[2,2,16,1024]{3,2,1,0:T(8,128)(2,1)S(1)}, u32[]{:S(2)}, u32[]{:S(2)}) collective-permute-start(bf16[2,2,16,1024]{3,2,1,0:T(8,128)(2,1)S(1)} %pad_maximum_fusion), channel_id=1, source_target_pairs={{0,4},{1,5},{2,6},{3,7},{4,0},{5,1},{6,2},{7,3},{8,12},{9,13},{10,... | collective-permute-start | bytes 393224 | tf_op jit(solution)/shard_map/ppermute | solution.py:325
  8.5 8.3 %collective-permute-start.5 = (bf16[2,2,16,1024]{3,2,1,0:T(8,128)(2,1)S(1)}, bf16[2,2,16,1024]{3,2,1,0:T(8,128)(2,1)S(1)}, u32[]{:S(2)}, u32[]{:S(2)}) collective-permute-start(bf16[2,2,16,1024]{3,2,1,0:T(8,128)(2,1)S(1)} %pad_maximum_fusion.1), channel_id=1, source_target_pairs={{0,12},{1,13},{2,14},{3,15},{4,8},{5,9},{6,10},{7,11},{8,4},{9,5},... | collective-permute-start | bytes 393224 | tf_op jit(solution)/shard_map/ppermute | solution.py:325
  9.9 9.3 %collective-permute-start.6 = (bf16[1,16,1024]{2,1,0:T(8,128)(2,1)S(1)}, bf16[1,16,1024]{2,1,0:T(8,128)(2,1)S(1)}, u32[]{:S(2)}, u32[]{:S(2)}) collective-permute-start(bf16[1,16,1024]{2,1,0:T(8,128)(2,1)S(1)} %get-tuple-element.32), channel_id=1, source_target_pairs={{0,8},{1,9},{2,10},{3,11},{4,12},{5,13},{6,14},{7,15},{8,0},{9,1},... | collective-permute-start | bytes 98312 | tf_op jit(solution)/shard_map/ppermute | solution.py:325
  10.6 10.2 %collective-permute-start.4 = (bf16[1,16,1024]{2,1,0:T(8,128)(2,1)S(1)}, bf16[1,16,1024]{2,1,0:T(8,128)(2,1)S(1)}, u32[]{:S(2)}, u32[]{:S(2)}) collective-permute-start(bf16[1,16,1024]{2,1,0:T(8,128)(2,1)S(1)} %get-tuple-element.33), channel_id=1, source_target_pairs={{0,8},{1,9},{2,10},{3,11},{4,12},{5,13},{6,14},{7,15},{8,0},{9,1},... | collective-permute-start | bytes 98312 | tf_op jit(solution)/shard_map/ppermute | solution.py:325
  12.9 10.9 %collective-permute-start.12 = (bf16[4,16,1024]{2,1,0:T(8,128)(2,1)S(1)}, bf16[4,16,1024]{2,1,0:T(8,128)(2,1)S(1)}, u32[]{:S(2)}, u32[]{:S(2)}) collective-permute-start(bf16[4,16,1024]{2,1,0:T(8,128)(2,1)S(1)} %pad_maximum_fusion.5), channel_id=1, source_target_pairs={{0,2},{1,3},{2,0},{3,1},{4,6},{5,7},{6,4},{7,5},{8,10},{9,11},{10,... | collective-permute-start | bytes 393224 | tf_op jit(solution)/shard_map/ppermute | solution.py:325
  14.6 9.3 %collective-permute-start.10 = (bf16[4,16,1024]{2,1,0:T(8,128)(2,1)S(1)}, bf16[4,16,1024]{2,1,0:T(8,128)(2,1)S(1)}, u32[]{:S(2)}, u32[]{:S(2)}) collective-permute-start(bf16[4,16,1024]{2,1,0:T(8,128)(2,1)S(1)} %pad_maximum_fusion.5), channel_id=1, source_target_pairs={{0,18},{1,19},{2,16},{3,17},{4,22},{5,23},{6,20},{7,21},{8,26},{9,... | collective-permute-start | bytes 393224 | tf_op jit(solution)/shard_map/ppermute | solution.py:327
  16.8 5.4 %collective-permute-start.11 = (bf16[4,16,1024]{2,1,0:T(8,128)(2,1)S(1)}, bf16[4,16,1024]{2,1,0:T(8,128)(2,1)S(1)}, u32[]{:S(2)}, u32[]{:S(2)}) collective-permute-start(bf16[4,16,1024]{2,1,0:T(8,128)(2,1)S(1)} %pad_maximum_fusion.4.refs_0_), channel_id=1, source_target_pairs={{0,16},{1,17},{2,18},{3,19},{4,20},{5,21},{6,22},{7,23},{8,24},{9,... | collective-permute-start | bytes 393224 | tf_op jit(solution)/shard_map/ppermute | solution.py:327
  19.2 8.9 %collective-permute-start.9 = (bf16[4,16,1024]{2,1,0:T(8,128)(2,1)S(1)}, bf16[4,16,1024]{2,1,0:T(8,128)(2,1)S(1)}, u32[]{:S(2)}, u32[]{:S(2)}) collective-permute-start(bf16[4,16,1024]{2,1,0:T(8,128)(2,1)S(1)} %pad_maximum_fusion.3), channel_id=1, source_target_pairs={{0,2},{1,3},{2,0},{3,1},{4,6},{5,7},{6,4},{7,5},{8,10},{9,11},{10,... | collective-permute-start | bytes 393224 | tf_op jit(solution)/shard_map/ppermute | solution.py:325
  20.8 7.3 %collective-permute-start.7 = (bf16[4,16,1024]{2,1,0:T(8,128)(2,1)S(1)}, bf16[4,16,1024]{2,1,0:T(8,128)(2,1)S(1)}, u32[]{:S(2)}, u32[]{:S(2)}) collective-permute-start(bf16[4,16,1024]{2,1,0:T(8,128)(2,1)S(1)} %pad_maximum_fusion.3), channel_id=1, source_target_pairs={{0,18},{1,19},{2,16},{3,17},{4,22},{5,23},{6,20},{7,21},{8,26},{9,... | collective-permute-start | bytes 393224 | tf_op jit(solution)/shard_map/ppermute | solution.py:327
  22.3 5.9 %collective-permute-start.8 = (bf16[4,16,1024]{2,1,0:T(8,128)(2,1)S(1)}, bf16[4,16,1024]{2,1,0:T(8,128)(2,1)S(1)}, u32[]{:S(2)}, u32[]{:S(2)}) collective-permute-start(bf16[4,16,1024]{2,1,0:T(8,128)(2,1)S(1)} %pad_maximum_fusion.2.refs_0_), channel_id=1, source_target_pairs={{0,16},{1,17},{2,18},{3,19},{4,20},{5,21},{6,22},{7,23},{8,24},{9,... | collective-permute-start | bytes 393224 | tf_op jit(solution)/shard_map/ppermute | solution.py:327

commit v6 on v5

--- a/solution.py
+++ b/solution.py
@@ -237,14 +237,17 @@
     block = arrays[0].shape[1]
     me = lax.axis_index("gate")
     lower = (me ^ far) // FAR * half
-    for array, (side, places) in zip(arrays, plan, strict=True):
+    core = me % 2
+    for array, ((side, along), (side_odd, along_odd), places) in zip(arrays, plan, strict=True):
+        side = side + core * (side_odd - side)
+        along = along + core * (along_odd - along)
         for index, apart in enumerate(places):
             if apart // FAR * FAR == far:
-                start = side * half + (me ^ apart) * block - lower
+                start = side * half + (me ^ (apart + along)) * block - lower
                 data[pl.ds(pl.multiple_of(start, block), block), :] = array[index]
     for side in range(2):
         source = pl.multiple_of(side * 2 * half + lower, half)
-        columns[:, pl.ds(side * half, half)] = table[:, pl.ds(source, half)]
+        columns[:, pl.ds(side * half, half)] = table[lax.axis_index("sub"), :, pl.ds(source, half)]
     tile = 256
     copies = []
     for row in range(0, out.shape[0], tile):
@@ -261,13 +264,13 @@
         copy.wait()
 
 
-def form_image(table, arrays, plan):
-    rows, depth = table.shape[0], table.shape[1] // 2
+def form_image(tables, arrays, plan):
+    rows, depth = tables.shape[1], tables.shape[2] // 2
     shape = rows, arrays[0].shape[-1]
     vmem = pl.BlockSpec(memory_space=pltpu.VMEM)
     total = []
     for far in (0, FAR):
-        used = [i for i, (_, places) in enumerate(plan) if any(apart // FAR * FAR == far for apart in places)]
+        used = [i for i, (*_, places) in enumerate(plan) if any(apart // FAR * FAR == far for apart in places)]
         image = pl.pallas_call(
             functools.partial(image_kernel, [plan[i] for i in used], far, bool(total)),
             out_shape=jax.ShapeDtypeStruct(shape, jnp.bfloat16) if far else pltpu.VMEM(shape, jnp.float32),
@@ -280,7 +283,7 @@
             ),
             compiler_params=pltpu.CompilerParams(vmem_limit_bytes=32 * 2**20),
             name="image",
-        )(table, *[arrays[i] for i in used], *total)
+        )(tables, *[arrays[i] for i in used], *total)
         total = [image]
     return image.reshape(2, ANGLES, shape[1])
 
@@ -319,11 +322,9 @@
     return current
 
 
-def swap(array, apart, other_sub=False):
-    count = lax.axis_size("gate")
-    if not other_sub:
-        return lax.ppermute(array, "gate", [(i, i ^ apart) for i in range(count)])
-    pairs = [(i, i ^ (count + apart)) for i in range(2 * count)]
+def swap(array, even, odd=None):
+    count = 2 * lax.axis_size("gate")
+    pairs = [(i, i ^ (even if odd is None or i % 2 == 0 else odd)) for i in range(count)]
     return lax.ppermute(array, ("sub", "gate"), pairs)
 
 
@@ -332,6 +333,9 @@
 
 def after(array, other):
     return lax.optimization_barrier((array, other))[0]
+
+
+EXCHANGES = [((1, 0), (0, Y)), ((1, Y), (1, 0)), ((0, Y), (1, Y))]
 
 
 def corner_turn(send):
@@ -346,21 +350,25 @@
     two = swap(two, 2 * Z)
     one = swap(jnp.stack([one, mates[1]], axis=1), Z)
     three = swap(jnp.stack([three, mates[2]], axis=1), 3 * Z)
-    two_away = swap(mates_two[1:], 2 * Z)
-    two_home = swap(mates_two[:1], 2 * Z)
+    mates_two = swap(mates_two, 2 * Z)
     two = after(two, one)
     here = jnp.stack([here, mates[0]], axis=1)
-    near = [0, CORE, Z, Z + CORE]
     groups = [
-        ([here[0], one[0]], [here[1], one[1]], near),
-        ([two[:1], two_home, three[0]], [two[1:], two_away, three[1]], [FAR + i for i in near]),
+        ([here[0], one[0], two[:1]], [here[1], one[1], two[1:]], [0, CORE, Z, Z + CORE, FAR]),
+        ([mates_two[:1], three[0]], [mates_two[1:], three[1]], [FAR + CORE, FAR + Z, FAR + Z + CORE]),
     ]
+    first_core = lax.axis_index("gate") % 2 == 0
+    across = lax.axis_size("gate")
     arrays, places = [], []
     for home, away, apart in groups:
         home, away = jnp.concatenate(home), jnp.concatenate(away)
-        apart_y = [i + Y for i in apart]
-        arrays += [home, swap(away, Y, True), swap(home, 0, True), swap(away, Y)]
-        places += [(0, apart), (1, apart_y), (1, apart), (0, apart_y)]
+        arrays.append(home)
+        places.append(((0, 0), (0, 0), apart))
+        for even, odd in EXCHANGES:
+            blocks = [away if along else home for _, along in (even, odd)]
+            sent = away if even[1] and odd[1] else jnp.where(first_core, *blocks)
+            arrays.append(swap(sent, *(side * across + along for side, along in (even, odd))))
+            places.append((even, odd, apart))
     return arrays, places
 
 
@@ -379,9 +387,7 @@
         received = received.reshape(2 * sub_pulses, SAMPLES // gate_count)
         return merge_levels(received, pulse_count, sub_pulses, depth_count)
     arrays, places = corner_turn(send)
-    tables = jnp.asarray(image_tables(sub_pulses, pulse_count))
-    table = lax.dynamic_index_in_dim(tables, lax.axis_index("sub"), 0, keepdims=False)
-    return form_image(table, arrays, places)
+    return form_image(image_tables(sub_pulses, pulse_count), arrays, places)
 
 
 def solution(mesh):

time: 29.6 us -> 29.2 us (0.986)
  starting transfers between devices: 19.4 us -> 15.1 us
  waiting for transfers between devices: 5.5 us -> 9.37 us
    ppermute x9 -> x0, starting transfers between devices: 13.5 us -> none  [swap(): return lax.ppermute(array, 'gate', [(i, i ^ apart) for i in range(count)])]
    ppermute x4 -> x12, starting transfers between devices: 5.88 us -> 15.1 us  [swap(): return lax.ppermute(array, ('sub', 'gate'), pairs)]
    ppermute x4 -> x12, waiting for transfers between devices: 3.78 us -> 9.37 us  [swap(): return lax.ppermute(array, ('sub', 'gate'), pairs)]
    ppermute x9 -> x0, waiting for transfers between devices: 1.72 us -> none  [swap(): return lax.ppermute(array, 'gate', [(i, i ^ apart) for i in range(count)])]
  transfers between devices with their start and end apart: 13 -> 12, of which waited for: 3 -> 9; matrix products, arithmetic and copies ran while one was open for 1% -> 1% of each run, Pallas kernels for 2% -> 2%
where the time goes in v6:
time: 29.2 us; the launch traced here: 29 us
  starting transfers between devices  15.1 us (52%)
  waiting for transfers between devices  9.37 us (32%)
  Pallas kernels  4.27 us (15%)
    ppermute x12, starting transfers between devices, swap(): return lax.ppermute(array, ('sub', 'gate'), pairs)  15.1 us
    ppermute x12, waiting for transfers between devices, swap(): return lax.ppermute(array, ('sub', 'gate'), pairs)  9.37 us
    pallas_call x1, Pallas kernels, range_compress(): pl.pallas_call(functools.partial(compress_kernel, plan), out_shape=[pltpu...  2.46 us
    pallas_call x2, Pallas kernels, form_image(): pl.pallas_call(functools.partial(image_kernel, [plan[i] for i in used], f...  1.81 us
  transfers between devices with their start and end apart: 12, of which 9 were waited for; matrix products, arithmetic and copies ran while one was open for 1% of the time, Pallas kernels for 2%

profile of v6, /device:TPU:0, one launch (start us, length us, event | category | flops | bytes accessed | tf_op | source)
XLA Modules:
  0.0 29.0 jit_solution(30871655102904082)
XLA Ops:
  0.0 0.0 copy-start
  0.0 2.5 %compress.1 = (bf16[2,16,1024]{2,1,0:T(8,128)(2,1)S(1)}, bf16[2,16,1024]{2,1,0:T(8,128)(2,1)S(1)}, bf16[2,16,1024]{2,1,0:T(8,128)(2,1)S(1)}, bf16[2,16,1024]{2,1...) custom-call(s32[8]{0:T(128)} %delays_far.1, bf16[2,8,16384]{2,1,0:T(8,128)(2,1)} %raw_far.1, ...), custom_call_target="tpu_custom_call" | custom-call | tf_op jit(solution)/shard_map/compress/pallas_call | solution.py:205
  2.5 0.5 %collective-permute-start = (bf16[6,16,1024]{2,1,0:T(8,128)(2,1)S(1)}, bf16[6,16,1024]{2,1,0:T(8,128)(2,1)S(1)}, u32[]{:S(2)}, u32[]{:S(2)}) collective-permute-start(bf16[6,16,1024]{2,1,0:T(8,128)(2,1)S(1)} %get-tuple-element.14), channel_id=1, source_target_pairs={{0,1},{1,0},{2,3},{3,2},{4,5},{5,4},{6,7},{7,6},{8,9},{9,8},{10,11... | collective-permute-start | bytes 589832 | tf_op jit(solution)/shard_map/ppermute | solution.py:328
  3.0 3.7 %collective-permute-start.2 = (bf16[2,16,1024]{2,1,0:T(8,128)(2,1)S(1)}, bf16[2,16,1024]{2,1,0:T(8,128)(2,1)S(1)}, u32[]{:S(2)}, u32[]{:S(2)}) collective-permute-start(bf16[2,16,1024]{2,1,0:T(8,128)(2,1)S(1)} %get-tuple-element.16), channel_id=1, source_target_pairs={{0,8},{1,9},{2,10},{3,11},{4,12},{5,13},{6,14},{7,15},{8,0},{9,1},... | collective-permute-start | bytes 196616 | tf_op jit(solution)/shard_map/ppermute | solution.py:328
  6.6 0.0 collective-permute-done
  6.6 0.2 collective-permute-start.6
  6.9 1.6 %collective-permute-start.1 = (bf16[2,2,16,1024]{3,2,0,1:T(8,128)(2,1)S(1)}, bf16[2,2,16,1024]{3,2,0,1:T(8,128)(2,1)S(1)}, u32[]{:S(2)}, u32[]{:S(2)}) collective-permute-start(bf16[2,2,16,1024]{3,2,0,1:T(8,128)(2,1)S(1)} %pad_maximum_fusion.2), channel_id=1, source_target_pairs={{0,4},{1,5},{2,6},{3,7},{4,0},{5,1},{6,2},{7,3},{8,12},{9,13},{10,... | collective-permute-start | bytes 393224 | tf_op jit(solution)/shard_map/ppermute | solution.py:328
  8.5 1.3 %collective-permute-start.8 = (bf16[2,2,16,1024]{3,2,1,0:T(8,128)(2,1)S(1)}, bf16[2,2,16,1024]{3,2,1,0:T(8,128)(2,1)S(1)}, u32[]{:S(2)}, u32[]{:S(2)}) collective-permute-start(bf16[2,2,16,1024]{3,2,1,0:T(8,128)(2,1)S(1)} %pad_maximum_fusion.3), channel_id=1, source_target_pairs={{0,12},{1,13},{2,14},{3,15},{4,8},{5,9},{6,10},{7,11},{8,4},{9,5},... | collective-permute-start | bytes 393224 | tf_op jit(solution)/shard_map/ppermute | solution.py:328
  9.8 0.0 collective-permute-done.6
  9.8 0.7 %collective-permute-start.7 = (bf16[2,16,1024]{2,1,0:T(8,128)(2,1)S(1)}, bf16[2,16,1024]{2,1,0:T(8,128)(2,1)S(1)}, u32[]{:S(2)}, u32[]{:S(2)}) collective-permute-start(bf16[2,16,1024]{2,1,0:T(8,128)(2,1)S(1)} %collective-permute-done.6), channel_id=1, source_target_pairs={{0,8},{1,9},{2,10},{3,11},{4,12},{5,13},{6,14},{7,15},{8,0},{9,1},... | collective-permute-start | bytes 196616 | tf_op jit(solution)/shard_map/ppermute | solution.py:328
  10.6 0.3 collective-permute-done.2
  10.8 2.1 %collective-permute-done.1 = bf16[2,2,16,1024]{3,2,0,1:T(8,128)(2,1)S(1)} collective-permute-done((bf16[2,2,16,1024]{3,2,0,1:T(8,128)(2,1)S(1)}, bf16[2,2,16,1024]{3,2,0,1:T(8,128)(2,1)S(1)}, u32[]{:S(2)}, u32[]{:S(2)}) %collective-permute-start.1) | collective-permute-done | bytes 131104 | tf_op jit(solution)/shard_map/ppermute | solution.py:328
  12.9 0.1 broadcast_select_fusion
  13.0 2.6 %collective-permute-start.4 = (bf16[5,16,1024]{2,1,0:T(8,128)(2,1)S(1)}, bf16[5,16,1024]{2,1,0:T(8,128)(2,1)S(1)}, u32[]{:S(2)}, u32[]{:S(2)}) collective-permute-start(bf16[5,16,1024]{2,1,0:T(8,128)(2,1)S(1)} %get-tuple-element.21), channel_id=1, source_target_pairs={{0,18},{1,17},{2,16},{3,19},{4,22},{5,21},{6,20},{7,23},{8,26},{9,... | collective-permute-start | bytes 491528 | tf_op jit(solution)/shard_map/ppermute | solution.py:328
  15.6 0.5 %collective-permute-start.3 = (bf16[5,16,1024]{2,1,0:T(8,128)(2,1)S(1)}, bf16[5,16,1024]{2,1,0:T(8,128)(2,1)S(1)}, u32[]{:S(2)}, u32[]{:S(2)}) collective-permute-start(bf16[5,16,1024]{2,1,0:T(8,128)(2,1)S(1)} %get-tuple-element.22), channel_id=1, source_target_pairs={{0,16},{1,3},{2,18},{3,1},{4,20},{5,7},{6,22},{7,5},{8,24},{9,11},... | collective-permute-start | bytes 491528 | tf_op jit(solution)/shard_map/ppermute | solution.py:328
  16.1 0.4 %collective-permute-start.5 = (bf16[5,16,1024]{2,1,0:T(8,128)(2,1)S(1)}, bf16[5,16,1024]{2,1,0:T(8,128)(2,1)S(1)}, u32[]{:S(2)}, u32[]{:S(2)}) collective-permute-start(bf16[5,16,1024]{2,1,0:T(8,128)(2,1)S(1)} %get-tuple-element.28), channel_id=1, source_target_pairs={{0,2},{1,19},{2,0},{3,17},{4,6},{5,23},{6,4},{7,21},{8,10},{9,27},... | collective-permute-start | bytes 491528 | tf_op jit(solution)/shard_map/ppermute | solution.py:328
  16.5 0.3 %collective-permute-done.8 = bf16[2,2,16,1024]{3,2,1,0:T(8,128)(2,1)S(1)} collective-permute-done((bf16[2,2,16,1024]{3,2,1,0:T(8,128)(2,1)S(1)}, bf16[2,2,16,1024]{3,2,1,0:T(8,128)(2,1)S(1)}, u32[]{:S(2)}, u32[]{:S(2)}) %collective-permute-start.8) | collective-permute-done | bytes 131104 | tf_op jit(solution)/shard_map/ppermute | solution.py:328
  16.8 2.7 %collective-permute-done.7 = bf16[2,16,1024]{2,1,0:T(8,128)(2,1)S(1)} collective-permute-done((bf16[2,16,1024]{2,1,0:T(8,128)(2,1)S(1)}, bf16[2,16,1024]{2,1,0:T(8,128)(2,1)S(1)}, u32[]{:S(2)}, u32[]{:S(2)}) %collective-permute-start.7) | collective-permute-done | bytes 65568 | tf_op jit(solution)/shard_map/ppermute | solution.py:328
  19.6 2.5 %collective-permute-start.10 = (bf16[3,16,1024]{2,1,0:T(8,128)(2,1)S(1)}, bf16[3,16,1024]{2,1,0:T(8,128)(2,1)S(1)}, u32[]{:S(2)}, u32[]{:S(2)}) collective-permute-start(bf16[3,16,1024]{2,1,0:T(8,128)(2,1)S(1)} %get-tuple-element.23), channel_id=1, source_target_pairs={{0,18},{1,17},{2,16},{3,19},{4,22},{5,21},{6,20},{7,23},{8,26},{9,... | collective-permute-start | bytes 294920 | tf_op jit(solution)/shard_map/ppermute | solution.py:328
  22.1 0.5 %collective-permute-start.9 = (bf16[3,16,1024]{2,1,0:T(8,128)(2,1)S(1)}, bf16[3,16,1024]{2,1,0:T(8,128)(2,1)S(1)}, u32[]{:S(2)}, u32[]{:S(2)}) collective-permute-start(bf16[3,16,1024]{2,1,0:T(8,128)(2,1)S(1)} %get-tuple-element.24), channel_id=1, source_target_pairs={{0,16},{1,3},{2,18},{3,1},{4,20},{5,7},{6,22},{7,5},{8,24},{9,11},... | collective-permute-start | bytes 294920 | tf_op jit(solution)/shard_map/ppermute | solution.py:328
  22.6 0.0 collective-permute-done.4.refs_2_
  22.6 0.5 %collective-permute-start.11 = (bf16[3,16,1024]{2,1,0:T(8,128)(2,1)S(1)}, bf16[3,16,1024]{2,1,0:T(8,128)(2,1)S(1)}, u32[]{:S(2)}, u32[]{:S(2)}) collective-permute-start(bf16[3,16,1024]{2,1,0:T(8,128)(2,1)S(1)} %get-tuple-element.36), channel_id=1, source_target_pairs={{0,2},{1,19},{2,0},{3,17},{4,6},{5,23},{6,4},{7,21},{8,10},{9,27},... | collective-permute-start | bytes 294920 | tf_op jit(solution)/shard_map/ppermute | solution.py:328
  23.1 0.8 %collective-permute-done.3.refs_1_ = bf16[5,16,1024]{2,1,0:T(8,128)(2,1)S(1)} collective-permute-done((bf16[5,16,1024]{2,1,0:T(8,128)(2,1)S(1)}, bf16[5,16,1024]{2,1,0:T(8,128)(2,1)S(1)}, u32[]{:S(2)}, u32[]{:S(2)}) %collective-permute-start.3) | collective-permute-done | bytes 163872 | tf_op jit(solution)/shard_map/ppermute | solution.py:328
  24.0 0.1 collective-permute-done.5.refs_3_
  24.1 0.0 copy-done
  24.1 0.5 %image.2.refs_8_ = f32[512,1024]{1,0:T(8,128)S(1)} custom-call(bf16[2,512,512]{2,1,0:T(8,128)(2,1)S(1)} %copy-done, bf16[5,16,1024]{2,1,0:T(8,128)(2,1)S(1)} %get-tuple-element.29.refs_0_, bf16[5,16,1024]{2,1,0:T(8,128)(2,1)S(1)} %collective-permute-done.3.refs_1_, bf16[5,16,1024]{2,1,0:T(8,128)(2,1)S(1)} %collective-permute-done.4.refs_2_, ...), custom_call_target="tpu_custom_call" | custom-call | flops 268435456 | bytes 2097152 | tf_op jit(solution)/shard_map/image/pallas_call | solution.py:274
  24.6 1.3 %collective-permute-done.10.refs_6_ = bf16[3,16,1024]{2,1,0:T(8,128)(2,1)S(1)} collective-permute-done((bf16[3,16,1024]{2,1,0:T(8,128)(2,1)S(1)}, bf16[3,16,1024]{2,1,0:T(8,128)(2,1)S(1)}, u32[]{:S(2)}, u32[]{:S(2)}) %collective-permute-start.10) | collective-permute-done | bytes 98336 | tf_op jit(solution)/shard_map/ppermute | solution.py:328
  25.9 1.3 %collective-permute-done.9.refs_5_ = bf16[3,16,1024]{2,1,0:T(8,128)(2,1)S(1)} collective-permute-done((bf16[3,16,1024]{2,1,0:T(8,128)(2,1)S(1)}, bf16[3,16,1024]{2,1,0:T(8,128)(2,1)S(1)}, u32[]{:S(2)}, u32[]{:S(2)}) %collective-permute-start.9) | collective-permute-done | bytes 98336 | tf_op jit(solution)/shard_map/ppermute | solution.py:328
  27.2 0.5 %collective-permute-done.11.refs_7_ = bf16[3,16,1024]{2,1,0:T(8,128)(2,1)S(1)} collective-permute-done((bf16[3,16,1024]{2,1,0:T(8,128)(2,1)S(1)}, bf16[3,16,1024]{2,1,0:T(8,128)(2,1)S(1)}, u32[]{:S(2)}, u32[]{:S(2)}) %collective-permute-start.11) | collective-permute-done | bytes 98336 | tf_op jit(solution)/shard_map/ppermute | solution.py:328
  27.7 1.3 %image.3 = bf16[512,1024]{1,0:T(8,128)(2,1)} custom-call(bf16[2,512,512]{2,1,0:T(8,128)(2,1)S(1)} %copy-done, bf16[5,16,1024]{2,1,0:T(8,128)(2,1)S(1)} %get-tuple-element.29.refs_0_, bf16[5,16,1024]{2,1,0:T(8,128)(2,1)S(1)} %collective-permute-done.3.refs_1_, bf16[5,16,1024]{2,1,0:T(8,128)(2,1)S(1)} %collective-permute-done.4.refs_2_, ...), custom_call_target="tpu_custom_call" | custom-call | flops 268435456 | bytes 2097152 | tf_op jit(solution)/shard_map/image/pallas_call | solution.py:274
  (9 shorter events, 0.1 us)
Async XLA Ops:
  0.0 24.1 %copy-start = (bf16[2,512,512]{2,1,0:T(8,128)(2,1)S(1)}, bf16[2,512,512]{2,1,0:T(8,128)(2,1)}, u32[]{:S(2)}) copy-start(bf16[2,512,512]{2,1,0:T(8,128)(2,1)} %constant.29.clone.table) | copy-start | bytes 3145732
  2.5 4.2 %collective-permute-start = (bf16[6,16,1024]{2,1,0:T(8,128)(2,1)S(1)}, bf16[6,16,1024]{2,1,0:T(8,128)(2,1)S(1)}, u32[]{:S(2)}, u32[]{:S(2)}) collective-permute-start(bf16[6,16,1024]{2,1,0:T(8,128)(2,1)S(1)} %get-tuple-element.14), channel_id=1, source_target_pairs={{0,1},{1,0},{2,3},{3,2},{4,5},{5,4},{6,7},{7,6},{8,9},{9,8},{10,11... | collective-permute-start | bytes 589832 | tf_op jit(solution)/shard_map/ppermute | solution.py:328
  3.0 7.9 %collective-permute-start.2 = (bf16[2,16,1024]{2,1,0:T(8,128)(2,1)S(1)}, bf16[2,16,1024]{2,1,0:T(8,128)(2,1)S(1)}, u32[]{:S(2)}, u32[]{:S(2)}) collective-permute-start(bf16[2,16,1024]{2,1,0:T(8,128)(2,1)S(1)} %get-tuple-element.16), channel_id=1, source_target_pairs={{0,8},{1,9},{2,10},{3,11},{4,12},{5,13},{6,14},{7,15},{8,0},{9,1},... | collective-permute-start | bytes 196616 | tf_op jit(solution)/shard_map/ppermute | solution.py:328
  6.6 3.2 %collective-permute-start.6 = (bf16[2,16,1024]{2,1,0:T(8,128)(2,1)S(1)}, bf16[2,16,1024]{2,1,0:T(8,128)(2,1)S(1)}, u32[]{:S(2)}, u32[]{:S(2)}) collective-permute-start(bf16[2,16,1024]{2,1,0:T(8,128)(2,1)S(1)} %get-tuple-element.19), channel_id=1, source_target_pairs={{0,1},{1,0},{2,3},{3,2},{4,5},{5,4},{6,7},{7,6},{8,9},{9,8},{10,11... | collective-permute-start | bytes 196616 | tf_op jit(solution)/shard_map/ppermute | solution.py:328
  6.9 6.0 %collective-permute-start.1 = (bf16[2,2,16,1024]{3,2,0,1:T(8,128)(2,1)S(1)}, bf16[2,2,16,1024]{3,2,0,1:T(8,128)(2,1)S(1)}, u32[]{:S(2)}, u32[]{:S(2)}) collective-permute-start(bf16[2,2,16,1024]{3,2,0,1:T(8,128)(2,1)S(1)} %pad_maximum_fusion.2), channel_id=1, source_target_pairs={{0,4},{1,5},{2,6},{3,7},{4,0},{5,1},{6,2},{7,3},{8,12},{9,13},{10,... | collective-permute-start | bytes 393224 | tf_op jit(solution)/shard_map/ppermute | solution.py:328
  8.5 8.3 %collective-permute-start.8 = (bf16[2,2,16,1024]{3,2,1,0:T(8,128)(2,1)S(1)}, bf16[2,2,16,1024]{3,2,1,0:T(8,128)(2,1)S(1)}, u32[]{:S(2)}, u32[]{:S(2)}) collective-permute-start(bf16[2,2,16,1024]{3,2,1,0:T(8,128)(2,1)S(1)} %pad_maximum_fusion.3), channel_id=1, source_target_pairs={{0,12},{1,13},{2,14},{3,15},{4,8},{5,9},{6,10},{7,11},{8,4},{9,5},... | collective-permute-start | bytes 393224 | tf_op jit(solution)/shard_map/ppermute | solution.py:328
  9.8 9.7 %collective-permute-start.7 = (bf16[2,16,1024]{2,1,0:T(8,128)(2,1)S(1)}, bf16[2,16,1024]{2,1,0:T(8,128)(2,1)S(1)}, u32[]{:S(2)}, u32[]{:S(2)}) collective-permute-start(bf16[2,16,1024]{2,1,0:T(8,128)(2,1)S(1)} %collective-permute-done.6), channel_id=1, source_target_pairs={{0,8},{1,9},{2,10},{3,11},{4,12},{5,13},{6,14},{7,15},{8,0},{9,1},... | collective-permute-start | bytes 196616 | tf_op jit(solution)/shard_map/ppermute | solution.py:328
  13.0 9.7 %collective-permute-start.4 = (bf16[5,16,1024]{2,1,0:T(8,128)(2,1)S(1)}, bf16[5,16,1024]{2,1,0:T(8,128)(2,1)S(1)}, u32[]{:S(2)}, u32[]{:S(2)}) collective-permute-start(bf16[5,16,1024]{2,1,0:T(8,128)(2,1)S(1)} %get-tuple-element.21), channel_id=1, source_target_pairs={{0,18},{1,17},{2,16},{3,19},{4,22},{5,21},{6,20},{7,23},{8,26},{9,... | collective-permute-start | bytes 491528 | tf_op jit(solution)/shard_map/ppermute | solution.py:328
  15.6 8.4 %collective-permute-start.3 = (bf16[5,16,1024]{2,1,0:T(8,128)(2,1)S(1)}, bf16[5,16,1024]{2,1,0:T(8,128)(2,1)S(1)}, u32[]{:S(2)}, u32[]{:S(2)}) collective-permute-start(bf16[5,16,1024]{2,1,0:T(8,128)(2,1)S(1)} %get-tuple-element.22), channel_id=1, source_target_pairs={{0,16},{1,3},{2,18},{3,1},{4,20},{5,7},{6,22},{7,5},{8,24},{9,11},... | collective-permute-start | bytes 491528 | tf_op jit(solution)/shard_map/ppermute | solution.py:328
  16.1 8.0 %collective-permute-start.5 = (bf16[5,16,1024]{2,1,0:T(8,128)(2,1)S(1)}, bf16[5,16,1024]{2,1,0:T(8,128)(2,1)S(1)}, u32[]{:S(2)}, u32[]{:S(2)}) collective-permute-start(bf16[5,16,1024]{2,1,0:T(8,128)(2,1)S(1)} %get-tuple-element.28), channel_id=1, source_target_pairs={{0,2},{1,19},{2,0},{3,17},{4,6},{5,23},{6,4},{7,21},{8,10},{9,27},... | collective-permute-start | bytes 491528 | tf_op jit(solution)/shard_map/ppermute | solution.py:328
  19.6 6.3 %collective-permute-start.10 = (bf16[3,16,1024]{2,1,0:T(8,128)(2,1)S(1)}, bf16[3,16,1024]{2,1,0:T(8,128)(2,1)S(1)}, u32[]{:S(2)}, u32[]{:S(2)}) collective-permute-start(bf16[3,16,1024]{2,1,0:T(8,128)(2,1)S(1)} %get-tuple-element.23), channel_id=1, source_target_pairs={{0,18},{1,17},{2,16},{3,19},{4,22},{5,21},{6,20},{7,23},{8,26},{9,... | collective-permute-start | bytes 294920 | tf_op jit(solution)/shard_map/ppermute | solution.py:328
  22.1 5.1 %collective-permute-start.9 = (bf16[3,16,1024]{2,1,0:T(8,128)(2,1)S(1)}, bf16[3,16,1024]{2,1,0:T(8,128)(2,1)S(1)}, u32[]{:S(2)}, u32[]{:S(2)}) collective-permute-start(bf16[3,16,1024]{2,1,0:T(8,128)(2,1)S(1)} %get-tuple-element.24), channel_id=1, source_target_pairs={{0,16},{1,3},{2,18},{3,1},{4,20},{5,7},{6,22},{7,5},{8,24},{9,11},... | collective-permute-start | bytes 294920 | tf_op jit(solution)/shard_map/ppermute | solution.py:328
  22.6 5.1 %collective-permute-start.11 = (bf16[3,16,1024]{2,1,0:T(8,128)(2,1)S(1)}, bf16[3,16,1024]{2,1,0:T(8,128)(2,1)S(1)}, u32[]{:S(2)}, u32[]{:S(2)}) collective-permute-start(bf16[3,16,1024]{2,1,0:T(8,128)(2,1)S(1)} %get-tuple-element.36), channel_id=1, source_target_pairs={{0,2},{1,19},{2,0},{3,17},{4,6},{5,23},{6,4},{7,21},{8,10},{9,27},... | collective-permute-start | bytes 294920 | tf_op jit(solution)/shard_map/ppermute | solution.py:328

commit v7 on v6

--- a/solution.py
+++ b/solution.py
@@ -15,7 +15,7 @@
 DELAY_MAX = 64
 LANES = 128
 RAW_PIECES = 4
-ROWS = RADIX + DELAY_MAX
+ROWS = RADIX + DELAY_MAX + 8
 
 
 TWO_PI = 2.0 * math.pi
@@ -96,13 +96,9 @@
     return to_bf16(np.stack(tables))
 
 
-def compress_kernel(
-    plan, delays_far, raw_far, dft_far, twiddle_far, near_far, *refs
-):
-    outs = refs[: len(plan)]
-    (
-    delays, raw, dft, twiddle, near, arrived, lines, grid_in, section, twisted, turned,
-    ) = refs[len(plan) :]
+def compress_kernel(plan, delays_far, raw_far, dft_far, twiddle_far, near_far, *refs):
+    outs, scratch = refs[: len(plan)], refs[len(plan) :]
+    delays, raw, dft, twiddle, near, arrived, lines, grid_in, section, twisted, turned = scratch
     pulse_count = raw.shape[1]
     width = outs[0].shape[-1]
     me = lax.axis_index("gate")
@@ -191,7 +187,8 @@
             start = pl.multiple_of((me ^ apart) * block_rows, block_rows)
             for step in range(width // LANES):
                 rows = pl.ds(start + step * pulse_count, pulse_count)
-                both = jnp.concatenate([turned[rows, :], turned[pl.ds(span + start + step * pulse_count, pulse_count), :]], axis=0)
+                imag_rows = pl.ds(span + start + step * pulse_count, pulse_count)
+                both = jnp.concatenate([turned[rows, :], turned[imag_rows, :]], axis=0)
                 out[index, :, pl.ds(step * LANES, LANES)] = both.astype(jnp.bfloat16)
 
 
@@ -216,11 +213,11 @@
             pltpu.VMEM(twiddle.shape, twiddle.dtype),
             pltpu.VMEM(near.shape, near.dtype),
             pltpu.SemaphoreType.DMA((RAW_PIECES + 4,)),
-            pltpu.VMEM((2 * span, LANES), jnp.float32),
+            pltpu.VMEM((2 * span + pulse_count, LANES), jnp.float32),
             pltpu.VMEM((2 * RADIX, pulse_count * LANES), jnp.bfloat16),
             pltpu.VMEM((pulse_count, 2, ROWS, LANES), jnp.float32),
             pltpu.VMEM((span, 2 * LANES), jnp.bfloat16),
-            pltpu.VMEM((2 * span, LANES), jnp.float32),
+            pltpu.VMEM((2 * span + pulse_count, LANES), jnp.float32),
         ],
         compiler_params=pltpu.CompilerParams(vmem_limit_bytes=60 * 2**20),
         name="compress",

time: 29.2 us -> 29.2 us (level)
  no operation moved by 1% of the time
where the time goes in v7:
time: 29.2 us; the launch traced here: 29.1 us
  starting transfers between devices  15.1 us (52%)
  waiting for transfers between devices  9.37 us (32%)
  Pallas kernels  4.29 us (15%)
    ppermute x12, starting transfers between devices, swap(): return lax.ppermute(array, ('sub', 'gate'), pairs)  15.1 us
    ppermute x12, waiting for transfers between devices, swap(): return lax.ppermute(array, ('sub', 'gate'), pairs)  9.37 us
    pallas_call x1, Pallas kernels, range_compress(): pl.pallas_call(functools.partial(compress_kernel, plan), out_shape=[pltpu...  2.48 us
    pallas_call x2, Pallas kernels, form_image(): pl.pallas_call(functools.partial(image_kernel, [plan[i] for i in used], f...  1.81 us
  transfers between devices with their start and end apart: 12, of which 9 were waited for; matrix products, arithmetic and copies ran while one was open for 1% of the time, Pallas kernels for 2%

profile of v7, /device:TPU:0, one launch (start us, length us, event | category | flops | bytes accessed | tf_op | source)
XLA Modules:
  0.0 29.1 jit_solution(717945130269733640)
XLA Ops:
  0.0 0.0 copy-start
  0.0 2.5 %compress.1 = (bf16[2,16,1024]{2,1,0:T(8,128)(2,1)S(1)}, bf16[2,16,1024]{2,1,0:T(8,128)(2,1)S(1)}, bf16[2,16,1024]{2,1,0:T(8,128)(2,1)S(1)}, bf16[2,16,1024]{2,1...) custom-call(s32[8]{0:T(128)} %delays_far.1, bf16[2,8,16384]{2,1,0:T(8,128)(2,1)} %raw_far.1, ...), custom_call_target="tpu_custom_call" | custom-call | tf_op jit(solution)/shard_map/compress/pallas_call | solution.py:202
  2.5 0.5 %collective-permute-start = (bf16[6,16,1024]{2,1,0:T(8,128)(2,1)S(1)}, bf16[6,16,1024]{2,1,0:T(8,128)(2,1)S(1)}, u32[]{:S(2)}, u32[]{:S(2)}) collective-permute-start(bf16[6,16,1024]{2,1,0:T(8,128)(2,1)S(1)} %get-tuple-element.14), channel_id=1, source_target_pairs={{0,1},{1,0},{2,3},{3,2},{4,5},{5,4},{6,7},{7,6},{8,9},{9,8},{10,11... | collective-permute-start | bytes 589832 | tf_op jit(solution)/shard_map/ppermute | solution.py:325
  3.0 3.7 %collective-permute-start.2 = (bf16[2,16,1024]{2,1,0:T(8,128)(2,1)S(1)}, bf16[2,16,1024]{2,1,0:T(8,128)(2,1)S(1)}, u32[]{:S(2)}, u32[]{:S(2)}) collective-permute-start(bf16[2,16,1024]{2,1,0:T(8,128)(2,1)S(1)} %get-tuple-element.16), channel_id=1, source_target_pairs={{0,8},{1,9},{2,10},{3,11},{4,12},{5,13},{6,14},{7,15},{8,0},{9,1},... | collective-permute-start | bytes 196616 | tf_op jit(solution)/shard_map/ppermute | solution.py:325
  6.7 0.0 collective-permute-done
  6.7 0.2 collective-permute-start.6
  6.9 1.6 %collective-permute-start.1 = (bf16[2,2,16,1024]{3,2,0,1:T(8,128)(2,1)S(1)}, bf16[2,2,16,1024]{3,2,0,1:T(8,128)(2,1)S(1)}, u32[]{:S(2)}, u32[]{:S(2)}) collective-permute-start(bf16[2,2,16,1024]{3,2,0,1:T(8,128)(2,1)S(1)} %pad_maximum_fusion.2), channel_id=1, source_target_pairs={{0,4},{1,5},{2,6},{3,7},{4,0},{5,1},{6,2},{7,3},{8,12},{9,13},{10,... | collective-permute-start | bytes 393224 | tf_op jit(solution)/shard_map/ppermute | solution.py:325
  8.5 1.3 %collective-permute-start.8 = (bf16[2,2,16,1024]{3,2,1,0:T(8,128)(2,1)S(1)}, bf16[2,2,16,1024]{3,2,1,0:T(8,128)(2,1)S(1)}, u32[]{:S(2)}, u32[]{:S(2)}) collective-permute-start(bf16[2,2,16,1024]{3,2,1,0:T(8,128)(2,1)S(1)} %pad_maximum_fusion.3), channel_id=1, source_target_pairs={{0,12},{1,13},{2,14},{3,15},{4,8},{5,9},{6,10},{7,11},{8,4},{9,5},... | collective-permute-start | bytes 393224 | tf_op jit(solution)/shard_map/ppermute | solution.py:325
  9.9 0.0 collective-permute-done.6
  9.9 0.7 %collective-permute-start.7 = (bf16[2,16,1024]{2,1,0:T(8,128)(2,1)S(1)}, bf16[2,16,1024]{2,1,0:T(8,128)(2,1)S(1)}, u32[]{:S(2)}, u32[]{:S(2)}) collective-permute-start(bf16[2,16,1024]{2,1,0:T(8,128)(2,1)S(1)} %collective-permute-done.6), channel_id=1, source_target_pairs={{0,8},{1,9},{2,10},{3,11},{4,12},{5,13},{6,14},{7,15},{8,0},{9,1},... | collective-permute-start | bytes 196616 | tf_op jit(solution)/shard_map/ppermute | solution.py:325
  10.6 0.3 collective-permute-done.2
  10.9 2.0 %collective-permute-done.1 = bf16[2,2,16,1024]{3,2,0,1:T(8,128)(2,1)S(1)} collective-permute-done((bf16[2,2,16,1024]{3,2,0,1:T(8,128)(2,1)S(1)}, bf16[2,2,16,1024]{3,2,0,1:T(8,128)(2,1)S(1)}, u32[]{:S(2)}, u32[]{:S(2)}) %collective-permute-start.1) | collective-permute-done | bytes 131104 | tf_op jit(solution)/shard_map/ppermute | solution.py:325
  12.9 0.1 broadcast_select_fusion
  13.0 2.6 %collective-permute-start.4 = (bf16[5,16,1024]{2,1,0:T(8,128)(2,1)S(1)}, bf16[5,16,1024]{2,1,0:T(8,128)(2,1)S(1)}, u32[]{:S(2)}, u32[]{:S(2)}) collective-permute-start(bf16[5,16,1024]{2,1,0:T(8,128)(2,1)S(1)} %get-tuple-element.21), channel_id=1, source_target_pairs={{0,18},{1,17},{2,16},{3,19},{4,22},{5,21},{6,20},{7,23},{8,26},{9,... | collective-permute-start | bytes 491528 | tf_op jit(solution)/shard_map/ppermute | solution.py:325
  15.6 0.5 %collective-permute-start.3 = (bf16[5,16,1024]{2,1,0:T(8,128)(2,1)S(1)}, bf16[5,16,1024]{2,1,0:T(8,128)(2,1)S(1)}, u32[]{:S(2)}, u32[]{:S(2)}) collective-permute-start(bf16[5,16,1024]{2,1,0:T(8,128)(2,1)S(1)} %get-tuple-element.22), channel_id=1, source_target_pairs={{0,16},{1,3},{2,18},{3,1},{4,20},{5,7},{6,22},{7,5},{8,24},{9,11},... | collective-permute-start | bytes 491528 | tf_op jit(solution)/shard_map/ppermute | solution.py:325
  16.1 0.4 %collective-permute-start.5 = (bf16[5,16,1024]{2,1,0:T(8,128)(2,1)S(1)}, bf16[5,16,1024]{2,1,0:T(8,128)(2,1)S(1)}, u32[]{:S(2)}, u32[]{:S(2)}) collective-permute-start(bf16[5,16,1024]{2,1,0:T(8,128)(2,1)S(1)} %get-tuple-element.28), channel_id=1, source_target_pairs={{0,2},{1,19},{2,0},{3,17},{4,6},{5,23},{6,4},{7,21},{8,10},{9,27},... | collective-permute-start | bytes 491528 | tf_op jit(solution)/shard_map/ppermute | solution.py:325
  16.6 0.3 %collective-permute-done.8 = bf16[2,2,16,1024]{3,2,1,0:T(8,128)(2,1)S(1)} collective-permute-done((bf16[2,2,16,1024]{3,2,1,0:T(8,128)(2,1)S(1)}, bf16[2,2,16,1024]{3,2,1,0:T(8,128)(2,1)S(1)}, u32[]{:S(2)}, u32[]{:S(2)}) %collective-permute-start.8) | collective-permute-done | bytes 131104 | tf_op jit(solution)/shard_map/ppermute | solution.py:325
  16.9 2.7 %collective-permute-done.7 = bf16[2,16,1024]{2,1,0:T(8,128)(2,1)S(1)} collective-permute-done((bf16[2,16,1024]{2,1,0:T(8,128)(2,1)S(1)}, bf16[2,16,1024]{2,1,0:T(8,128)(2,1)S(1)}, u32[]{:S(2)}, u32[]{:S(2)}) %collective-permute-start.7) | collective-permute-done | bytes 65568 | tf_op jit(solution)/shard_map/ppermute | solution.py:325
  19.6 2.5 %collective-permute-start.10 = (bf16[3,16,1024]{2,1,0:T(8,128)(2,1)S(1)}, bf16[3,16,1024]{2,1,0:T(8,128)(2,1)S(1)}, u32[]{:S(2)}, u32[]{:S(2)}) collective-permute-start(bf16[3,16,1024]{2,1,0:T(8,128)(2,1)S(1)} %get-tuple-element.23), channel_id=1, source_target_pairs={{0,18},{1,17},{2,16},{3,19},{4,22},{5,21},{6,20},{7,23},{8,26},{9,... | collective-permute-start | bytes 294920 | tf_op jit(solution)/shard_map/ppermute | solution.py:325
  22.1 0.5 %collective-permute-start.9 = (bf16[3,16,1024]{2,1,0:T(8,128)(2,1)S(1)}, bf16[3,16,1024]{2,1,0:T(8,128)(2,1)S(1)}, u32[]{:S(2)}, u32[]{:S(2)}) collective-permute-start(bf16[3,16,1024]{2,1,0:T(8,128)(2,1)S(1)} %get-tuple-element.24), channel_id=1, source_target_pairs={{0,16},{1,3},{2,18},{3,1},{4,20},{5,7},{6,22},{7,5},{8,24},{9,11},... | collective-permute-start | bytes 294920 | tf_op jit(solution)/shard_map/ppermute | solution.py:325
  22.7 0.0 collective-permute-done.4.refs_2_
  22.7 0.5 %collective-permute-start.11 = (bf16[3,16,1024]{2,1,0:T(8,128)(2,1)S(1)}, bf16[3,16,1024]{2,1,0:T(8,128)(2,1)S(1)}, u32[]{:S(2)}, u32[]{:S(2)}) collective-permute-start(bf16[3,16,1024]{2,1,0:T(8,128)(2,1)S(1)} %get-tuple-element.36), channel_id=1, source_target_pairs={{0,2},{1,19},{2,0},{3,17},{4,6},{5,23},{6,4},{7,21},{8,10},{9,27},... | collective-permute-start | bytes 294920 | tf_op jit(solution)/shard_map/ppermute | solution.py:325
  23.2 0.9 %collective-permute-done.3.refs_1_ = bf16[5,16,1024]{2,1,0:T(8,128)(2,1)S(1)} collective-permute-done((bf16[5,16,1024]{2,1,0:T(8,128)(2,1)S(1)}, bf16[5,16,1024]{2,1,0:T(8,128)(2,1)S(1)}, u32[]{:S(2)}, u32[]{:S(2)}) %collective-permute-start.3) | collective-permute-done | bytes 163872 | tf_op jit(solution)/shard_map/ppermute | solution.py:325
  24.0 0.1 collective-permute-done.5.refs_3_
  24.1 0.0 copy-done
  24.1 0.5 %image.2.refs_8_ = f32[512,1024]{1,0:T(8,128)S(1)} custom-call(bf16[2,512,512]{2,1,0:T(8,128)(2,1)S(1)} %copy-done, bf16[5,16,1024]{2,1,0:T(8,128)(2,1)S(1)} %get-tuple-element.29.refs_0_, bf16[5,16,1024]{2,1,0:T(8,128)(2,1)S(1)} %collective-permute-done.3.refs_1_, bf16[5,16,1024]{2,1,0:T(8,128)(2,1)S(1)} %collective-permute-done.4.refs_2_, ...), custom_call_target="tpu_custom_call" | custom-call | flops 268435456 | bytes 2097152 | tf_op jit(solution)/shard_map/image/pallas_call | solution.py:271
  24.6 1.3 %collective-permute-done.10.refs_6_ = bf16[3,16,1024]{2,1,0:T(8,128)(2,1)S(1)} collective-permute-done((bf16[3,16,1024]{2,1,0:T(8,128)(2,1)S(1)}, bf16[3,16,1024]{2,1,0:T(8,128)(2,1)S(1)}, u32[]{:S(2)}, u32[]{:S(2)}) %collective-permute-start.10) | collective-permute-done | bytes 98336 | tf_op jit(solution)/shard_map/ppermute | solution.py:325
  26.0 1.3 %collective-permute-done.9.refs_5_ = bf16[3,16,1024]{2,1,0:T(8,128)(2,1)S(1)} collective-permute-done((bf16[3,16,1024]{2,1,0:T(8,128)(2,1)S(1)}, bf16[3,16,1024]{2,1,0:T(8,128)(2,1)S(1)}, u32[]{:S(2)}, u32[]{:S(2)}) %collective-permute-start.9) | collective-permute-done | bytes 98336 | tf_op jit(solution)/shard_map/ppermute | solution.py:325
  27.2 0.5 %collective-permute-done.11.refs_7_ = bf16[3,16,1024]{2,1,0:T(8,128)(2,1)S(1)} collective-permute-done((bf16[3,16,1024]{2,1,0:T(8,128)(2,1)S(1)}, bf16[3,16,1024]{2,1,0:T(8,128)(2,1)S(1)}, u32[]{:S(2)}, u32[]{:S(2)}) %collective-permute-start.11) | collective-permute-done | bytes 98336 | tf_op jit(solution)/shard_map/ppermute | solution.py:325
  27.7 1.3 %image.3 = bf16[512,1024]{1,0:T(8,128)(2,1)} custom-call(bf16[2,512,512]{2,1,0:T(8,128)(2,1)S(1)} %copy-done, bf16[5,16,1024]{2,1,0:T(8,128)(2,1)S(1)} %get-tuple-element.29.refs_0_, bf16[5,16,1024]{2,1,0:T(8,128)(2,1)S(1)} %collective-permute-done.3.refs_1_, bf16[5,16,1024]{2,1,0:T(8,128)(2,1)S(1)} %collective-permute-done.4.refs_2_, ...), custom_call_target="tpu_custom_call" | custom-call | flops 268435456 | bytes 2097152 | tf_op jit(solution)/shard_map/image/pallas_call | solution.py:271
  (9 shorter events, 0.1 us)
Async XLA Ops:
  0.0 24.1 %copy-start = (bf16[2,512,512]{2,1,0:T(8,128)(2,1)S(1)}, bf16[2,512,512]{2,1,0:T(8,128)(2,1)}, u32[]{:S(2)}) copy-start(bf16[2,512,512]{2,1,0:T(8,128)(2,1)} %constant.29.clone.table) | copy-start | bytes 3145732
  2.5 4.2 %collective-permute-start = (bf16[6,16,1024]{2,1,0:T(8,128)(2,1)S(1)}, bf16[6,16,1024]{2,1,0:T(8,128)(2,1)S(1)}, u32[]{:S(2)}, u32[]{:S(2)}) collective-permute-start(bf16[6,16,1024]{2,1,0:T(8,128)(2,1)S(1)} %get-tuple-element.14), channel_id=1, source_target_pairs={{0,1},{1,0},{2,3},{3,2},{4,5},{5,4},{6,7},{7,6},{8,9},{9,8},{10,11... | collective-permute-start | bytes 589832 | tf_op jit(solution)/shard_map/ppermute | solution.py:325
  3.0 7.9 %collective-permute-start.2 = (bf16[2,16,1024]{2,1,0:T(8,128)(2,1)S(1)}, bf16[2,16,1024]{2,1,0:T(8,128)(2,1)S(1)}, u32[]{:S(2)}, u32[]{:S(2)}) collective-permute-start(bf16[2,16,1024]{2,1,0:T(8,128)(2,1)S(1)} %get-tuple-element.16), channel_id=1, source_target_pairs={{0,8},{1,9},{2,10},{3,11},{4,12},{5,13},{6,14},{7,15},{8,0},{9,1},... | collective-permute-start | bytes 196616 | tf_op jit(solution)/shard_map/ppermute | solution.py:325
  6.7 3.2 %collective-permute-start.6 = (bf16[2,16,1024]{2,1,0:T(8,128)(2,1)S(1)}, bf16[2,16,1024]{2,1,0:T(8,128)(2,1)S(1)}, u32[]{:S(2)}, u32[]{:S(2)}) collective-permute-start(bf16[2,16,1024]{2,1,0:T(8,128)(2,1)S(1)} %get-tuple-element.19), channel_id=1, source_target_pairs={{0,1},{1,0},{2,3},{3,2},{4,5},{5,4},{6,7},{7,6},{8,9},{9,8},{10,11... | collective-permute-start | bytes 196616 | tf_op jit(solution)/shard_map/ppermute | solution.py:325
  6.9 6.0 %collective-permute-start.1 = (bf16[2,2,16,1024]{3,2,0,1:T(8,128)(2,1)S(1)}, bf16[2,2,16,1024]{3,2,0,1:T(8,128)(2,1)S(1)}, u32[]{:S(2)}, u32[]{:S(2)}) collective-permute-start(bf16[2,2,16,1024]{3,2,0,1:T(8,128)(2,1)S(1)} %pad_maximum_fusion.2), channel_id=1, source_target_pairs={{0,4},{1,5},{2,6},{3,7},{4,0},{5,1},{6,2},{7,3},{8,12},{9,13},{10,... | collective-permute-start | bytes 393224 | tf_op jit(solution)/shard_map/ppermute | solution.py:325
  8.5 8.3 %collective-permute-start.8 = (bf16[2,2,16,1024]{3,2,1,0:T(8,128)(2,1)S(1)}, bf16[2,2,16,1024]{3,2,1,0:T(8,128)(2,1)S(1)}, u32[]{:S(2)}, u32[]{:S(2)}) collective-permute-start(bf16[2,2,16,1024]{3,2,1,0:T(8,128)(2,1)S(1)} %pad_maximum_fusion.3), channel_id=1, source_target_pairs={{0,12},{1,13},{2,14},{3,15},{4,8},{5,9},{6,10},{7,11},{8,4},{9,5},... | collective-permute-start | bytes 393224 | tf_op jit(solution)/shard_map/ppermute | solution.py:325
  9.9 9.7 %collective-permute-start.7 = (bf16[2,16,1024]{2,1,0:T(8,128)(2,1)S(1)}, bf16[2,16,1024]{2,1,0:T(8,128)(2,1)S(1)}, u32[]{:S(2)}, u32[]{:S(2)}) collective-permute-start(bf16[2,16,1024]{2,1,0:T(8,128)(2,1)S(1)} %collective-permute-done.6), channel_id=1, source_target_pairs={{0,8},{1,9},{2,10},{3,11},{4,12},{5,13},{6,14},{7,15},{8,0},{9,1},... | collective-permute-start | bytes 196616 | tf_op jit(solution)/shard_map/ppermute | solution.py:325
  13.0 9.7 %collective-permute-start.4 = (bf16[5,16,1024]{2,1,0:T(8,128)(2,1)S(1)}, bf16[5,16,1024]{2,1,0:T(8,128)(2,1)S(1)}, u32[]{:S(2)}, u32[]{:S(2)}) collective-permute-start(bf16[5,16,1024]{2,1,0:T(8,128)(2,1)S(1)} %get-tuple-element.21), channel_id=1, source_target_pairs={{0,18},{1,17},{2,16},{3,19},{4,22},{5,21},{6,20},{7,23},{8,26},{9,... | collective-permute-start | bytes 491528 | tf_op jit(solution)/shard_map/ppermute | solution.py:325
  15.6 8.4 %collective-permute-start.3 = (bf16[5,16,1024]{2,1,0:T(8,128)(2,1)S(1)}, bf16[5,16,1024]{2,1,0:T(8,128)(2,1)S(1)}, u32[]{:S(2)}, u32[]{:S(2)}) collective-permute-start(bf16[5,16,1024]{2,1,0:T(8,128)(2,1)S(1)} %get-tuple-element.22), channel_id=1, source_target_pairs={{0,16},{1,3},{2,18},{3,1},{4,20},{5,7},{6,22},{7,5},{8,24},{9,11},... | collective-permute-start | bytes 491528 | tf_op jit(solution)/shard_map/ppermute | solution.py:325
  16.1 8.0 %collective-permute-start.5 = (bf16[5,16,1024]{2,1,0:T(8,128)(2,1)S(1)}, bf16[5,16,1024]{2,1,0:T(8,128)(2,1)S(1)}, u32[]{:S(2)}, u32[]{:S(2)}) collective-permute-start(bf16[5,16,1024]{2,1,0:T(8,128)(2,1)S(1)} %get-tuple-element.28), channel_id=1, source_target_pairs={{0,2},{1,19},{2,0},{3,17},{4,6},{5,23},{6,4},{7,21},{8,10},{9,27},... | collective-permute-start | bytes 491528 | tf_op jit(solution)/shard_map/ppermute | solution.py:325
  19.6 6.3 %collective-permute-start.10 = (bf16[3,16,1024]{2,1,0:T(8,128)(2,1)S(1)}, bf16[3,16,1024]{2,1,0:T(8,128)(2,1)S(1)}, u32[]{:S(2)}, u32[]{:S(2)}) collective-permute-start(bf16[3,16,1024]{2,1,0:T(8,128)(2,1)S(1)} %get-tuple-element.23), channel_id=1, source_target_pairs={{0,18},{1,17},{2,16},{3,19},{4,22},{5,21},{6,20},{7,23},{8,26},{9,... | collective-permute-start | bytes 294920 | tf_op jit(solution)/shard_map/ppermute | solution.py:325
  22.1 5.1 %collective-permute-start.9 = (bf16[3,16,1024]{2,1,0:T(8,128)(2,1)S(1)}, bf16[3,16,1024]{2,1,0:T(8,128)(2,1)S(1)}, u32[]{:S(2)}, u32[]{:S(2)}) collective-permute-start(bf16[3,16,1024]{2,1,0:T(8,128)(2,1)S(1)} %get-tuple-element.24), channel_id=1, source_target_pairs={{0,16},{1,3},{2,18},{3,1},{4,20},{5,7},{6,22},{7,5},{8,24},{9,11},... | collective-permute-start | bytes 294920 | tf_op jit(solution)/shard_map/ppermute | solution.py:325
  22.7 5.1 %collective-permute-start.11 = (bf16[3,16,1024]{2,1,0:T(8,128)(2,1)S(1)}, bf16[3,16,1024]{2,1,0:T(8,128)(2,1)S(1)}, u32[]{:S(2)}, u32[]{:S(2)}) collective-permute-start(bf16[3,16,1024]{2,1,0:T(8,128)(2,1)S(1)} %get-tuple-element.36), channel_id=1, source_target_pairs={{0,2},{1,19},{2,0},{3,17},{4,6},{5,23},{6,4},{7,21},{8,10},{9,27},... | collective-permute-start | bytes 294920 | tf_op jit(solution)/shard_map/ppermute | solution.py:325

commit v8 on v7

--- a/solution.py
+++ b/solution.py
@@ -15,7 +15,7 @@
 DELAY_MAX = 64
 LANES = 128
 RAW_PIECES = 4
-ROWS = RADIX + DELAY_MAX + 8
+ROWS = RADIX + DELAY_MAX
 
 
 TWO_PI = 2.0 * math.pi

time: 29.2 us -> 29.2 us (level)
  no operation moved by 1% of the time
where the time goes in v8:
time: 29.2 us; the launch traced here: 29 us
  starting transfers between devices  15.1 us (52%)
  waiting for transfers between devices  9.37 us (32%)
  Pallas kernels  4.28 us (15%)
    ppermute x12, starting transfers between devices, swap(): return lax.ppermute(array, ('sub', 'gate'), pairs)  15.1 us
    ppermute x12, waiting for transfers between devices, swap(): return lax.ppermute(array, ('sub', 'gate'), pairs)  9.37 us
    pallas_call x1, Pallas kernels, range_compress(): pl.pallas_call(functools.partial(compress_kernel, plan), out_shape=[pltpu...  2.47 us
    pallas_call x2, Pallas kernels, form_image(): pl.pallas_call(functools.partial(image_kernel, [plan[i] for i in used], f...  1.81 us
  transfers between devices with their start and end apart: 12, of which 9 were waited for; matrix products, arithmetic and copies ran while one was open for 1% of the time, Pallas kernels for 2%

profile of v8, /device:TPU:0, one launch (start us, length us, event | category | flops | bytes accessed | tf_op | source)
XLA Modules:
  0.0 29.0 jit_solution(17094976986400459145)
XLA Ops:
  0.0 0.0 copy-start
  0.0 2.5 %compress.1 = (bf16[2,16,1024]{2,1,0:T(8,128)(2,1)S(1)}, bf16[2,16,1024]{2,1,0:T(8,128)(2,1)S(1)}, bf16[2,16,1024]{2,1,0:T(8,128)(2,1)S(1)}, bf16[2,16,1024]{2,1...) custom-call(s32[8]{0:T(128)} %delays_far.1, bf16[2,8,16384]{2,1,0:T(8,128)(2,1)} %raw_far.1, ...), custom_call_target="tpu_custom_call" | custom-call | tf_op jit(solution)/shard_map/compress/pallas_call | solution.py:202
  2.5 0.5 %collective-permute-start = (bf16[6,16,1024]{2,1,0:T(8,128)(2,1)S(1)}, bf16[6,16,1024]{2,1,0:T(8,128)(2,1)S(1)}, u32[]{:S(2)}, u32[]{:S(2)}) collective-permute-start(bf16[6,16,1024]{2,1,0:T(8,128)(2,1)S(1)} %get-tuple-element.14), channel_id=1, source_target_pairs={{0,1},{1,0},{2,3},{3,2},{4,5},{5,4},{6,7},{7,6},{8,9},{9,8},{10,11... | collective-permute-start | bytes 589832 | tf_op jit(solution)/shard_map/ppermute | solution.py:325
  3.0 3.7 %collective-permute-start.2 = (bf16[2,16,1024]{2,1,0:T(8,128)(2,1)S(1)}, bf16[2,16,1024]{2,1,0:T(8,128)(2,1)S(1)}, u32[]{:S(2)}, u32[]{:S(2)}) collective-permute-start(bf16[2,16,1024]{2,1,0:T(8,128)(2,1)S(1)} %get-tuple-element.16), channel_id=1, source_target_pairs={{0,8},{1,9},{2,10},{3,11},{4,12},{5,13},{6,14},{7,15},{8,0},{9,1},... | collective-permute-start | bytes 196616 | tf_op jit(solution)/shard_map/ppermute | solution.py:325
  6.7 0.0 collective-permute-done
  6.7 0.2 collective-permute-start.6
  6.9 1.6 %collective-permute-start.1 = (bf16[2,2,16,1024]{3,2,0,1:T(8,128)(2,1)S(1)}, bf16[2,2,16,1024]{3,2,0,1:T(8,128)(2,1)S(1)}, u32[]{:S(2)}, u32[]{:S(2)}) collective-permute-start(bf16[2,2,16,1024]{3,2,0,1:T(8,128)(2,1)S(1)} %pad_maximum_fusion.2), channel_id=1, source_target_pairs={{0,4},{1,5},{2,6},{3,7},{4,0},{5,1},{6,2},{7,3},{8,12},{9,13},{10,... | collective-permute-start | bytes 393224 | tf_op jit(solution)/shard_map/ppermute | solution.py:325
  8.5 1.3 %collective-permute-start.8 = (bf16[2,2,16,1024]{3,2,1,0:T(8,128)(2,1)S(1)}, bf16[2,2,16,1024]{3,2,1,0:T(8,128)(2,1)S(1)}, u32[]{:S(2)}, u32[]{:S(2)}) collective-permute-start(bf16[2,2,16,1024]{3,2,1,0:T(8,128)(2,1)S(1)} %pad_maximum_fusion.3), channel_id=1, source_target_pairs={{0,12},{1,13},{2,14},{3,15},{4,8},{5,9},{6,10},{7,11},{8,4},{9,5},... | collective-permute-start | bytes 393224 | tf_op jit(solution)/shard_map/ppermute | solution.py:325
  9.8 0.0 collective-permute-done.6
  9.9 0.7 %collective-permute-start.7 = (bf16[2,16,1024]{2,1,0:T(8,128)(2,1)S(1)}, bf16[2,16,1024]{2,1,0:T(8,128)(2,1)S(1)}, u32[]{:S(2)}, u32[]{:S(2)}) collective-permute-start(bf16[2,16,1024]{2,1,0:T(8,128)(2,1)S(1)} %collective-permute-done.6), channel_id=1, source_target_pairs={{0,8},{1,9},{2,10},{3,11},{4,12},{5,13},{6,14},{7,15},{8,0},{9,1},... | collective-permute-start | bytes 196616 | tf_op jit(solution)/shard_map/ppermute | solution.py:325
  10.6 0.3 collective-permute-done.2
  10.9 2.1 %collective-permute-done.1 = bf16[2,2,16,1024]{3,2,0,1:T(8,128)(2,1)S(1)} collective-permute-done((bf16[2,2,16,1024]{3,2,0,1:T(8,128)(2,1)S(1)}, bf16[2,2,16,1024]{3,2,0,1:T(8,128)(2,1)S(1)}, u32[]{:S(2)}, u32[]{:S(2)}) %collective-permute-start.1) | collective-permute-done | bytes 131104 | tf_op jit(solution)/shard_map/ppermute | solution.py:325
  12.9 0.1 broadcast_select_fusion
  13.0 2.6 %collective-permute-start.4 = (bf16[5,16,1024]{2,1,0:T(8,128)(2,1)S(1)}, bf16[5,16,1024]{2,1,0:T(8,128)(2,1)S(1)}, u32[]{:S(2)}, u32[]{:S(2)}) collective-permute-start(bf16[5,16,1024]{2,1,0:T(8,128)(2,1)S(1)} %get-tuple-element.21), channel_id=1, source_target_pairs={{0,18},{1,17},{2,16},{3,19},{4,22},{5,21},{6,20},{7,23},{8,26},{9,... | collective-permute-start | bytes 491528 | tf_op jit(solution)/shard_map/ppermute | solution.py:325
  15.6 0.5 %collective-permute-start.3 = (bf16[5,16,1024]{2,1,0:T(8,128)(2,1)S(1)}, bf16[5,16,1024]{2,1,0:T(8,128)(2,1)S(1)}, u32[]{:S(2)}, u32[]{:S(2)}) collective-permute-start(bf16[5,16,1024]{2,1,0:T(8,128)(2,1)S(1)} %get-tuple-element.22), channel_id=1, source_target_pairs={{0,16},{1,3},{2,18},{3,1},{4,20},{5,7},{6,22},{7,5},{8,24},{9,11},... | collective-permute-start | bytes 491528 | tf_op jit(solution)/shard_map/ppermute | solution.py:325
  16.1 0.4 %collective-permute-start.5 = (bf16[5,16,1024]{2,1,0:T(8,128)(2,1)S(1)}, bf16[5,16,1024]{2,1,0:T(8,128)(2,1)S(1)}, u32[]{:S(2)}, u32[]{:S(2)}) collective-permute-start(bf16[5,16,1024]{2,1,0:T(8,128)(2,1)S(1)} %get-tuple-element.28), channel_id=1, source_target_pairs={{0,2},{1,19},{2,0},{3,17},{4,6},{5,23},{6,4},{7,21},{8,10},{9,27},... | collective-permute-start | bytes 491528 | tf_op jit(solution)/shard_map/ppermute | solution.py:325
  16.6 0.3 %collective-permute-done.8 = bf16[2,2,16,1024]{3,2,1,0:T(8,128)(2,1)S(1)} collective-permute-done((bf16[2,2,16,1024]{3,2,1,0:T(8,128)(2,1)S(1)}, bf16[2,2,16,1024]{3,2,1,0:T(8,128)(2,1)S(1)}, u32[]{:S(2)}, u32[]{:S(2)}) %collective-permute-start.8) | collective-permute-done | bytes 131104 | tf_op jit(solution)/shard_map/ppermute | solution.py:325
  16.9 2.7 %collective-permute-done.7 = bf16[2,16,1024]{2,1,0:T(8,128)(2,1)S(1)} collective-permute-done((bf16[2,16,1024]{2,1,0:T(8,128)(2,1)S(1)}, bf16[2,16,1024]{2,1,0:T(8,128)(2,1)S(1)}, u32[]{:S(2)}, u32[]{:S(2)}) %collective-permute-start.7) | collective-permute-done | bytes 65568 | tf_op jit(solution)/shard_map/ppermute | solution.py:325
  19.6 2.5 %collective-permute-start.10 = (bf16[3,16,1024]{2,1,0:T(8,128)(2,1)S(1)}, bf16[3,16,1024]{2,1,0:T(8,128)(2,1)S(1)}, u32[]{:S(2)}, u32[]{:S(2)}) collective-permute-start(bf16[3,16,1024]{2,1,0:T(8,128)(2,1)S(1)} %get-tuple-element.23), channel_id=1, source_target_pairs={{0,18},{1,17},{2,16},{3,19},{4,22},{5,21},{6,20},{7,23},{8,26},{9,... | collective-permute-start | bytes 294920 | tf_op jit(solution)/shard_map/ppermute | solution.py:325
  22.1 0.5 %collective-permute-start.9 = (bf16[3,16,1024]{2,1,0:T(8,128)(2,1)S(1)}, bf16[3,16,1024]{2,1,0:T(8,128)(2,1)S(1)}, u32[]{:S(2)}, u32[]{:S(2)}) collective-permute-start(bf16[3,16,1024]{2,1,0:T(8,128)(2,1)S(1)} %get-tuple-element.24), channel_id=1, source_target_pairs={{0,16},{1,3},{2,18},{3,1},{4,20},{5,7},{6,22},{7,5},{8,24},{9,11},... | collective-permute-start | bytes 294920 | tf_op jit(solution)/shard_map/ppermute | solution.py:325
  22.7 0.0 collective-permute-done.4.refs_2_
  22.7 0.5 %collective-permute-start.11 = (bf16[3,16,1024]{2,1,0:T(8,128)(2,1)S(1)}, bf16[3,16,1024]{2,1,0:T(8,128)(2,1)S(1)}, u32[]{:S(2)}, u32[]{:S(2)}) collective-permute-start(bf16[3,16,1024]{2,1,0:T(8,128)(2,1)S(1)} %get-tuple-element.36), channel_id=1, source_target_pairs={{0,2},{1,19},{2,0},{3,17},{4,6},{5,23},{6,4},{7,21},{8,10},{9,27},... | collective-permute-start | bytes 294920 | tf_op jit(solution)/shard_map/ppermute | solution.py:325
  23.2 0.8 %collective-permute-done.3.refs_1_ = bf16[5,16,1024]{2,1,0:T(8,128)(2,1)S(1)} collective-permute-done((bf16[5,16,1024]{2,1,0:T(8,128)(2,1)S(1)}, bf16[5,16,1024]{2,1,0:T(8,128)(2,1)S(1)}, u32[]{:S(2)}, u32[]{:S(2)}) %collective-permute-start.3) | collective-permute-done | bytes 163872 | tf_op jit(solution)/shard_map/ppermute | solution.py:325
  24.0 0.1 collective-permute-done.5.refs_3_
  24.1 0.0 copy-done
  24.1 0.5 %image.2.refs_8_ = f32[512,1024]{1,0:T(8,128)S(1)} custom-call(bf16[2,512,512]{2,1,0:T(8,128)(2,1)S(1)} %copy-done, bf16[5,16,1024]{2,1,0:T(8,128)(2,1)S(1)} %get-tuple-element.29.refs_0_, bf16[5,16,1024]{2,1,0:T(8,128)(2,1)S(1)} %collective-permute-done.3.refs_1_, bf16[5,16,1024]{2,1,0:T(8,128)(2,1)S(1)} %collective-permute-done.4.refs_2_, ...), custom_call_target="tpu_custom_call" | custom-call | flops 268435456 | bytes 2097152 | tf_op jit(solution)/shard_map/image/pallas_call | solution.py:271
  24.6 1.4 %collective-permute-done.10.refs_6_ = bf16[3,16,1024]{2,1,0:T(8,128)(2,1)S(1)} collective-permute-done((bf16[3,16,1024]{2,1,0:T(8,128)(2,1)S(1)}, bf16[3,16,1024]{2,1,0:T(8,128)(2,1)S(1)}, u32[]{:S(2)}, u32[]{:S(2)}) %collective-permute-start.10) | collective-permute-done | bytes 98336 | tf_op jit(solution)/shard_map/ppermute | solution.py:325
  25.9 1.3 %collective-permute-done.9.refs_5_ = bf16[3,16,1024]{2,1,0:T(8,128)(2,1)S(1)} collective-permute-done((bf16[3,16,1024]{2,1,0:T(8,128)(2,1)S(1)}, bf16[3,16,1024]{2,1,0:T(8,128)(2,1)S(1)}, u32[]{:S(2)}, u32[]{:S(2)}) %collective-permute-start.9) | collective-permute-done | bytes 98336 | tf_op jit(solution)/shard_map/ppermute | solution.py:325
  27.2 0.5 %collective-permute-done.11.refs_7_ = bf16[3,16,1024]{2,1,0:T(8,128)(2,1)S(1)} collective-permute-done((bf16[3,16,1024]{2,1,0:T(8,128)(2,1)S(1)}, bf16[3,16,1024]{2,1,0:T(8,128)(2,1)S(1)}, u32[]{:S(2)}, u32[]{:S(2)}) %collective-permute-start.11) | collective-permute-done | bytes 98336 | tf_op jit(solution)/shard_map/ppermute | solution.py:325
  27.7 1.3 %image.3 = bf16[512,1024]{1,0:T(8,128)(2,1)} custom-call(bf16[2,512,512]{2,1,0:T(8,128)(2,1)S(1)} %copy-done, bf16[5,16,1024]{2,1,0:T(8,128)(2,1)S(1)} %get-tuple-element.29.refs_0_, bf16[5,16,1024]{2,1,0:T(8,128)(2,1)S(1)} %collective-permute-done.3.refs_1_, bf16[5,16,1024]{2,1,0:T(8,128)(2,1)S(1)} %collective-permute-done.4.refs_2_, ...), custom_call_target="tpu_custom_call" | custom-call | flops 268435456 | bytes 2097152 | tf_op jit(solution)/shard_map/image/pallas_call | solution.py:271
  (9 shorter events, 0.1 us)
Async XLA Ops:
  0.0 24.1 %copy-start = (bf16[2,512,512]{2,1,0:T(8,128)(2,1)S(1)}, bf16[2,512,512]{2,1,0:T(8,128)(2,1)}, u32[]{:S(2)}) copy-start(bf16[2,512,512]{2,1,0:T(8,128)(2,1)} %constant.29.clone.table) | copy-start | bytes 3145732
  2.5 4.2 %collective-permute-start = (bf16[6,16,1024]{2,1,0:T(8,128)(2,1)S(1)}, bf16[6,16,1024]{2,1,0:T(8,128)(2,1)S(1)}, u32[]{:S(2)}, u32[]{:S(2)}) collective-permute-start(bf16[6,16,1024]{2,1,0:T(8,128)(2,1)S(1)} %get-tuple-element.14), channel_id=1, source_target_pairs={{0,1},{1,0},{2,3},{3,2},{4,5},{5,4},{6,7},{7,6},{8,9},{9,8},{10,11... | collective-permute-start | bytes 589832 | tf_op jit(solution)/shard_map/ppermute | solution.py:325
  3.0 7.9 %collective-permute-start.2 = (bf16[2,16,1024]{2,1,0:T(8,128)(2,1)S(1)}, bf16[2,16,1024]{2,1,0:T(8,128)(2,1)S(1)}, u32[]{:S(2)}, u32[]{:S(2)}) collective-permute-start(bf16[2,16,1024]{2,1,0:T(8,128)(2,1)S(1)} %get-tuple-element.16), channel_id=1, source_target_pairs={{0,8},{1,9},{2,10},{3,11},{4,12},{5,13},{6,14},{7,15},{8,0},{9,1},... | collective-permute-start | bytes 196616 | tf_op jit(solution)/shard_map/ppermute | solution.py:325
  6.7 3.2 %collective-permute-start.6 = (bf16[2,16,1024]{2,1,0:T(8,128)(2,1)S(1)}, bf16[2,16,1024]{2,1,0:T(8,128)(2,1)S(1)}, u32[]{:S(2)}, u32[]{:S(2)}) collective-permute-start(bf16[2,16,1024]{2,1,0:T(8,128)(2,1)S(1)} %get-tuple-element.19), channel_id=1, source_target_pairs={{0,1},{1,0},{2,3},{3,2},{4,5},{5,4},{6,7},{7,6},{8,9},{9,8},{10,11... | collective-permute-start | bytes 196616 | tf_op jit(solution)/shard_map/ppermute | solution.py:325
  6.9 6.0 %collective-permute-start.1 = (bf16[2,2,16,1024]{3,2,0,1:T(8,128)(2,1)S(1)}, bf16[2,2,16,1024]{3,2,0,1:T(8,128)(2,1)S(1)}, u32[]{:S(2)}, u32[]{:S(2)}) collective-permute-start(bf16[2,2,16,1024]{3,2,0,1:T(8,128)(2,1)S(1)} %pad_maximum_fusion.2), channel_id=1, source_target_pairs={{0,4},{1,5},{2,6},{3,7},{4,0},{5,1},{6,2},{7,3},{8,12},{9,13},{10,... | collective-permute-start | bytes 393224 | tf_op jit(solution)/shard_map/ppermute | solution.py:325
  8.5 8.3 %collective-permute-start.8 = (bf16[2,2,16,1024]{3,2,1,0:T(8,128)(2,1)S(1)}, bf16[2,2,16,1024]{3,2,1,0:T(8,128)(2,1)S(1)}, u32[]{:S(2)}, u32[]{:S(2)}) collective-permute-start(bf16[2,2,16,1024]{3,2,1,0:T(8,128)(2,1)S(1)} %pad_maximum_fusion.3), channel_id=1, source_target_pairs={{0,12},{1,13},{2,14},{3,15},{4,8},{5,9},{6,10},{7,11},{8,4},{9,5},... | collective-permute-start | bytes 393224 | tf_op jit(solution)/shard_map/ppermute | solution.py:325
  9.9 9.7 %collective-permute-start.7 = (bf16[2,16,1024]{2,1,0:T(8,128)(2,1)S(1)}, bf16[2,16,1024]{2,1,0:T(8,128)(2,1)S(1)}, u32[]{:S(2)}, u32[]{:S(2)}) collective-permute-start(bf16[2,16,1024]{2,1,0:T(8,128)(2,1)S(1)} %collective-permute-done.6), channel_id=1, source_target_pairs={{0,8},{1,9},{2,10},{3,11},{4,12},{5,13},{6,14},{7,15},{8,0},{9,1},... | collective-permute-start | bytes 196616 | tf_op jit(solution)/shard_map/ppermute | solution.py:325
  13.0 9.7 %collective-permute-start.4 = (bf16[5,16,1024]{2,1,0:T(8,128)(2,1)S(1)}, bf16[5,16,1024]{2,1,0:T(8,128)(2,1)S(1)}, u32[]{:S(2)}, u32[]{:S(2)}) collective-permute-start(bf16[5,16,1024]{2,1,0:T(8,128)(2,1)S(1)} %get-tuple-element.21), channel_id=1, source_target_pairs={{0,18},{1,17},{2,16},{3,19},{4,22},{5,21},{6,20},{7,23},{8,26},{9,... | collective-permute-start | bytes 491528 | tf_op jit(solution)/shard_map/ppermute | solution.py:325
  15.6 8.4 %collective-permute-start.3 = (bf16[5,16,1024]{2,1,0:T(8,128)(2,1)S(1)}, bf16[5,16,1024]{2,1,0:T(8,128)(2,1)S(1)}, u32[]{:S(2)}, u32[]{:S(2)}) collective-permute-start(bf16[5,16,1024]{2,1,0:T(8,128)(2,1)S(1)} %get-tuple-element.22), channel_id=1, source_target_pairs={{0,16},{1,3},{2,18},{3,1},{4,20},{5,7},{6,22},{7,5},{8,24},{9,11},... | collective-permute-start | bytes 491528 | tf_op jit(solution)/shard_map/ppermute | solution.py:325
  16.1 8.0 %collective-permute-start.5 = (bf16[5,16,1024]{2,1,0:T(8,128)(2,1)S(1)}, bf16[5,16,1024]{2,1,0:T(8,128)(2,1)S(1)}, u32[]{:S(2)}, u32[]{:S(2)}) collective-permute-start(bf16[5,16,1024]{2,1,0:T(8,128)(2,1)S(1)} %get-tuple-element.28), channel_id=1, source_target_pairs={{0,2},{1,19},{2,0},{3,17},{4,6},{5,23},{6,4},{7,21},{8,10},{9,27},... | collective-permute-start | bytes 491528 | tf_op jit(solution)/shard_map/ppermute | solution.py:325
  19.6 6.3 %collective-permute-start.10 = (bf16[3,16,1024]{2,1,0:T(8,128)(2,1)S(1)}, bf16[3,16,1024]{2,1,0:T(8,128)(2,1)S(1)}, u32[]{:S(2)}, u32[]{:S(2)}) collective-permute-start(bf16[3,16,1024]{2,1,0:T(8,128)(2,1)S(1)} %get-tuple-element.23), channel_id=1, source_target_pairs={{0,18},{1,17},{2,16},{3,19},{4,22},{5,21},{6,20},{7,23},{8,26},{9,... | collective-permute-start | bytes 294920 | tf_op jit(solution)/shard_map/ppermute | solution.py:325
  22.1 5.1 %collective-permute-start.9 = (bf16[3,16,1024]{2,1,0:T(8,128)(2,1)S(1)}, bf16[3,16,1024]{2,1,0:T(8,128)(2,1)S(1)}, u32[]{:S(2)}, u32[]{:S(2)}) collective-permute-start(bf16[3,16,1024]{2,1,0:T(8,128)(2,1)S(1)} %get-tuple-element.24), channel_id=1, source_target_pairs={{0,16},{1,3},{2,18},{3,1},{4,20},{5,7},{6,22},{7,5},{8,24},{9,11},... | collective-permute-start | bytes 294920 | tf_op jit(solution)/shard_map/ppermute | solution.py:325
  22.7 5.1 %collective-permute-start.11 = (bf16[3,16,1024]{2,1,0:T(8,128)(2,1)S(1)}, bf16[3,16,1024]{2,1,0:T(8,128)(2,1)S(1)}, u32[]{:S(2)}, u32[]{:S(2)}) collective-permute-start(bf16[3,16,1024]{2,1,0:T(8,128)(2,1)S(1)} %get-tuple-element.36), channel_id=1, source_target_pairs={{0,2},{1,19},{2,0},{3,17},{4,6},{5,23},{6,4},{7,21},{8,10},{9,27},... | collective-permute-start | bytes 294920 | tf_op jit(solution)/shard_map/ppermute | solution.py:325

commit v9 on v8

--- a/solution.py
+++ b/solution.py
@@ -227,9 +227,9 @@
 def image_kernel(plan, far, has_total, table, *refs):
     arrays, refs = refs[: len(plan)], refs[len(plan) :]
     if has_total:
-        total, out_far, data, columns, out, sent = refs
+        total, columns, out_far, data, out, sent = refs
     else:
-        out, data, columns = refs
+        out, columns_next, data, columns = refs
     half = data.shape[0] // 2
     block = arrays[0].shape[1]
     me = lax.axis_index("gate")
@@ -242,9 +242,10 @@
             if apart // FAR * FAR == far:
                 start = side * half + (me ^ (apart + along)) * block - lower
                 data[pl.ds(pl.multiple_of(start, block), block), :] = array[index]
-    for side in range(2):
-        source = pl.multiple_of(side * 2 * half + lower, half)
-        columns[:, pl.ds(side * half, half)] = table[lax.axis_index("sub"), :, pl.ds(source, half)]
+    for side in range(0 if has_total else 2):
+        for part, begin in ((columns, lower), (columns_next, half - lower)):
+            source = pl.multiple_of(side * 2 * half + begin, half)
+            part[:, pl.ds(side * half, half)] = table[lax.axis_index("sub"), :, pl.ds(source, half)]
     tile = 256
     copies = []
     for row in range(0, out.shape[0], tile):
@@ -270,18 +271,20 @@
         used = [i for i, (*_, places) in enumerate(plan) if any(apart // FAR * FAR == far for apart in places)]
         image = pl.pallas_call(
             functools.partial(image_kernel, [plan[i] for i in used], far, bool(total)),
-            out_shape=jax.ShapeDtypeStruct(shape, jnp.bfloat16) if far else pltpu.VMEM(shape, jnp.float32),
+            out_shape=jax.ShapeDtypeStruct(shape, jnp.bfloat16)
+            if far
+            else [pltpu.VMEM(shape, jnp.float32), pltpu.VMEM((rows, depth), jnp.bfloat16)],
             in_specs=[vmem] * (1 + len(used) + len(total)),
-            out_specs=pl.BlockSpec(memory_space=pltpu.HBM) if far else vmem,
-            scratch_shapes=[pltpu.VMEM((depth, shape[1]), jnp.bfloat16), pltpu.VMEM((rows, depth), jnp.bfloat16)]
-            + ([pltpu.VMEM(shape, jnp.bfloat16), pltpu.SemaphoreType.DMA((rows // 256 * (shape[1] // 256),))] if far else []),
+            out_specs=pl.BlockSpec(memory_space=pltpu.HBM) if far else [vmem, vmem],
+            scratch_shapes=[pltpu.VMEM((depth, shape[1]), jnp.bfloat16)]
+            + ([pltpu.VMEM(shape, jnp.bfloat16), pltpu.SemaphoreType.DMA((rows // 256 * (shape[1] // 256),))] if far else [pltpu.VMEM((rows, depth), jnp.bfloat16)]),
             cost_estimate=pl.CostEstimate(
                 flops=2 * depth * math.prod(shape), bytes_accessed=4 * math.prod(shape), transcendentals=0
             ),
             compiler_params=pltpu.CompilerParams(vmem_limit_bytes=32 * 2**20),
             name="image",
         )(tables, *[arrays[i] for i in used], *total)
-        total = [image]
+        total = image
     return image.reshape(2, ANGLES, shape[1])
 
 

time: 29.2 us -> 29.2 us (level)
  no operation moved by 1% of the time
where the time goes in v9:
time: 29.2 us; the launch traced here: 29 us
  starting transfers between devices  15.1 us (52%)
  waiting for transfers between devices  9.32 us (32%)
  Pallas kernels  4.3 us (15%)
    ppermute x12, starting transfers between devices, swap(): return lax.ppermute(array, ('sub', 'gate'), pairs)  15.1 us
    ppermute x12, waiting for transfers between devices, swap(): return lax.ppermute(array, ('sub', 'gate'), pairs)  9.32 us
    pallas_call x1, Pallas kernels, range_compress(): pl.pallas_call(functools.partial(compress_kernel, plan), out_shape=[pltpu...  2.47 us
    pallas_call x2, Pallas kernels, form_image(): pl.pallas_call(functools.partial(image_kernel, [plan[i] for i in used], f...  1.83 us
  transfers between devices with their start and end apart: 12, of which 9 were waited for; matrix products, arithmetic and copies ran while one was open for 1% of the time, Pallas kernels for 2%

profile of v9, /device:TPU:0, one launch (start us, length us, event | category | flops | bytes accessed | tf_op | source)
XLA Modules:
  0.0 29.0 jit_solution(3607422371883360690)
XLA Ops:
  0.0 0.0 copy-start
  0.0 2.5 %compress.1 = (bf16[2,16,1024]{2,1,0:T(8,128)(2,1)S(1)}, bf16[2,16,1024]{2,1,0:T(8,128)(2,1)S(1)}, bf16[2,16,1024]{2,1,0:T(8,128)(2,1)S(1)}, bf16[2,16,1024]{2,1...) custom-call(s32[8]{0:T(128)} %delays_far.1, bf16[2,8,16384]{2,1,0:T(8,128)(2,1)} %raw_far.1, ...), custom_call_target="tpu_custom_call" | custom-call | tf_op jit(solution)/shard_map/compress/pallas_call | solution.py:202
  2.5 0.5 %collective-permute-start = (bf16[6,16,1024]{2,1,0:T(8,128)(2,1)S(1)}, bf16[6,16,1024]{2,1,0:T(8,128)(2,1)S(1)}, u32[]{:S(2)}, u32[]{:S(2)}) collective-permute-start(bf16[6,16,1024]{2,1,0:T(8,128)(2,1)S(1)} %get-tuple-element.16), channel_id=1, source_target_pairs={{0,1},{1,0},{2,3},{3,2},{4,5},{5,4},{6,7},{7,6},{8,9},{9,8},{10,11... | collective-permute-start | bytes 589832 | tf_op jit(solution)/shard_map/ppermute | solution.py:328
  3.0 3.7 %collective-permute-start.2 = (bf16[2,16,1024]{2,1,0:T(8,128)(2,1)S(1)}, bf16[2,16,1024]{2,1,0:T(8,128)(2,1)S(1)}, u32[]{:S(2)}, u32[]{:S(2)}) collective-permute-start(bf16[2,16,1024]{2,1,0:T(8,128)(2,1)S(1)} %get-tuple-element.18), channel_id=1, source_target_pairs={{0,8},{1,9},{2,10},{3,11},{4,12},{5,13},{6,14},{7,15},{8,0},{9,1},... | collective-permute-start | bytes 196616 | tf_op jit(solution)/shard_map/ppermute | solution.py:328
  6.7 0.0 collective-permute-done
  6.7 0.2 collective-permute-start.6
  6.9 1.6 %collective-permute-start.1 = (bf16[2,2,16,1024]{3,2,0,1:T(8,128)(2,1)S(1)}, bf16[2,2,16,1024]{3,2,0,1:T(8,128)(2,1)S(1)}, u32[]{:S(2)}, u32[]{:S(2)}) collective-permute-start(bf16[2,2,16,1024]{3,2,0,1:T(8,128)(2,1)S(1)} %pad_maximum_fusion.2), channel_id=1, source_target_pairs={{0,4},{1,5},{2,6},{3,7},{4,0},{5,1},{6,2},{7,3},{8,12},{9,13},{10,... | collective-permute-start | bytes 393224 | tf_op jit(solution)/shard_map/ppermute | solution.py:328
  8.5 1.3 %collective-permute-start.8 = (bf16[2,2,16,1024]{3,2,1,0:T(8,128)(2,1)S(1)}, bf16[2,2,16,1024]{3,2,1,0:T(8,128)(2,1)S(1)}, u32[]{:S(2)}, u32[]{:S(2)}) collective-permute-start(bf16[2,2,16,1024]{3,2,1,0:T(8,128)(2,1)S(1)} %pad_maximum_fusion.3), channel_id=1, source_target_pairs={{0,12},{1,13},{2,14},{3,15},{4,8},{5,9},{6,10},{7,11},{8,4},{9,5},... | collective-permute-start | bytes 393224 | tf_op jit(solution)/shard_map/ppermute | solution.py:328
  9.8 0.0 collective-permute-done.6
  9.9 0.7 %collective-permute-start.7 = (bf16[2,16,1024]{2,1,0:T(8,128)(2,1)S(1)}, bf16[2,16,1024]{2,1,0:T(8,128)(2,1)S(1)}, u32[]{:S(2)}, u32[]{:S(2)}) collective-permute-start(bf16[2,16,1024]{2,1,0:T(8,128)(2,1)S(1)} %collective-permute-done.6), channel_id=1, source_target_pairs={{0,8},{1,9},{2,10},{3,11},{4,12},{5,13},{6,14},{7,15},{8,0},{9,1},... | collective-permute-start | bytes 196616 | tf_op jit(solution)/shard_map/ppermute | solution.py:328
  10.6 0.3 collective-permute-done.2
  10.9 2.1 %collective-permute-done.1 = bf16[2,2,16,1024]{3,2,0,1:T(8,128)(2,1)S(1)} collective-permute-done((bf16[2,2,16,1024]{3,2,0,1:T(8,128)(2,1)S(1)}, bf16[2,2,16,1024]{3,2,0,1:T(8,128)(2,1)S(1)}, u32[]{:S(2)}, u32[]{:S(2)}) %collective-permute-start.1) | collective-permute-done | bytes 131104 | tf_op jit(solution)/shard_map/ppermute | solution.py:328
  12.9 0.1 broadcast_select_fusion
  13.0 2.6 %collective-permute-start.4 = (bf16[5,16,1024]{2,1,0:T(8,128)(2,1)S(1)}, bf16[5,16,1024]{2,1,0:T(8,128)(2,1)S(1)}, u32[]{:S(2)}, u32[]{:S(2)}) collective-permute-start(bf16[5,16,1024]{2,1,0:T(8,128)(2,1)S(1)} %get-tuple-element.25), channel_id=1, source_target_pairs={{0,18},{1,17},{2,16},{3,19},{4,22},{5,21},{6,20},{7,23},{8,26},{9,... | collective-permute-start | bytes 491528 | tf_op jit(solution)/shard_map/ppermute | solution.py:328
  15.6 0.5 %collective-permute-start.3 = (bf16[5,16,1024]{2,1,0:T(8,128)(2,1)S(1)}, bf16[5,16,1024]{2,1,0:T(8,128)(2,1)S(1)}, u32[]{:S(2)}, u32[]{:S(2)}) collective-permute-start(bf16[5,16,1024]{2,1,0:T(8,128)(2,1)S(1)} %get-tuple-element.26), channel_id=1, source_target_pairs={{0,16},{1,3},{2,18},{3,1},{4,20},{5,7},{6,22},{7,5},{8,24},{9,11},... | collective-permute-start | bytes 491528 | tf_op jit(solution)/shard_map/ppermute | solution.py:328
  16.1 0.4 %collective-permute-start.5 = (bf16[5,16,1024]{2,1,0:T(8,128)(2,1)S(1)}, bf16[5,16,1024]{2,1,0:T(8,128)(2,1)S(1)}, u32[]{:S(2)}, u32[]{:S(2)}) collective-permute-start(bf16[5,16,1024]{2,1,0:T(8,128)(2,1)S(1)} %get-tuple-element.32), channel_id=1, source_target_pairs={{0,2},{1,19},{2,0},{3,17},{4,6},{5,23},{6,4},{7,21},{8,10},{9,27},... | collective-permute-start | bytes 491528 | tf_op jit(solution)/shard_map/ppermute | solution.py:328
  16.6 0.3 %collective-permute-done.8 = bf16[2,2,16,1024]{3,2,1,0:T(8,128)(2,1)S(1)} collective-permute-done((bf16[2,2,16,1024]{3,2,1,0:T(8,128)(2,1)S(1)}, bf16[2,2,16,1024]{3,2,1,0:T(8,128)(2,1)S(1)}, u32[]{:S(2)}, u32[]{:S(2)}) %collective-permute-start.8) | collective-permute-done | bytes 131104 | tf_op jit(solution)/shard_map/ppermute | solution.py:328
  16.9 2.7 %collective-permute-done.7 = bf16[2,16,1024]{2,1,0:T(8,128)(2,1)S(1)} collective-permute-done((bf16[2,16,1024]{2,1,0:T(8,128)(2,1)S(1)}, bf16[2,16,1024]{2,1,0:T(8,128)(2,1)S(1)}, u32[]{:S(2)}, u32[]{:S(2)}) %collective-permute-start.7) | collective-permute-done | bytes 65568 | tf_op jit(solution)/shard_map/ppermute | solution.py:328
  19.6 2.5 %collective-permute-start.10 = (bf16[3,16,1024]{2,1,0:T(8,128)(2,1)S(1)}, bf16[3,16,1024]{2,1,0:T(8,128)(2,1)S(1)}, u32[]{:S(2)}, u32[]{:S(2)}) collective-permute-start(bf16[3,16,1024]{2,1,0:T(8,128)(2,1)S(1)} %get-tuple-element.27), channel_id=1, source_target_pairs={{0,18},{1,17},{2,16},{3,19},{4,22},{5,21},{6,20},{7,23},{8,26},{9,... | collective-permute-start | bytes 294920 | tf_op jit(solution)/shard_map/ppermute | solution.py:328
  22.1 0.5 %collective-permute-start.9 = (bf16[3,16,1024]{2,1,0:T(8,128)(2,1)S(1)}, bf16[3,16,1024]{2,1,0:T(8,128)(2,1)S(1)}, u32[]{:S(2)}, u32[]{:S(2)}) collective-permute-start(bf16[3,16,1024]{2,1,0:T(8,128)(2,1)S(1)} %get-tuple-element.28), channel_id=1, source_target_pairs={{0,16},{1,3},{2,18},{3,1},{4,20},{5,7},{6,22},{7,5},{8,24},{9,11},... | collective-permute-start | bytes 294920 | tf_op jit(solution)/shard_map/ppermute | solution.py:328
  22.7 0.0 collective-permute-done.4.refs_2_
  22.7 0.5 %collective-permute-start.11 = (bf16[3,16,1024]{2,1,0:T(8,128)(2,1)S(1)}, bf16[3,16,1024]{2,1,0:T(8,128)(2,1)S(1)}, u32[]{:S(2)}, u32[]{:S(2)}) collective-permute-start(bf16[3,16,1024]{2,1,0:T(8,128)(2,1)S(1)} %get-tuple-element.40), channel_id=1, source_target_pairs={{0,2},{1,19},{2,0},{3,17},{4,6},{5,23},{6,4},{7,21},{8,10},{9,27},... | collective-permute-start | bytes 294920 | tf_op jit(solution)/shard_map/ppermute | solution.py:328
  23.2 0.9 %collective-permute-done.3.refs_1_ = bf16[5,16,1024]{2,1,0:T(8,128)(2,1)S(1)} collective-permute-done((bf16[5,16,1024]{2,1,0:T(8,128)(2,1)S(1)}, bf16[5,16,1024]{2,1,0:T(8,128)(2,1)S(1)}, u32[]{:S(2)}, u32[]{:S(2)}) %collective-permute-start.3) | collective-permute-done | bytes 163872 | tf_op jit(solution)/shard_map/ppermute | solution.py:328
  24.0 0.1 collective-permute-done.5.refs_3_
  24.1 0.0 copy-done
  24.1 0.5 %image.2 = (f32[512,1024]{1,0:T(8,128)S(1)}, bf16[512,256]{1,0:T(8,128)(2,1)S(1)}) custom-call(bf16[2,512,512]{2,1,0:T(8,128)(2,1)S(1)} %copy-done, bf16[5,16,1024]{2,1,0:T(8,128)(2,1)S(1)} %get-tuple-element.33.refs_0_, bf16[5,16,1024]{2,1,0:T(8,128)(2,1)S(1)} %collective-permute-done.3.refs_1_, bf16[5,16,1024]{2,1,0:T(8,128)(2,1)S(1)} %collective-permute-done.4.refs_2_, ...), custom_call_target="tpu_custom_call" | custom-call | flops 268435456 | bytes 2097152 | tf_op jit(solution)/shard_map/image/pallas_call | solution.py:272
  24.6 1.3 %collective-permute-done.10.refs_6_ = bf16[3,16,1024]{2,1,0:T(8,128)(2,1)S(1)} collective-permute-done((bf16[3,16,1024]{2,1,0:T(8,128)(2,1)S(1)}, bf16[3,16,1024]{2,1,0:T(8,128)(2,1)S(1)}, u32[]{:S(2)}, u32[]{:S(2)}) %collective-permute-start.10) | collective-permute-done | bytes 98336 | tf_op jit(solution)/shard_map/ppermute | solution.py:328
  25.9 1.3 %collective-permute-done.9.refs_5_ = bf16[3,16,1024]{2,1,0:T(8,128)(2,1)S(1)} collective-permute-done((bf16[3,16,1024]{2,1,0:T(8,128)(2,1)S(1)}, bf16[3,16,1024]{2,1,0:T(8,128)(2,1)S(1)}, u32[]{:S(2)}, u32[]{:S(2)}) %collective-permute-start.9) | collective-permute-done | bytes 98336 | tf_op jit(solution)/shard_map/ppermute | solution.py:328
  27.2 0.5 %collective-permute-done.11.refs_7_ = bf16[3,16,1024]{2,1,0:T(8,128)(2,1)S(1)} collective-permute-done((bf16[3,16,1024]{2,1,0:T(8,128)(2,1)S(1)}, bf16[3,16,1024]{2,1,0:T(8,128)(2,1)S(1)}, u32[]{:S(2)}, u32[]{:S(2)}) %collective-permute-start.11) | collective-permute-done | bytes 98336 | tf_op jit(solution)/shard_map/ppermute | solution.py:328
  27.7 1.3 %image.3 = bf16[512,1024]{1,0:T(8,128)(2,1)} custom-call(bf16[2,512,512]{2,1,0:T(8,128)(2,1)S(1)} %copy-done, bf16[5,16,1024]{2,1,0:T(8,128)(2,1)S(1)} %get-tuple-element.33.refs_0_, bf16[5,16,1024]{2,1,0:T(8,128)(2,1)S(1)} %collective-permute-done.3.refs_1_, bf16[5,16,1024]{2,1,0:T(8,128)(2,1)S(1)} %collective-permute-done.4.refs_2_, ...), custom_call_target="tpu_custom_call" | custom-call | flops 268435456 | bytes 2097152 | tf_op jit(solution)/shard_map/image/pallas_call | solution.py:272
  (9 shorter events, 0.1 us)
Async XLA Ops:
  0.0 24.1 %copy-start = (bf16[2,512,512]{2,1,0:T(8,128)(2,1)S(1)}, bf16[2,512,512]{2,1,0:T(8,128)(2,1)}, u32[]{:S(2)}) copy-start(bf16[2,512,512]{2,1,0:T(8,128)(2,1)} %constant.29.clone.table) | copy-start | bytes 3145732
  2.5 4.2 %collective-permute-start = (bf16[6,16,1024]{2,1,0:T(8,128)(2,1)S(1)}, bf16[6,16,1024]{2,1,0:T(8,128)(2,1)S(1)}, u32[]{:S(2)}, u32[]{:S(2)}) collective-permute-start(bf16[6,16,1024]{2,1,0:T(8,128)(2,1)S(1)} %get-tuple-element.16), channel_id=1, source_target_pairs={{0,1},{1,0},{2,3},{3,2},{4,5},{5,4},{6,7},{7,6},{8,9},{9,8},{10,11... | collective-permute-start | bytes 589832 | tf_op jit(solution)/shard_map/ppermute | solution.py:328
  3.0 7.9 %collective-permute-start.2 = (bf16[2,16,1024]{2,1,0:T(8,128)(2,1)S(1)}, bf16[2,16,1024]{2,1,0:T(8,128)(2,1)S(1)}, u32[]{:S(2)}, u32[]{:S(2)}) collective-permute-start(bf16[2,16,1024]{2,1,0:T(8,128)(2,1)S(1)} %get-tuple-element.18), channel_id=1, source_target_pairs={{0,8},{1,9},{2,10},{3,11},{4,12},{5,13},{6,14},{7,15},{8,0},{9,1},... | collective-permute-start | bytes 196616 | tf_op jit(solution)/shard_map/ppermute | solution.py:328
  6.7 3.2 %collective-permute-start.6 = (bf16[2,16,1024]{2,1,0:T(8,128)(2,1)S(1)}, bf16[2,16,1024]{2,1,0:T(8,128)(2,1)S(1)}, u32[]{:S(2)}, u32[]{:S(2)}) collective-permute-start(bf16[2,16,1024]{2,1,0:T(8,128)(2,1)S(1)} %get-tuple-element.21), channel_id=1, source_target_pairs={{0,1},{1,0},{2,3},{3,2},{4,5},{5,4},{6,7},{7,6},{8,9},{9,8},{10,11... | collective-permute-start | bytes 196616 | tf_op jit(solution)/shard_map/ppermute | solution.py:328
  6.9 6.0 %collective-permute-start.1 = (bf16[2,2,16,1024]{3,2,0,1:T(8,128)(2,1)S(1)}, bf16[2,2,16,1024]{3,2,0,1:T(8,128)(2,1)S(1)}, u32[]{:S(2)}, u32[]{:S(2)}) collective-permute-start(bf16[2,2,16,1024]{3,2,0,1:T(8,128)(2,1)S(1)} %pad_maximum_fusion.2), channel_id=1, source_target_pairs={{0,4},{1,5},{2,6},{3,7},{4,0},{5,1},{6,2},{7,3},{8,12},{9,13},{10,... | collective-permute-start | bytes 393224 | tf_op jit(solution)/shard_map/ppermute | solution.py:328
  8.5 8.3 %collective-permute-start.8 = (bf16[2,2,16,1024]{3,2,1,0:T(8,128)(2,1)S(1)}, bf16[2,2,16,1024]{3,2,1,0:T(8,128)(2,1)S(1)}, u32[]{:S(2)}, u32[]{:S(2)}) collective-permute-start(bf16[2,2,16,1024]{3,2,1,0:T(8,128)(2,1)S(1)} %pad_maximum_fusion.3), channel_id=1, source_target_pairs={{0,12},{1,13},{2,14},{3,15},{4,8},{5,9},{6,10},{7,11},{8,4},{9,5},... | collective-permute-start | bytes 393224 | tf_op jit(solution)/shard_map/ppermute | solution.py:328
  9.9 9.7 %collective-permute-start.7 = (bf16[2,16,1024]{2,1,0:T(8,128)(2,1)S(1)}, bf16[2,16,1024]{2,1,0:T(8,128)(2,1)S(1)}, u32[]{:S(2)}, u32[]{:S(2)}) collective-permute-start(bf16[2,16,1024]{2,1,0:T(8,128)(2,1)S(1)} %collective-permute-done.6), channel_id=1, source_target_pairs={{0,8},{1,9},{2,10},{3,11},{4,12},{5,13},{6,14},{7,15},{8,0},{9,1},... | collective-permute-start | bytes 196616 | tf_op jit(solution)/shard_map/ppermute | solution.py:328
  13.0 9.7 %collective-permute-start.4 = (bf16[5,16,1024]{2,1,0:T(8,128)(2,1)S(1)}, bf16[5,16,1024]{2,1,0:T(8,128)(2,1)S(1)}, u32[]{:S(2)}, u32[]{:S(2)}) collective-permute-start(bf16[5,16,1024]{2,1,0:T(8,128)(2,1)S(1)} %get-tuple-element.25), channel_id=1, source_target_pairs={{0,18},{1,17},{2,16},{3,19},{4,22},{5,21},{6,20},{7,23},{8,26},{9,... | collective-permute-start | bytes 491528 | tf_op jit(solution)/shard_map/ppermute | solution.py:328
  15.6 8.4 %collective-permute-start.3 = (bf16[5,16,1024]{2,1,0:T(8,128)(2,1)S(1)}, bf16[5,16,1024]{2,1,0:T(8,128)(2,1)S(1)}, u32[]{:S(2)}, u32[]{:S(2)}) collective-permute-start(bf16[5,16,1024]{2,1,0:T(8,128)(2,1)S(1)} %get-tuple-element.26), channel_id=1, source_target_pairs={{0,16},{1,3},{2,18},{3,1},{4,20},{5,7},{6,22},{7,5},{8,24},{9,11},... | collective-permute-start | bytes 491528 | tf_op jit(solution)/shard_map/ppermute | solution.py:328
  16.1 8.0 %collective-permute-start.5 = (bf16[5,16,1024]{2,1,0:T(8,128)(2,1)S(1)}, bf16[5,16,1024]{2,1,0:T(8,128)(2,1)S(1)}, u32[]{:S(2)}, u32[]{:S(2)}) collective-permute-start(bf16[5,16,1024]{2,1,0:T(8,128)(2,1)S(1)} %get-tuple-element.32), channel_id=1, source_target_pairs={{0,2},{1,19},{2,0},{3,17},{4,6},{5,23},{6,4},{7,21},{8,10},{9,27},... | collective-permute-start | bytes 491528 | tf_op jit(solution)/shard_map/ppermute | solution.py:328
  19.6 6.3 %collective-permute-start.10 = (bf16[3,16,1024]{2,1,0:T(8,128)(2,1)S(1)}, bf16[3,16,1024]{2,1,0:T(8,128)(2,1)S(1)}, u32[]{:S(2)}, u32[]{:S(2)}) collective-permute-start(bf16[3,16,1024]{2,1,0:T(8,128)(2,1)S(1)} %get-tuple-element.27), channel_id=1, source_target_pairs={{0,18},{1,17},{2,16},{3,19},{4,22},{5,21},{6,20},{7,23},{8,26},{9,... | collective-permute-start | bytes 294920 | tf_op jit(solution)/shard_map/ppermute | solution.py:328
  22.1 5.1 %collective-permute-start.9 = (bf16[3,16,1024]{2,1,0:T(8,128)(2,1)S(1)}, bf16[3,16,1024]{2,1,0:T(8,128)(2,1)S(1)}, u32[]{:S(2)}, u32[]{:S(2)}) collective-permute-start(bf16[3,16,1024]{2,1,0:T(8,128)(2,1)S(1)} %get-tuple-element.28), channel_id=1, source_target_pairs={{0,16},{1,3},{2,18},{3,1},{4,20},{5,7},{6,22},{7,5},{8,24},{9,11},... | collective-permute-start | bytes 294920 | tf_op jit(solution)/shard_map/ppermute | solution.py:328
  22.7 5.1 %collective-permute-start.11 = (bf16[3,16,1024]{2,1,0:T(8,128)(2,1)S(1)}, bf16[3,16,1024]{2,1,0:T(8,128)(2,1)S(1)}, u32[]{:S(2)}, u32[]{:S(2)}) collective-permute-start(bf16[3,16,1024]{2,1,0:T(8,128)(2,1)S(1)} %get-tuple-element.40), channel_id=1, source_target_pairs={{0,2},{1,19},{2,0},{3,17},{4,6},{5,23},{6,4},{7,21},{8,10},{9,27},... | collective-permute-start | bytes 294920 | tf_op jit(solution)/shard_map/ppermute | solution.py:328
